TPU v7x, 512 devices: a whole 4x8x8 slice. The times are simulated.
512 devices in a mesh: wave: 64 (over z, y), lev: 8 (over x, core).
Axes of the slice: x: 4, y: 8, z: 8, core: 2. Of those that a mesh axis runs over, the one named last changes fastest.
Arguments:
- fourier_in: bfloat16 [2, 32, 2560, 256], P(None, 'lev', 'wave'), may hold values from -6 to 6
- table: bfloat16 [64, 1281, 2560], P('wave', None, 'lev'), may hold values from -0.125 to 0.125
- points: int32 [2560], replicated, may hold values from 20 to 5136, as said below
- pair_low: int32 [64], P('wave'), may hold values from 0 to 639, as said below
- gamma: float32 [32], replicated, may hold values from 1 to 100
- beta: float32 [32], replicated, may hold values from 0.5 to 2
Outputs:
- fourier_out: bfloat16 [2, 32, 2560, 256], P(None, 'lev', 'wave')
Inputs may be any that keep to these rules, and one draw needn't show every extreme that they name: `points`: each is a multiple of 4; row i has at most 20 + 4 min(i, 2559 - i) points and at most 32 fewer; the two middle rows have exactly the most. `pair_low`: all distinct.
All inputs are finite; a program needn't handle non-finite values.
Results may differ from a plain program's by a relative error of at most 0.0055.
Values may be sent and summed in bfloat16 or wider, within the bound.
No kernel may reach another device: no remote copies, remote signals or barrier semaphores. Data moves between devices by JAX's collectives and lax.ppermute only.
A program may use at most 64 MiB of HBM per device.

v0:
```python
import jax
import jax.numpy as jnp
from jax import lax
from jax.sharding import PartitionSpec as P


def solve_levels(spectra, gamma, beta, eig):
    drive = spectra[:, 0]
    mass = spectra[:, 1]
    gval = gamma[:, None, None, None]
    bval = beta[:, None, None, None]
    solved = (drive - bval * eig * mass) / (1.0 + gval * eig)
    return jnp.stack([solved, mass + bval * solved], axis=1).astype(jnp.bfloat16)


def local(fourier_in, table, points, pair_low, gamma, beta):
    pair_dev = table.shape[0]
    packed = table.shape[1]
    slab = table.shape[2]
    lev_dev = fourier_in.shape[1]
    nlat = points.shape[0]
    levels = gamma.shape[0]
    cut_off = packed - 2
    moved = lax.all_to_all(fourier_in, "wave", split_axis=3, concat_axis=2, tiled=True)
    moved = jnp.swapaxes(moved, 2, 3)
    sliced = lax.all_to_all(moved, "lev", split_axis=3, concat_axis=1, tiled=True)
    first_row = lax.axis_index("lev") * slab
    row_points = lax.dynamic_slice_in_dim(points, first_row, slab)
    weights = nlat * row_points.astype(jnp.float32) / jnp.sum(points.astype(jnp.float32))
    limit = jnp.minimum(cut_off, row_points // 2 - 1)
    wnum = jnp.stack([pair_low, cut_off - pair_low], axis=1)
    keep = (wnum[:, :, None] <= limit[None, None, :])[:, :, None, :]
    data = sliced.reshape(2, levels, pair_dev, 2, 2, slab)
    weighted = jnp.where(keep, data.astype(jnp.float32) * weights, 0.0).astype(jnp.bfloat16)
    kidx = jnp.arange(packed, dtype=jnp.int32)
    first = kidx[None, :] <= (cut_off - pair_low)[:, None]
    degree = jnp.where(first, pair_low[:, None] + kidx[None, :], kidx[None, :] - 1).astype(
        jnp.float32
    )
    eig = degree * (degree + 1.0) / (cut_off * (cut_off + 1.0))
    raw = jnp.einsum("pki,fvpmci->vfcpmk", table, weighted, preferred_element_type=jnp.float32)
    own = lax.psum_scatter(
        jnp.where(first, raw[:, :, :, :, 0], raw[:, :, :, :, 1]),
        "lev",
        scatter_dimension=0,
        tiled=True,
    )
    first_level = lax.axis_index("lev") * lev_dev
    own_gamma = lax.dynamic_slice_in_dim(gamma, first_level, lev_dev)
    own_beta = lax.dynamic_slice_in_dim(beta, first_level, lev_dev)
    spec = solve_levels(own, own_gamma, own_beta, eig)
    piece = lax.all_gather(spec, "lev", axis=0, tiled=True)
    zero = jnp.zeros_like(piece)
    expanded = jnp.stack([jnp.where(first, piece, zero), jnp.where(first, zero, piece)], axis=4)
    result = jnp.einsum("pki,vfcpmk->fvpmci", table, expanded, preferred_element_type=jnp.float32)
    result = jnp.where(keep, result, 0.0).astype(jnp.bfloat16)
    result = result.reshape(2, piece.shape[0], 4 * pair_dev, slab)
    back = lax.all_to_all(result, "lev", split_axis=1, concat_axis=3, tiled=True)
    back = jnp.swapaxes(back, 2, 3)
    return lax.all_to_all(back, "wave", split_axis=2, concat_axis=3, tiled=True)


def solution(mesh):
    placed = (P(None, "lev", "wave", None), P("wave", None, "lev"), P(), P("wave"), P(), P())
    return jax.shard_map(
        local, mesh=mesh, in_specs=placed, out_specs=P(None, "lev", "wave", None), check_vma=False
    )
```

profile of v0, /device:TPU:1, one launch (start us, length us, event | category | flops | bytes accessed | tf_op | source)
XLA Modules:
  0.0 246.1 jit_solution(13745605636998316820)
XLA Ops:
  6.5 1.3 copy.46
  7.9 1.5 reshape.216
  9.3 17.1 %all-to-all-start = ((bf16[64,2,640]{2,1,0:T(2,128)(2,1)}), bf16[64,2,640]{2,1,0:T(2,128)(2,1)S(1)}, u32[]{:S(2)}, u32[]{:S(2)}) async-start(bf16[64,2,640]{2,1,0:T(2,128)(2,1)} %reshape.216), calls=%async_computation | async-start | bytes 327680 | tf_op jit(solution)/shard_map/all_to_all | solution.py:24
  27.1 1.3 convert_reduce_fusion
  28.4 0.8 fusion.13
  29.2 1.3 multiply_divide_fusion
  30.7 7.5 %all-to-all-done = bf16[64,2,640]{2,1,0:T(2,128)(2,1)S(1)} async-done(((bf16[64,2,640]{2,1,0:T(2,128)(2,1)}), bf16[64,2,640]{2,1,0:T(2,128)(2,1)S(1)}, u32[]{:S(2)}, u32[]{:S(2)}) %all-to-all-start) | async-done | bytes 163872 | tf_op jit(solution)/shard_map/all_to_all | solution.py:24
  38.2 0.8 reshape.217
  39.2 0.8 all_to_all.49
  40.0 5.4 %copy.49 = bf16[2,4,4,2560]{2,1,0,3:T(4,128)(2,1)} copy(bf16[2,4,4,2560]{3,2,1,0:T(4,128)(2,1)S(1)} %bitcast.94) | data formatting | bytes 327680 | tf_op jit(solution)/shard_map/transpose | solution.py:25
  45.4 11.6 %reshape.218 = bf16[8,2,5120]{2,1,0:T(2,128)(2,1)} reshape(bf16[2560,2,4,4]{3,2,1,0:T(4,128)(2,1)} %bitcast.80) | data formatting | bytes 327680
  57.0 6.7 %all-to-all-start.1 = ((bf16[8,2,5120]{2,1,0:T(2,128)(2,1)}), bf16[8,2,5120]{2,1,0:T(2,128)(2,1)S(1)}, u32[]{:S(2)}, u32[]{:S(2)}) async-start(bf16[8,2,5120]{2,1,0:T(2,128)(2,1)} %reshape.218), calls=%async_computation.1 | async-start | bytes 327680 | tf_op jit(solution)/shard_map/all_to_all | solution.py:26
  63.9 1.3 dynamic-slice
  65.8 3.5 %all-to-all-done.1 = bf16[8,2,5120]{2,1,0:T(2,128)(2,1)S(1)} async-done(((bf16[8,2,5120]{2,1,0:T(2,128)(2,1)}), bf16[8,2,5120]{2,1,0:T(2,128)(2,1)S(1)}, u32[]{:S(2)}, u32[]{:S(2)}) %all-to-all-start.1) | async-done | bytes 163872 | tf_op jit(solution)/shard_map/all_to_all | solution.py:26
  69.3 12.3 %reshape.219 = bf16[2560,2,4,4]{3,2,1,0:T(4,128)(2,1)} reshape(bf16[8,2,5120]{2,1,0:T(2,128)(2,1)S(1)} %all-to-all-done.1) | data formatting | bytes 327680
  81.6 6.8 %copy.50 = bf16[2,4,4,2560]{3,2,1,0:T(4,128)(2,1)S(1)} copy(bf16[2,4,4,2560]{2,1,0,3:T(4,128)(2,1)} %bitcast.81) | data formatting | bytes 327680 | tf_op jit(solution)/shard_map/all_to_all | solution.py:26
  88.6 0.2 copy.51
  88.8 0.5 convolution_bitcast_fusion
  89.4 1.0 fusion.5
  90.4 60.8 %all-reduce.3.cloned.1.call-done = f32[32,2,2,1,1281]{4,0,2,1,3:T(8,128)} async-done(((f32[32,2,2,1,1281]{4,0,2,1,3:T(8,128)}), f32[32,2,2,1,1281]{4,0,2,1,3:T(8,128)}) %all-reduce.3.cloned.1.call-update) | async-done | bytes 655888
  151.3 1.0 fusion.15
  152.2 1.0 add_convert_fusion
  153.3 15.0 %all_gather.3 = bf16[32,2,2,1,1281]{4,2,3,1,0:T(2,128)(2,1)S(1)} all-gather(bf16[4,2,2,1,1281]{4,2,3,1,0:T(2,128)(2,1)S(1)} %copy.54), channel_id=1, replica_groups=mesh['wave'=64,'lev'=8] {'lev'}, dimensions={0}, use_global_device_ids=true | all-gather | bytes 368928 | tf_op jit(solution)/shard_map/all_gather | solution.py:52
  168.4 0.6 fusion.2
  169.1 8.6 %all_to_all.63 = bf16[2,32,4,320]{3,2,0,1:T(4,128)(2,1)S(1)} all-to-all(bf16[2,32,4,320]{3,2,0,1:T(4,128)(2,1)S(1)} %copy.59), channel_id=1, replica_groups=mesh['wave'=64,'lev'=8] {'lev'}, dimensions={1} | all-to-all | bytes 327680 | tf_op jit(solution)/shard_map/all_to_all | solution.py:58
  177.9 5.4 %copy.61 = bf16[2,4,2560,4]{3,1,0,2:T(4,128)(2,1)} copy(bf16[2,4,2560,4]{2,3,1,0:T(4,128)(2,1)S(1)} %bitcast.93) | data formatting | bytes 327680 | tf_op jit(solution)/shard_map/transpose | solution.py:59
  183.3 10.6 %reshape.220 = bf16[64,2,640]{2,1,0:T(2,128)(2,1)S(1)} reshape(bf16[2560,2,4,4]{3,2,1,0:T(4,128)(2,1)} %bitcast.82) | data formatting | bytes 327680
  193.9 24.6 %all_to_all.64 = bf16[64,2,640]{2,1,0:T(2,128)(2,1)S(1)} all-to-all(bf16[64,2,640]{2,1,0:T(2,128)(2,1)S(1)} %reshape.220), channel_id=1, replica_groups=mesh['wave'=64,'lev'=8] {'wave'}, dimensions={0} | all-to-all | bytes 327680 | tf_op jit(solution)/shard_map/all_to_all | solution.py:60
  218.5 12.2 %reshape.221 = bf16[2560,2,4,4]{3,2,1,0:T(4,128)(2,1)} reshape(bf16[64,2,640]{2,1,0:T(2,128)(2,1)S(1)} %all_to_all.64) | data formatting | bytes 327680
  230.7 7.3 %copy.66 = bf16[2,4,64,40,4]{3,2,4,1,0:T(8,128)(2,1)S(1)} copy(bf16[2,4,64,40,4]{4,1,0,3,2:T(4,128)(2,1)} %bitcast.83) | data formatting | bytes 327680 | tf_op jit(solution)/shard_map/all_to_all | solution.py:60
  238.0 0.4 copy.63
  238.4 0.9 copy.64
  (28 shorter events, 1.4 us)
Async XLA Ops:
  6.5 82.3 %copy-start = (bf16[1,1281,320]{1,2,0:T(8,128)(2,1)S(1)}, bf16[1,1281,320]{1,2,0:T(8,128)(2,1)}, u32[]{:S(2)}) copy-start(bf16[1,1281,320]{1,2,0:T(8,128)(2,1)} %param.7) | copy-start | bytes 2459524
  9.3 28.9 %all-to-all-start = ((bf16[64,2,640]{2,1,0:T(2,128)(2,1)}), bf16[64,2,640]{2,1,0:T(2,128)(2,1)S(1)}, u32[]{:S(2)}, u32[]{:S(2)}) async-start(bf16[64,2,640]{2,1,0:T(2,128)(2,1)} %reshape.216), calls=%async_computation | async-start | bytes 327680 | tf_op jit(solution)/shard_map/all_to_all | solution.py:24
  40.0 23.7 %copy-start.1 = (f32[32]{0:T(128)S(1)}, f32[32]{0:T(128)}, u32[]{:S(2)}) copy-start(f32[32]{0:T(128)} %param.11) | copy-start | bytes 388
  40.0 23.8 %copy-start.2 = (f32[32]{0:T(128)S(1)}, f32[32]{0:T(128)}, u32[]{:S(2)}) copy-start(f32[32]{0:T(128)} %param.10) | copy-start | bytes 388
  57.0 12.3 %all-to-all-start.1 = ((bf16[8,2,5120]{2,1,0:T(2,128)(2,1)}), bf16[8,2,5120]{2,1,0:T(2,128)(2,1)S(1)}, u32[]{:S(2)}, u32[]{:S(2)}) async-start(bf16[8,2,5120]{2,1,0:T(2,128)(2,1)} %reshape.218), calls=%async_computation.1 | async-start | bytes 327680 | tf_op jit(solution)/shard_map/all_to_all | solution.py:26
  63.7 87.5 %all-reduce.3.cloned.1.call-start = ((), (), s32[]{:S(2)}) async-start(), calls=%async_computation.4 | async-start | bytes 1441792
Sparse Core Ops, SparseCore 0:
  90.5 60.7 all-reduce.2
where the time goes:
time: 247 us; the launch traced here: 246 us
  local copies, waits for them, and re-layouts  79.6 us (32%)
  waiting for transfers between devices  71.9 us (29%)
  blocking collectives  48.2 us (20%)
  starting transfers between devices  23.8 us (10%)
  between operations  14.8 us (6%)
  other arithmetic  6.76 us (3%)
    unnamed x2, waiting for transfers between devices  60.8 us
    unnamed x14, local copies, waits for them, and re-layouts  51.6 us
    all_to_all x1, blocking collectives, local(): return lax.all_to_all(back, 'wave', split_axis=2, concat_axis=3, tiled=True)  24.6 us
    all_to_all x1, starting transfers between devices, local(): lax.all_to_all(fourier_in, 'wave', split_axis=3, concat_axis=2, tiled=True)  17.1 us
    all_gather x1, blocking collectives, local(): piece = lax.all_gather(spec, 'lev', axis=0, tiled=True)  15 us
    all_to_all x1, blocking collectives, local(): lax.all_to_all(result, 'lev', split_axis=1, concat_axis=3, tiled=True)  8.59 us
    all_to_all x3, local copies, waits for them, and re-layouts, local(): return lax.all_to_all(back, 'wave', split_axis=2, concat_axis=3, tiled=True)  8.56 us
    all_to_all x1, waiting for transfers between devices, local(): lax.all_to_all(fourier_in, 'wave', split_axis=3, concat_axis=2, tiled=True)  7.54 us
  transfers between devices with their start and end apart: 3, of which 3 were waited for; matrix products, arithmetic and copies ran while one was open for 2% of the time, Pallas kernels for 0%

commit v1 on v0

v1 whole, which is shorter than its diff:
```python
import jax
import jax.numpy as jnp
from jax import lax
from jax.experimental import pallas as pl
from jax.experimental.pallas import tpu as pltpu
from jax.sharding import PartitionSpec as P

F = 2
V = 4
R = 40
PAIRS = 64
SLABS = 8
SLAB = 320
KP = 1281
CUT = KP - 2
NLAT = 2560
STEPS = R // 4
COLS = 32
HALF = 640
NEAR = 8 * 10**9
NEARS = 4

NT = (((1,), (1,)), ((), ()))
NN = (((1,), (0,)), ((), ()))
TN = (((0,), (0,)), ((), ()))
VMEM = pl.BlockSpec(memory_space=pltpu.VMEM)
ANY = pl.BlockSpec(memory_space=pl.ANY)
SMEM = pl.BlockSpec(memory_space=pltpu.SMEM)


def iota(shape, dim):
    return lax.broadcasted_iota(jnp.int32, shape, dim)


def ones_where(cond):
    return jnp.where(cond, 1.0, 0.0).astype(jnp.bfloat16)


def mul(a, b, dims):
    return lax.dot_general(a, b, dims, preferred_element_type=jnp.float32)


def by_member():
    row = iota((4 * PAIRS, 4 * PAIRS), 0)
    return ones_where(iota((4 * PAIRS, 4 * PAIRS), 1) == 4 * (row & (PAIRS - 1)) + (row >> 6))


def by_place():
    lane = iota((1, STEPS * 128), 1)
    source = ((lane >> 3) & 1) * V + ((lane >> 1) & 3)
    source = source * R + 4 * (lane >> 7) + ((lane >> 5) & 3)
    return ones_where(iota((F * V * R, STEPS * 128), 0) == source)


def lane_part(shape):
    lane = iota(shape, 1)
    return ((lane >> 4) & 1) * 2 + (lane & 1)


def pack_kernel(x_ref, o_ref):
    x = x_ref[...].astype(jnp.float32).reshape(F * V * R, 4 * PAIRS).astype(jnp.bfloat16)
    turned = mul(by_member(), x, NT).astype(jnp.bfloat16)
    placed = mul(turned, by_place(), NN)
    part = lane_part((PAIRS, STEPS * 128))
    out = placed[:PAIRS]
    for q in range(1, 4):
        out = jnp.where(part == q, placed[q * PAIRS:(q + 1) * PAIRS], out)
    halves = jnp.stack([out[:, :HALF], out[:, HALF:]], axis=0)
    o_ref[...] = jnp.swapaxes(halves, 0, 1).astype(jnp.bfloat16)


def unpack_kernel(b_ref, o_ref):
    b = jnp.swapaxes(b_ref[...].astype(jnp.float32), 0, 1)
    b = jnp.concatenate([b[0], b[1]], axis=1)
    part = lane_part((PAIRS, STEPS * 128))
    parts = [jnp.where(part == q, b, 0.0).astype(jnp.bfloat16) for q in range(4)]
    turned = mul(by_place(), jnp.concatenate(parts, axis=0), NT).astype(jnp.bfloat16)
    x = mul(turned, by_member(), NN)
    o_ref[...] = x.reshape(F, V, R, 4 * PAIRS).astype(jnp.bfloat16)


def spread_rows():
    row = iota((STEPS * SLABS, SLAB), 0)
    gap = iota((STEPS * SLABS, SLAB), 1) - (row & 7) * R - 4 * (row >> 3)
    return ones_where((gap >= 0) & (gap < 4))


def own_group():
    return (iota((4 * COLS, SLAB), 0) >> 5) == (iota((4 * COLS, SLAB), 1) & 3)


def coef_kernel(low_ref, lev_ref, gamma_ref, beta_ref, points_ref, scale_ref, mask_ref, level_ref):
    low = low_ref[0]
    points = jnp.concatenate([points_ref[:, s * SLAB:(s + 1) * SLAB] for s in range(SLABS)], axis=0)
    pts = points.astype(jnp.float32)
    weights = NLAT * pts / jnp.sum(pts)
    limit = jnp.minimum(CUT, (points >> 1) - 1)
    rows = jnp.stack([jnp.where(low <= limit, weights, 0.0), jnp.where(CUT - low <= limit, weights, 0.0)], axis=0)
    for s in range(SLABS):
        scale_ref[s] = rows[:, s, :]
    columns = limit.astype(jnp.float32).T
    lane = iota((SLAB, 128), 1)
    group = (lane >> 5) == (iota((SLAB, 128), 0) & 3)
    wnum = jnp.where((lane & 16) == 0, low, CUT - low).astype(jnp.float32)
    for s in range(SLABS):
        mask_ref[s] = ones_where(group & (wnum <= columns[:, s:s + 1]))
    level = iota((SLABS, 128), 0) >> 1
    gval = jnp.zeros((SLABS, 128), jnp.float32)
    bval = jnp.zeros((SLABS, 128), jnp.float32)
    for v in range(V):
        gval = jnp.where(level == v, gamma_ref[lev_ref[0] * V + v], gval)
        bval = jnp.where(level == v, beta_ref[lev_ref[0] * V + v], bval)
    level_ref[0] = gval
    level_ref[1] = bval


def members(pair):
    return jnp.concatenate([jnp.broadcast_to(pair[m:m + 1], (COLS // 2, SLAB)) for m in range(2)], axis=0)


def weigh_kernel(y_ref, scale_ref, o_ref):
    spread = spread_rows()
    group = own_group()
    y = jnp.swapaxes(y_ref[...].astype(jnp.float32), 0, 1)
    for s in range(SLABS):
        rows = y[:, s * SLABS:(s + 1) * SLABS]
        block = jnp.concatenate([rows[j // 5, :, (j % 5) * 128:(j % 5 + 1) * 128] for j in range(STEPS)], axis=0)
        turned = jnp.where(group, mul(block.astype(jnp.bfloat16), spread, TN), 0.0)
        turned = turned[:32] + turned[32:64] + turned[64:96] + turned[96:]
        o_ref[s] = (turned * members(scale_ref[s])).astype(jnp.bfloat16)


def slab_order(lev):
    way = 2 - 4 * (lev & 1)
    behind, ahead, far = (lev - way) & 7, (lev + way) & 7, (lev + 4) & 7
    return [lev, lev ^ 1, behind, behind ^ 1, ahead ^ 1, ahead, far, far ^ 1]


def add_up(raw, w_ref, slabs, tabs):
    for slab, tab in zip(slabs, tabs):
        term = mul(w_ref[slab], tab[...], NN)
        raw = term if raw is None else raw + term
    return raw


def near_kernel(lev_ref, w_ref, *refs):
    tabs, raw_ref, kept_refs, sems = refs[:NEARS], refs[NEARS], refs[NEARS + 1:-1], refs[-1]
    copies = [pltpu.make_async_copy(tabs[n], kept_refs[n], sems.at[n]) for n in range(NEARS)]
    for copy in copies:
        copy.start()
    slabs = slab_order(lev_ref[0])
    raw = None
    for n in range(NEARS):
        copies[n].wait()
        raw = add_up(raw, w_ref, slabs[n:n + 1], [kept_refs[n]])
    raw_ref[...] = raw


def far_kernel(lev_ref, w_ref, raw_ref, *refs):
    *tabs, total_ref = refs
    total_ref[...] = add_up(raw_ref[...], w_ref, slab_order(lev_ref[0])[4:], tabs)


def pass_kernel(token_ref, tab_ref, same_ref):
    pass


def solve_kernel(low_ref, lev_ref, level_ref, w_ref, mask_ref, raw_ref, *refs):
    *tabs, o_ref, out_ref = refs
    low = low_ref[0]
    slabs = slab_order(lev_ref[0])
    wide = add_up(raw_ref[...], w_ref, slabs[7:], tabs[7:])
    kidx = iota((1, KP), 1)
    first = kidx <= CUT - low
    degree = jnp.where(first, low + kidx, kidx - 1).astype(jnp.float32)
    eig = degree * (degree + 1.0) / (CUT * (CUT + 1.0))
    gval = level_ref[0, :, 0:1]
    bval = level_ref[1, :, 0:1]
    spectra = jnp.where(first, wide[:16], wide[16:])
    drive, mass = spectra[:8], spectra[8:]
    solved = (drive - bval * eig * mass) / (1.0 + gval * eig)
    spec = jnp.concatenate([solved, mass + bval * solved], axis=0)
    expanded = [jnp.where(first, spec, 0.0), jnp.where(first, 0.0, spec)] * 4
    expanded = jnp.concatenate(expanded, axis=0).T.astype(jnp.bfloat16)
    spread = spread_rows()
    for slab, tab in zip(slabs, tabs):
        rows = mul(tab[:, :KP - 1], expanded[:KP - 1], NN)
        rows = rows + tab[:, KP - 1:].astype(jnp.float32) * expanded[KP - 1:].astype(jnp.float32)
        rows = rows.astype(jnp.bfloat16) * mask_ref[slab]
        block = mul(spread, rows, NN)
        place = pl.ds(pl.multiple_of(slab * SLABS, SLABS), SLABS)
        for j in range(STEPS):
            out_ref[j // 5, place, (j % 5) * 128:(j % 5 + 1) * 128] = block[j * SLABS:(j + 1) * SLABS]
    o_ref[...] = jnp.swapaxes(out_ref[...], 0, 1).astype(jnp.bfloat16)


def params(mib):
    return pltpu.CompilerParams(vmem_limit_bytes=mib * 1024 * 1024)


def cost(rows, depth, columns):
    return pl.CostEstimate(flops=2 * max(rows, 256) * depth * columns, transcendentals=0,
                           bytes_accessed=2 * depth * columns)


def chunks():
    return jax.ShapeDtypeStruct((PAIRS, 2, HALF), jnp.bfloat16)


def pack(x):
    return pl.pallas_call(pack_kernel, out_shape=chunks(), in_specs=[VMEM], out_specs=VMEM,
                          compiler_params=params(12), cost_estimate=cost(PAIRS * 4, SLAB, 2 * KP), name="pack")(x)


def unpack(b):
    return pl.pallas_call(unpack_kernel, out_shape=jax.ShapeDtypeStruct((F, V, R, 4 * PAIRS), jnp.bfloat16),
                          in_specs=[VMEM], out_specs=VMEM, compiler_params=params(12), cost_estimate=cost(SLAB, PAIRS * 4, 2 * KP),
                          name="unpack")(b)


def coef(low, lev, gamma, beta, points):
    return pl.pallas_call(
        coef_kernel, out_shape=(jax.ShapeDtypeStruct((SLABS, 2, SLAB), jnp.float32),
                                jax.ShapeDtypeStruct((SLABS, SLAB, 128), jnp.bfloat16),
                                jax.ShapeDtypeStruct((2, SLABS, 128), jnp.float32)),
        in_specs=[SMEM] * 4 + [VMEM], out_specs=(VMEM,) * 3, compiler_params=params(8),
        name="coef")(low, lev, gamma, beta, points)


def like(tab):
    return jax.ShapeDtypeStruct(tab.shape, tab.dtype)


def weigh(y, scale):
    return pl.pallas_call(
        weigh_kernel, out_shape=jax.ShapeDtypeStruct((SLABS, COLS, SLAB), jnp.bfloat16),
        in_specs=[VMEM, VMEM], out_specs=VMEM, compiler_params=params(8),
        cost_estimate=cost(SLABS * 128, SLAB, 128), name="weigh")(y, scale)


def pass_on(token, tab):
    return pl.pallas_call(pass_kernel, out_shape=like(tab), in_specs=[ANY, ANY], out_specs=ANY,
                          input_output_aliases={1: 0}, compiler_params=params(1), name="pass_on")(token, tab)


RAW = jax.ShapeDtypeStruct((COLS, KP), jnp.float32)


def near(lev, w, tabs):
    return pl.pallas_call(
        near_kernel, out_shape=(RAW,) + tuple(like(t) for t in tabs), in_specs=[SMEM, VMEM] + [ANY] * NEARS,
        out_specs=(VMEM,) * (1 + NEARS), scratch_shapes=[pltpu.SemaphoreType.DMA((NEARS,))],
        compiler_params=params(8), cost_estimate=pl.CostEstimate(flops=NEAR, bytes_accessed=0, transcendentals=0),
        name="near")(lev, w, *tabs)


def far(lev, w, raw, tabs):
    return pl.pallas_call(
        far_kernel, out_shape=RAW, in_specs=[SMEM] + [VMEM] * (2 + len(tabs)), out_specs=VMEM,
        compiler_params=params(8), cost_estimate=cost(COLS, 3 * SLAB, KP), name="far")(lev, w, raw, *tabs)


def solve(low, lev, level, w, mask, raw, tabs):
    return pl.pallas_call(
        solve_kernel, out_shape=chunks(), in_specs=[SMEM] * 2 + [VMEM] * (4 + len(tabs)), out_specs=VMEM,
        scratch_shapes=[pltpu.VMEM((2, PAIRS, HALF), jnp.float32)],
        compiler_params=params(12), cost_estimate=cost(COLS, 9 * SLAB, KP),
        name="solve")(low, lev, level, w, mask, raw, *tabs)


def along_x(array):
    return lax.ppermute(array, "lev", [(d, (d + 2 - 4 * (d % 2)) % SLABS) for d in range(SLABS)])


def other_core(array):
    return lax.ppermute(array, "lev", [(d, d ^ 1) for d in range(SLABS)])


def local(fourier_in, table, points, pair_low, gamma, beta):
    lev = lax.axis_index("lev").astype(jnp.int32).reshape(1)
    own = jnp.swapaxes(table, 1, 2)[0]
    twin = other_core(own)
    first = along_x(own)
    second = along_x(twin)
    sent = pack(fourier_in)
    moved = lax.all_to_all(sent, "wave", split_axis=0, concat_axis=0, tiled=True)
    first = pass_on(sent, first)
    third = along_x(first)
    second = pass_on(sent, second)
    cores = [other_core(first), other_core(second)]
    scale, mask, level = coef(pair_low, lev, gamma, beta, points.reshape(1, NLAT))
    weighted = weigh(moved, scale)
    raw, *tabs = near(lev, weighted, [own, twin, first, second])
    third = pass_on(raw, third)
    tabs += cores + [third]
    raw = far(lev, weighted, raw, tabs[NEARS:])
    tabs += [other_core(third)]
    result = solve(pair_low, lev, level, weighted, mask, raw, tabs)
    back = lax.all_to_all(result, "wave", split_axis=0, concat_axis=0, tiled=True)
    return unpack(back)


def solution(mesh):
    placed = (P(None, "lev", "wave", None), P("wave", None, "lev"), P(), P("wave"), P(), P())
    return jax.shard_map(
        local, mesh=mesh, in_specs=placed, out_specs=P(None, "lev", "wave", None), check_vma=False
    )
```

time: 247 us -> 80.4 us (0.33)
  local copies, waits for them, and re-layouts: 79.6 us -> 1.59 us
  waiting for transfers between devices: 71.9 us -> 9.27 us
  blocking collectives: 48.2 us -> 19.2 us
  between operations: 14.8 us -> 0.88 us
  starting transfers between devices: 23.8 us -> 36.7 us
  Pallas kernels: 0 us -> 12 us
  other arithmetic: 6.76 us -> 0 us
    unnamed x2 -> x0, waiting for transfers between devices: 60.8 us -> none
    unnamed x14 -> x10, local copies, waits for them, and re-layouts: 51.6 us -> 1.58 us
    ppermute x0 -> x7, starting transfers between devices: none -> 23.2 us  [the longest x4 17.1 us: other_core(): return lax.ppermute(array, 'lev', [(d, d ^ 1) for d in range(SLABS)])]
    all_to_all x9 -> x0, local copies, waits for them, and re-layouts: 16.5 us -> none  [the longest x3 8.56 us: local(): return lax.all_to_all(back, 'wave', split_axis=2, concat_axis=3, tiled=True)]
    all_gather x1 -> x0, blocking collectives: 15 us -> none  [local(): piece = lax.all_gather(spec, 'lev', axis=0, tiled=True)]
    all_to_all x2 -> x1, blocking collectives: 33.2 us -> 19.2 us  [local(): lax.all_to_all(result, 'wave', split_axis=0, concat_axis=0, tiled=True)]
    pallas_call x0 -> x10, Pallas kernels: none -> 12 us  [the longest x1 4.79 us: solve(): pl.pallas_call(solve_kernel, out_shape=chunks(), in_specs=[SMEM] * 2 + [V...]
    transpose x2 -> x0, local copies, waits for them, and re-layouts: 10.8 us -> none  [the longest x1 5.39 us: local(): moved = jnp.swapaxes(moved, 2, 3)]
  transfers between devices with their start and end apart: 3 -> 8, of which waited for: 3 -> 3; matrix products, arithmetic and copies ran while one was open for 2% -> 0% of each run, Pallas kernels for 0% -> 7%
where the time goes in v1:
time: 80.4 us; the launch traced here: 79.7 us
  starting transfers between devices  36.7 us (46%)
  blocking collectives  19.2 us (24%)
  Pallas kernels  12 us (15%)
  waiting for transfers between devices  9.27 us (12%)
  local copies, waits for them, and re-layouts  1.59 us (2%)
  between operations  0.88 us (1%)
    all_to_all x1, blocking collectives, local(): lax.all_to_all(result, 'wave', split_axis=0, concat_axis=0, tiled=True)  19.2 us
    ppermute x4, starting transfers between devices, other_core(): return lax.ppermute(array, 'lev', [(d, d ^ 1) for d in range(SLABS)])  17.1 us
    all_to_all x1, starting transfers between devices, local(): lax.all_to_all(sent, 'wave', split_axis=0, concat_axis=0, tiled=True)  13.5 us
    all_to_all x1, waiting for transfers between devices, local(): lax.all_to_all(sent, 'wave', split_axis=0, concat_axis=0, tiled=True)  7.28 us
    ppermute x3, starting transfers between devices, along_x(): lax.ppermute(array, 'lev', [(d, (d + 2 - 4 * (d % 2)) % SLABS) for d in r...  6.2 us
    pallas_call x1, Pallas kernels, solve(): pl.pallas_call(solve_kernel, out_shape=chunks(), in_specs=[SMEM] * 2 + [V...  4.79 us
    pallas_call x1, Pallas kernels, near(): pl.pallas_call(near_kernel, out_shape=(RAW,) + tuple((like(t) for t in ta...  2.31 us
    ppermute x4, waiting for transfers between devices, other_core(): return lax.ppermute(array, 'lev', [(d, d ^ 1) for d in range(SLABS)])  1.99 us
  transfers between devices with their start and end apart: 8, of which 3 were waited for; matrix products, arithmetic and copies ran while one was open for 0% of the time, Pallas kernels for 7%

profile of v1, /device:TPU:1, one launch (start us, length us, event | category | flops | bytes accessed | tf_op | source)
XLA Modules:
  0.0 79.7 jit_solution(15444691978447632920)
XLA Ops:
  0.0 8.8 %collective-permute-start = (bf16[320,1281]{1,0:T(8,128)(2,1)}, bf16[320,1281]{1,0:T(8,128)(2,1)}, u32[]{:S(2)}, u32[]{:S(2)}) collective-permute-start(bf16[320,1281]{1,0:T(8,128)(2,1)} %bitcast.4), channel_id=1, source_target_pairs={{0,1},{1,0},{2,3},{3,2},{4,5},{5,4},{6,7},{7,6},{8,9},{9,8},{10,11... | collective-permute-start | bytes 2459528 | tf_op jit(solution)/shard_map/ppermute | solution.py:276
  8.8 1.9 %collective-permute-start.1 = (bf16[320,1281]{1,0:T(8,128)(2,1)}, bf16[320,1281]{1,0:T(8,128)(2,1)S(1)}, u32[]{:S(2)}, u32[]{:S(2)}) collective-permute-start(bf16[320,1281]{1,0:T(8,128)(2,1)} %bitcast.5), channel_id=1, source_target_pairs={{0,2},{1,7},{2,4},{3,1},{4,6},{5,3},{6,0},{7,5},{8,10},{9,15},{10,... | collective-permute-start | bytes 2459528 | tf_op jit(solution)/shard_map/ppermute | solution.py:272
  10.7 0.5 collective-permute-done.refs_1_
  11.2 1.9 %collective-permute-start.2 = (bf16[320,1281]{1,0:T(8,128)(2,1)}, bf16[320,1281]{1,0:T(8,128)(2,1)S(1)}, u32[]{:S(2)}, u32[]{:S(2)}) collective-permute-start(bf16[320,1281]{1,0:T(8,128)(2,1)} %collective-permute-done.refs_1_), channel_id=1, source_target_pairs={{0,2},{1,7},{2,4},{3,1},{4,6},{5,3},{6,0},{7,5},{8,10},{9,15},{10,... | collective-permute-start | bytes 2459528 | tf_op jit(solution)/shard_map/ppermute | solution.py:272
  13.1 0.9 %copy-done.3 = bf16[2,4,40,256]{3,2,1,0:T(8,128)(2,1)S(1)} copy-done((bf16[2,4,40,256]{3,2,1,0:T(8,128)(2,1)S(1)}, bf16[2,4,40,256]{3,2,1,0:T(8,128)(2,1)}, u32[]{:S(2)}) %copy-start.3) | copy-done | bytes 163864
  14.0 1.5 %pack.1.token_ref = bf16[64,2,640]{2,1,0:T(2,128)(2,1)} custom-call(bf16[2,4,40,256]{3,2,1,0:T(8,128)(2,1)S(1)} %copy-done.3), custom_call_target="tpu_custom_call" | custom-call | flops 419758080 | bytes 1639680 | tf_op jit(solution)/shard_map/pack/pallas_call | solution.py:211
  15.5 13.5 %all-to-all-start = ((bf16[64,2,640]{2,1,0:T(2,128)(2,1)}), bf16[64,2,640]{2,1,0:T(2,128)(2,1)S(1)}, u32[]{:S(2)}, u32[]{:S(2)}) async-start(bf16[64,2,640]{2,1,0:T(2,128)(2,1)} %pack.1.token_ref), calls=%async_computation | async-start | bytes 327680 | tf_op jit(solution)/shard_map/all_to_all | solution.py:286
  29.0 0.0 collective-permute-done.1.tab_ref
  29.0 0.0 copy-start.4
  29.1 2.4 %collective-permute-start.5 = (bf16[320,1281]{1,0:T(8,128)(2,1)S(1)}, bf16[320,1281]{1,0:T(8,128)(2,1)S(1)}, u32[]{:S(2)}, u32[]{:S(2)}) collective-permute-start(bf16[320,1281]{1,0:T(8,128)(2,1)S(1)} %pass_on.3.refs_2_), channel_id=1, source_target_pairs={{0,2},{1,7},{2,4},{3,1},{4,6},{5,3},{6,0},{7,5},{8,10},{9,15},{10,... | collective-permute-start | bytes 2459528 | tf_op jit(solution)/shard_map/ppermute | solution.py:272
  32.1 0.0 copy-done.4
  32.1 0.0 copy-start
  32.1 0.0 copy-start.1
  32.1 0.6 copy-done
  32.8 0.0 copy-done.1
  32.8 1.1 %coef.1 = (f32[8,2,320]{2,1,0:T(2,128)S(1)}, bf16[8,320,128]{2,1,0:T(8,128)(2,1)S(1)}, f32[2,8,128]{2,1,0:T(8,128)S(1)}) custom-call(s32[1]{0:T(128)S(6)} %copy.13.low_ref, s32[1]{0:T(128)} %bitcast.lev_ref, f32[32]{0:T(128)S(1)} %copy-done, f32[32]{0:T(128)S(1)} %copy-done.1, s32[1,2560]{1,0:T(1,128)S(1)} %reshape.7.points_ref), custom_call_target="tpu_custom_call" | custom-call | tf_op jit(solution)/shard_map/coef/pallas_call | solution.py:222
  34.0 7.3 %all-to-all-done.y_ref = bf16[64,2,640]{2,1,0:T(2,128)(2,1)S(1)} async-done(((bf16[64,2,640]{2,1,0:T(2,128)(2,1)}), bf16[64,2,640]{2,1,0:T(2,128)(2,1)S(1)}, u32[]{:S(2)}, u32[]{:S(2)}) %all-to-all-start) | async-done | bytes 163872 | tf_op jit(solution)/shard_map/all_to_all | solution.py:286
  41.2 0.4 weigh.1.w_ref
  41.7 0.0 copy-start.2
  41.7 3.9 %collective-permute-start.3 = (bf16[320,1281]{1,0:T(8,128)(2,1)S(1)}, bf16[320,1281]{1,0:T(8,128)(2,1)S(1)}, u32[]{:S(2)}, u32[]{:S(2)}) collective-permute-start(bf16[320,1281]{1,0:T(8,128)(2,1)S(1)} %pass_on.3.refs_2_), channel_id=1, source_target_pairs={{0,1},{1,0},{2,3},{3,2},{4,5},{5,4},{6,7},{7,6},{8,9},{9,8},{10,11... | collective-permute-start | bytes 2459528 | tf_op jit(solution)/shard_map/ppermute | solution.py:276
  45.7 0.0 collective-permute-done.2.tab_ref
  45.7 1.9 %collective-permute-start.4 = (bf16[320,1281]{1,0:T(8,128)(2,1)S(1)}, bf16[320,1281]{1,0:T(8,128)(2,1)S(1)}, u32[]{:S(2)}, u32[]{:S(2)}) collective-permute-start(bf16[320,1281]{1,0:T(8,128)(2,1)S(1)} %pass_on.4.refs_3_), channel_id=1, source_target_pairs={{0,1},{1,0},{2,3},{3,2},{4,5},{5,4},{6,7},{7,6},{8,9},{9,8},{10,11... | collective-permute-start | bytes 2459528 | tf_op jit(solution)/shard_map/ppermute | solution.py:276
  47.6 2.3 %near.1 = (f32[32,1281]{1,0:T(8,128)S(1)}, bf16[320,1281]{1,0:T(8,128)(2,1)S(1)}, bf16[320,1281]{1,0:T(8,128)(2,1)S(1)}, bf16[320,1281]{1,0:T(8,128)(2,1)S(1)}, bf16[320,1281]{1,0:T(8,128)(2,1)S(1)}) custom-call(s32[1]{0:T(128)} %bitcast.lev_ref, bf16[8,32,320]{2,1,0:T(8,128)(2,1)S(1)} %weigh.1.w_ref, bf16[320,1281]{1,0:T(8,128)(2,1)S(1)} %bitcast.6, ...), custom_call_target="tpu_custom_call" | custom-call | flops 8000000000 | tf_op jit(solution)/shard_map/near/pallas_call | solution.py:250
  49.9 0.0 collective-permute-done.5.tab_ref
  49.9 2.4 %collective-permute-start.6 = (bf16[320,1281]{1,0:T(8,128)(2,1)S(1)}, bf16[320,1281]{1,0:T(8,128)(2,1)S(1)}, u32[]{:S(2)}, u32[]{:S(2)}) collective-permute-start(bf16[320,1281]{1,0:T(8,128)(2,1)S(1)} %pass_on.5.refs_2_.refs_6_), channel_id=1, source_target_pairs={{0,1},{1,0},{2,3},{3,2},{4,5},{5,4},{6,7},{7,6},{8,9},{9,8},{10,11... | collective-permute-start | bytes 2459528 | tf_op jit(solution)/shard_map/ppermute | solution.py:276
  52.4 0.0 collective-permute-done.3.refs_0_.refs_4_
  52.4 0.0 collective-permute-done.4.refs_1_.refs_5_
  52.4 0.5 far.1.raw_ref
  52.9 1.5 %collective-permute-done.6.refs_7_ = bf16[320,1281]{1,0:T(8,128)(2,1)S(1)} collective-permute-done((bf16[320,1281]{1,0:T(8,128)(2,1)S(1)}, bf16[320,1281]{1,0:T(8,128)(2,1)S(1)}, u32[]{:S(2)}, u32[]{:S(2)}) %collective-permute-start.6) | collective-permute-done | bytes 819872 | tf_op jit(solution)/shard_map/ppermute | solution.py:276
  54.4 4.8 %solve.1 = bf16[64,2,640]{2,1,0:T(2,128)(2,1)S(1)} custom-call(s32[1]{0:T(128)S(6)} %copy.13.low_ref, s32[1]{0:T(128)} %bitcast.lev_ref, f32[2,8,128]{2,1,0:T(8,128)S(1)} %get-tuple-element.13.level_ref, bf16[8,32,320]{2,1,0:T(8,128)(2,1)S(1)} %weigh.1.w_ref, bf16[8,320,128]{2,1,0:T(8,128)(2,1)S(1)} %get-tuple-element.15.mask_ref, ...), custom_call_target="tpu_custom_call" | custom-call | flops 1888911360 | bytes 7378560 | tf_op jit(solution)/shard_map/solve/pallas_call | solution.py:264
  59.2 19.2 %all_to_all.10.b_ref = bf16[64,2,640]{2,1,0:T(2,128)(2,1)S(1)} all-to-all(bf16[64,2,640]{2,1,0:T(2,128)(2,1)S(1)} %solve.1), channel_id=1, replica_groups=mesh['wave'=64,'lev'=8] {'wave'}, dimensions={0} | all-to-all | bytes 327680 | tf_op jit(solution)/shard_map/all_to_all | solution.py:299
  78.4 1.3 %unpack.1 = bf16[2,4,40,256]{3,2,1,0:T(8,128)(2,1)} custom-call(bf16[64,2,640]{2,1,0:T(2,128)(2,1)S(1)} %all_to_all.10.b_ref), custom_call_target="tpu_custom_call" | custom-call | flops 419758080 | bytes 1311744 | tf_op jit(solution)/shard_map/unpack/pallas_call | solution.py:216
  (6 shorter events, 0.0 us)
Async XLA Ops:
  0.0 11.2 %collective-permute-start = (bf16[320,1281]{1,0:T(8,128)(2,1)}, bf16[320,1281]{1,0:T(8,128)(2,1)}, u32[]{:S(2)}, u32[]{:S(2)}) collective-permute-start(bf16[320,1281]{1,0:T(8,128)(2,1)} %bitcast.4), channel_id=1, source_target_pairs={{0,1},{1,0},{2,3},{3,2},{4,5},{5,4},{6,7},{7,6},{8,9},{9,8},{10,11... | collective-permute-start | bytes 2459528 | tf_op jit(solution)/shard_map/ppermute | solution.py:276
  8.8 20.3 %collective-permute-start.1 = (bf16[320,1281]{1,0:T(8,128)(2,1)}, bf16[320,1281]{1,0:T(8,128)(2,1)S(1)}, u32[]{:S(2)}, u32[]{:S(2)}) collective-permute-start(bf16[320,1281]{1,0:T(8,128)(2,1)} %bitcast.5), channel_id=1, source_target_pairs={{0,2},{1,7},{2,4},{3,1},{4,6},{5,3},{6,0},{7,5},{8,10},{9,15},{10,... | collective-permute-start | bytes 2459528 | tf_op jit(solution)/shard_map/ppermute | solution.py:272
  11.2 34.5 %collective-permute-start.2 = (bf16[320,1281]{1,0:T(8,128)(2,1)}, bf16[320,1281]{1,0:T(8,128)(2,1)S(1)}, u32[]{:S(2)}, u32[]{:S(2)}) collective-permute-start(bf16[320,1281]{1,0:T(8,128)(2,1)} %collective-permute-done.refs_1_), channel_id=1, source_target_pairs={{0,2},{1,7},{2,4},{3,1},{4,6},{5,3},{6,0},{7,5},{8,10},{9,15},{10,... | collective-permute-start | bytes 2459528 | tf_op jit(solution)/shard_map/ppermute | solution.py:272
  13.1 0.9 %copy-start.3 = (bf16[2,4,40,256]{3,2,1,0:T(8,128)(2,1)S(1)}, bf16[2,4,40,256]{3,2,1,0:T(8,128)(2,1)}, u32[]{:S(2)}) copy-start(bf16[2,4,40,256]{3,2,1,0:T(8,128)(2,1)} %x_ref.1) | copy-start | bytes 491524
  15.5 25.7 %all-to-all-start = ((bf16[64,2,640]{2,1,0:T(2,128)(2,1)}), bf16[64,2,640]{2,1,0:T(2,128)(2,1)S(1)}, u32[]{:S(2)}, u32[]{:S(2)}) async-start(bf16[64,2,640]{2,1,0:T(2,128)(2,1)} %pack.1.token_ref), calls=%async_computation | async-start | bytes 327680 | tf_op jit(solution)/shard_map/all_to_all | solution.py:286
  29.0 3.1 %copy-start.4 = (s32[2560]{0:T(1024)S(1)}, s32[2560]{0:T(1024)}, u32[]{:S(2)}) copy-start(s32[2560]{0:T(1024)} %param.8) | copy-start | bytes 30724
  29.1 20.9 %collective-permute-start.5 = (bf16[320,1281]{1,0:T(8,128)(2,1)S(1)}, bf16[320,1281]{1,0:T(8,128)(2,1)S(1)}, u32[]{:S(2)}, u32[]{:S(2)}) collective-permute-start(bf16[320,1281]{1,0:T(8,128)(2,1)S(1)} %pass_on.3.refs_2_), channel_id=1, source_target_pairs={{0,2},{1,7},{2,4},{3,1},{4,6},{5,3},{6,0},{7,5},{8,10},{9,15},{10,... | collective-permute-start | bytes 2459528 | tf_op jit(solution)/shard_map/ppermute | solution.py:272
  32.1 0.7 copy-start
  32.1 0.7 copy-start.1
  41.7 5.9 %copy-start.2 = (bf16[1,1281,320]{1,2,0:T(8,128)(2,1)S(1)}, bf16[1,1281,320]{1,2,0:T(8,128)(2,1)}, u32[]{:S(2)}) copy-start(bf16[1,1281,320]{1,2,0:T(8,128)(2,1)} %param.7) | copy-start | bytes 2459524
  41.7 10.7 %collective-permute-start.3 = (bf16[320,1281]{1,0:T(8,128)(2,1)S(1)}, bf16[320,1281]{1,0:T(8,128)(2,1)S(1)}, u32[]{:S(2)}, u32[]{:S(2)}) collective-permute-start(bf16[320,1281]{1,0:T(8,128)(2,1)S(1)} %pass_on.3.refs_2_), channel_id=1, source_target_pairs={{0,1},{1,0},{2,3},{3,2},{4,5},{5,4},{6,7},{7,6},{8,9},{9,8},{10,11... | collective-permute-start | bytes 2459528 | tf_op jit(solution)/shard_map/ppermute | solution.py:276
  45.7 6.7 %collective-permute-start.4 = (bf16[320,1281]{1,0:T(8,128)(2,1)S(1)}, bf16[320,1281]{1,0:T(8,128)(2,1)S(1)}, u32[]{:S(2)}, u32[]{:S(2)}) collective-permute-start(bf16[320,1281]{1,0:T(8,128)(2,1)S(1)} %pass_on.4.refs_3_), channel_id=1, source_target_pairs={{0,1},{1,0},{2,3},{3,2},{4,5},{5,4},{6,7},{7,6},{8,9},{9,8},{10,11... | collective-permute-start | bytes 2459528 | tf_op jit(solution)/shard_map/ppermute | solution.py:276
  49.9 4.5 %collective-permute-start.6 = (bf16[320,1281]{1,0:T(8,128)(2,1)S(1)}, bf16[320,1281]{1,0:T(8,128)(2,1)S(1)}, u32[]{:S(2)}, u32[]{:S(2)}) collective-permute-start(bf16[320,1281]{1,0:T(8,128)(2,1)S(1)} %pass_on.5.refs_2_.refs_6_), channel_id=1, source_target_pairs={{0,1},{1,0},{2,3},{3,2},{4,5},{5,4},{6,7},{7,6},{8,9},{9,8},{10,11... | collective-permute-start | bytes 2459528 | tf_op jit(solution)/shard_map/ppermute | solution.py:276

commit v2 on v1

--- a/solution.py
+++ b/solution.py
@@ -89,7 +89,7 @@
     return (iota((4 * COLS, SLAB), 0) >> 5) == (iota((4 * COLS, SLAB), 1) & 3)
 
 
-def coef_kernel(low_ref, lev_ref, gamma_ref, beta_ref, points_ref, scale_ref, mask_ref, level_ref):
+def coef_kernel(low_ref, lev_ref, gamma_ref, beta_ref, points_ref, scale_ref, level_ref):
     low = low_ref[0]
     points = jnp.concatenate([points_ref[:, s * SLAB:(s + 1) * SLAB] for s in range(SLABS)], axis=0)
     pts = points.astype(jnp.float32)
@@ -98,12 +98,6 @@
     rows = jnp.stack([jnp.where(low <= limit, weights, 0.0), jnp.where(CUT - low <= limit, weights, 0.0)], axis=0)
     for s in range(SLABS):
         scale_ref[s] = rows[:, s, :]
-    columns = limit.astype(jnp.float32).T
-    lane = iota((SLAB, 128), 1)
-    group = (lane >> 5) == (iota((SLAB, 128), 0) & 3)
-    wnum = jnp.where((lane & 16) == 0, low, CUT - low).astype(jnp.float32)
-    for s in range(SLABS):
-        mask_ref[s] = ones_where(group & (wnum <= columns[:, s:s + 1]))
     level = iota((SLABS, 128), 0) >> 1
     gval = jnp.zeros((SLABS, 128), jnp.float32)
     bval = jnp.zeros((SLABS, 128), jnp.float32)
@@ -165,7 +159,7 @@
     pass
 
 
-def solve_kernel(low_ref, lev_ref, level_ref, w_ref, mask_ref, raw_ref, *refs):
+def solve_kernel(low_ref, lev_ref, level_ref, w_ref, scale_ref, raw_ref, *refs):
     *tabs, o_ref, out_ref = refs
     low = low_ref[0]
     slabs = slab_order(lev_ref[0])
@@ -180,14 +174,13 @@
     drive, mass = spectra[:8], spectra[8:]
     solved = (drive - bval * eig * mass) / (1.0 + gval * eig)
     spec = jnp.concatenate([solved, mass + bval * solved], axis=0)
-    expanded = [jnp.where(first, spec, 0.0), jnp.where(first, 0.0, spec)] * 4
-    expanded = jnp.concatenate(expanded, axis=0).T.astype(jnp.bfloat16)
+    expanded = jnp.concatenate([jnp.where(first, spec, 0.0), jnp.where(first, 0.0, spec)], axis=0).astype(jnp.bfloat16)
     spread = spread_rows()
+    group = own_group()
     for slab, tab in zip(slabs, tabs):
-        rows = mul(tab[:, :KP - 1], expanded[:KP - 1], NN)
-        rows = rows + tab[:, KP - 1:].astype(jnp.float32) * expanded[KP - 1:].astype(jnp.float32)
-        rows = rows.astype(jnp.bfloat16) * mask_ref[slab]
-        block = mul(spread, rows, NN)
+        rows = jnp.where(members(scale_ref[slab]) > 0.0, mul(expanded, tab[...], NT), 0.0)
+        rows = jnp.where(group, jnp.concatenate([rows] * 4, axis=0), 0.0).astype(jnp.bfloat16)
+        block = mul(spread, rows, NT)
         place = pl.ds(pl.multiple_of(slab * SLABS, SLABS), SLABS)
         for j in range(STEPS):
             out_ref[j // 5, place, (j % 5) * 128:(j % 5 + 1) * 128] = block[j * SLABS:(j + 1) * SLABS]
@@ -221,9 +214,8 @@
 def coef(low, lev, gamma, beta, points):
     return pl.pallas_call(
         coef_kernel, out_shape=(jax.ShapeDtypeStruct((SLABS, 2, SLAB), jnp.float32),
-                                jax.ShapeDtypeStruct((SLABS, SLAB, 128), jnp.bfloat16),
                                 jax.ShapeDtypeStruct((2, SLABS, 128), jnp.float32)),
-        in_specs=[SMEM] * 4 + [VMEM], out_specs=(VMEM,) * 3, compiler_params=params(8),
+        in_specs=[SMEM] * 4 + [VMEM], out_specs=(VMEM,) * 2, compiler_params=params(8),
         name="coef")(low, lev, gamma, beta, points)
 
 
@@ -260,12 +252,12 @@
         compiler_params=params(8), cost_estimate=cost(COLS, 3 * SLAB, KP), name="far")(lev, w, raw, *tabs)
 
 
-def solve(low, lev, level, w, mask, raw, tabs):
+def solve(low, lev, level, w, scale, raw, tabs):
     return pl.pallas_call(
         solve_kernel, out_shape=chunks(), in_specs=[SMEM] * 2 + [VMEM] * (4 + len(tabs)), out_specs=VMEM,
         scratch_shapes=[pltpu.VMEM((2, PAIRS, HALF), jnp.float32)],
         compiler_params=params(12), cost_estimate=cost(COLS, 9 * SLAB, KP),
-        name="solve")(low, lev, level, w, mask, raw, *tabs)
+        name="solve")(low, lev, level, w, scale, raw, *tabs)
 
 
 def along_x(array):
@@ -288,14 +280,14 @@
     third = along_x(first)
     second = pass_on(sent, second)
     cores = [other_core(first), other_core(second)]
-    scale, mask, level = coef(pair_low, lev, gamma, beta, points.reshape(1, NLAT))
+    scale, level = coef(pair_low, lev, gamma, beta, points.reshape(1, NLAT))
     weighted = weigh(moved, scale)
     raw, *tabs = near(lev, weighted, [own, twin, first, second])
     third = pass_on(raw, third)
     tabs += cores + [third]
     raw = far(lev, weighted, raw, tabs[NEARS:])
     tabs += [other_core(third)]
-    result = solve(pair_low, lev, level, weighted, mask, raw, tabs)
+    result = solve(pair_low, lev, level, weighted, scale, raw, tabs)
     back = lax.all_to_all(result, "wave", split_axis=0, concat_axis=0, tiled=True)
     return unpack(back)
 

time: 80.4 us -> 80.5 us (level)
  no operation moved by 1% of the time
where the time goes in v2:
time: 80.5 us; the launch traced here: 79.9 us
  starting transfers between devices  36.7 us (46%)
  blocking collectives  19.2 us (24%)
  Pallas kernels  11.8 us (15%)
  waiting for transfers between devices  9.67 us (12%)
  local copies, waits for them, and re-layouts  1.59 us (2%)
  between operations  0.88 us (1%)
    all_to_all x1, blocking collectives, local(): lax.all_to_all(result, 'wave', split_axis=0, concat_axis=0, tiled=True)  19.2 us
    ppermute x4, starting transfers between devices, other_core(): return lax.ppermute(array, 'lev', [(d, d ^ 1) for d in range(SLABS)])  17.1 us
    all_to_all x1, starting transfers between devices, local(): lax.all_to_all(sent, 'wave', split_axis=0, concat_axis=0, tiled=True)  13.5 us
    all_to_all x1, waiting for transfers between devices, local(): lax.all_to_all(sent, 'wave', split_axis=0, concat_axis=0, tiled=True)  7.67 us
    ppermute x3, starting transfers between devices, along_x(): lax.ppermute(array, 'lev', [(d, (d + 2 - 4 * (d % 2)) % SLABS) for d in r...  6.2 us
    pallas_call x1, Pallas kernels, solve(): pl.pallas_call(solve_kernel, out_shape=chunks(), in_specs=[SMEM] * 2 + [V...  4.94 us
    pallas_call x1, Pallas kernels, near(): pl.pallas_call(near_kernel, out_shape=(RAW,) + tuple((like(t) for t in ta...  2.31 us
    ppermute x4, waiting for transfers between devices, other_core(): return lax.ppermute(array, 'lev', [(d, d ^ 1) for d in range(SLABS)])  1.99 us
  transfers between devices with their start and end apart: 8, of which 3 were waited for; matrix products, arithmetic and copies ran while one was open for 0% of the time, Pallas kernels for 7%

profile of v2, /device:TPU:1, one launch (start us, length us, event | category | flops | bytes accessed | tf_op | source)
XLA Modules:
  0.0 79.9 jit_solution(13906225851786123042)
XLA Ops:
  0.0 8.8 %collective-permute-start = (bf16[320,1281]{1,0:T(8,128)(2,1)}, bf16[320,1281]{1,0:T(8,128)(2,1)}, u32[]{:S(2)}, u32[]{:S(2)}) collective-permute-start(bf16[320,1281]{1,0:T(8,128)(2,1)} %bitcast.4), channel_id=1, source_target_pairs={{0,1},{1,0},{2,3},{3,2},{4,5},{5,4},{6,7},{7,6},{8,9},{9,8},{10,11... | collective-permute-start | bytes 2459528 | tf_op jit(solution)/shard_map/ppermute | solution.py:268
  8.8 1.9 %collective-permute-start.1 = (bf16[320,1281]{1,0:T(8,128)(2,1)}, bf16[320,1281]{1,0:T(8,128)(2,1)S(1)}, u32[]{:S(2)}, u32[]{:S(2)}) collective-permute-start(bf16[320,1281]{1,0:T(8,128)(2,1)} %bitcast.5), channel_id=1, source_target_pairs={{0,2},{1,7},{2,4},{3,1},{4,6},{5,3},{6,0},{7,5},{8,10},{9,15},{10,... | collective-permute-start | bytes 2459528 | tf_op jit(solution)/shard_map/ppermute | solution.py:264
  10.7 0.5 collective-permute-done.refs_1_
  11.2 1.9 %collective-permute-start.2 = (bf16[320,1281]{1,0:T(8,128)(2,1)}, bf16[320,1281]{1,0:T(8,128)(2,1)S(1)}, u32[]{:S(2)}, u32[]{:S(2)}) collective-permute-start(bf16[320,1281]{1,0:T(8,128)(2,1)} %collective-permute-done.refs_1_), channel_id=1, source_target_pairs={{0,2},{1,7},{2,4},{3,1},{4,6},{5,3},{6,0},{7,5},{8,10},{9,15},{10,... | collective-permute-start | bytes 2459528 | tf_op jit(solution)/shard_map/ppermute | solution.py:264
  13.1 0.9 %copy-done.3 = bf16[2,4,40,256]{3,2,1,0:T(8,128)(2,1)S(1)} copy-done((bf16[2,4,40,256]{3,2,1,0:T(8,128)(2,1)S(1)}, bf16[2,4,40,256]{3,2,1,0:T(8,128)(2,1)}, u32[]{:S(2)}) %copy-start.3) | copy-done | bytes 163864
  14.0 1.5 %pack.1.token_ref = bf16[64,2,640]{2,1,0:T(2,128)(2,1)} custom-call(bf16[2,4,40,256]{3,2,1,0:T(8,128)(2,1)S(1)} %copy-done.3), custom_call_target="tpu_custom_call" | custom-call | flops 419758080 | bytes 1639680 | tf_op jit(solution)/shard_map/pack/pallas_call | solution.py:204
  15.5 13.5 %all-to-all-start = ((bf16[64,2,640]{2,1,0:T(2,128)(2,1)}), bf16[64,2,640]{2,1,0:T(2,128)(2,1)S(1)}, u32[]{:S(2)}, u32[]{:S(2)}) async-start(bf16[64,2,640]{2,1,0:T(2,128)(2,1)} %pack.1.token_ref), calls=%async_computation | async-start | bytes 327680 | tf_op jit(solution)/shard_map/all_to_all | solution.py:278
  29.0 0.0 collective-permute-done.1.tab_ref
  29.0 0.0 copy-start.4
  29.1 2.4 %collective-permute-start.5 = (bf16[320,1281]{1,0:T(8,128)(2,1)S(1)}, bf16[320,1281]{1,0:T(8,128)(2,1)S(1)}, u32[]{:S(2)}, u32[]{:S(2)}) collective-permute-start(bf16[320,1281]{1,0:T(8,128)(2,1)S(1)} %pass_on.3.refs_2_), channel_id=1, source_target_pairs={{0,2},{1,7},{2,4},{3,1},{4,6},{5,3},{6,0},{7,5},{8,10},{9,15},{10,... | collective-permute-start | bytes 2459528 | tf_op jit(solution)/shard_map/ppermute | solution.py:264
  32.1 0.0 copy-done.4
  32.1 0.0 copy-start
  32.1 0.0 copy-start.1
  32.1 0.6 copy-done
  32.8 0.0 copy-done.1
  32.8 0.8 coef.1
  33.6 7.7 %all-to-all-done.y_ref = bf16[64,2,640]{2,1,0:T(2,128)(2,1)S(1)} async-done(((bf16[64,2,640]{2,1,0:T(2,128)(2,1)}), bf16[64,2,640]{2,1,0:T(2,128)(2,1)S(1)}, u32[]{:S(2)}, u32[]{:S(2)}) %all-to-all-start) | async-done | bytes 163872 | tf_op jit(solution)/shard_map/all_to_all | solution.py:278
  41.2 0.4 weigh.1.w_ref
  41.7 0.0 copy-start.2
  41.7 3.9 %collective-permute-start.3 = (bf16[320,1281]{1,0:T(8,128)(2,1)S(1)}, bf16[320,1281]{1,0:T(8,128)(2,1)S(1)}, u32[]{:S(2)}, u32[]{:S(2)}) collective-permute-start(bf16[320,1281]{1,0:T(8,128)(2,1)S(1)} %pass_on.3.refs_2_), channel_id=1, source_target_pairs={{0,1},{1,0},{2,3},{3,2},{4,5},{5,4},{6,7},{7,6},{8,9},{9,8},{10,11... | collective-permute-start | bytes 2459528 | tf_op jit(solution)/shard_map/ppermute | solution.py:268
  45.7 0.0 collective-permute-done.2.tab_ref
  45.7 1.9 %collective-permute-start.4 = (bf16[320,1281]{1,0:T(8,128)(2,1)S(1)}, bf16[320,1281]{1,0:T(8,128)(2,1)S(1)}, u32[]{:S(2)}, u32[]{:S(2)}) collective-permute-start(bf16[320,1281]{1,0:T(8,128)(2,1)S(1)} %pass_on.4.refs_3_), channel_id=1, source_target_pairs={{0,1},{1,0},{2,3},{3,2},{4,5},{5,4},{6,7},{7,6},{8,9},{9,8},{10,11... | collective-permute-start | bytes 2459528 | tf_op jit(solution)/shard_map/ppermute | solution.py:268
  47.6 2.3 %near.1 = (f32[32,1281]{1,0:T(8,128)S(1)}, bf16[320,1281]{1,0:T(8,128)(2,1)S(1)}, bf16[320,1281]{1,0:T(8,128)(2,1)S(1)}, bf16[320,1281]{1,0:T(8,128)(2,1)S(1)}, bf16[320,1281]{1,0:T(8,128)(2,1)S(1)}) custom-call(s32[1]{0:T(128)} %bitcast.lev_ref, bf16[8,32,320]{2,1,0:T(8,128)(2,1)S(1)} %weigh.1.w_ref, bf16[320,1281]{1,0:T(8,128)(2,1)S(1)} %bitcast.6, ...), custom_call_target="tpu_custom_call" | custom-call | flops 8000000000 | tf_op jit(solution)/shard_map/near/pallas_call | solution.py:242
  49.9 0.0 collective-permute-done.5.tab_ref
  49.9 2.4 %collective-permute-start.6 = (bf16[320,1281]{1,0:T(8,128)(2,1)S(1)}, bf16[320,1281]{1,0:T(8,128)(2,1)S(1)}, u32[]{:S(2)}, u32[]{:S(2)}) collective-permute-start(bf16[320,1281]{1,0:T(8,128)(2,1)S(1)} %pass_on.5.refs_2_.refs_6_), channel_id=1, source_target_pairs={{0,1},{1,0},{2,3},{3,2},{4,5},{5,4},{6,7},{7,6},{8,9},{9,8},{10,11... | collective-permute-start | bytes 2459528 | tf_op jit(solution)/shard_map/ppermute | solution.py:268
  52.4 0.0 collective-permute-done.3.refs_0_.refs_4_
  52.4 0.0 collective-permute-done.4.refs_1_.refs_5_
  52.4 0.5 far.1.raw_ref
  52.9 1.5 %collective-permute-done.6.refs_7_ = bf16[320,1281]{1,0:T(8,128)(2,1)S(1)} collective-permute-done((bf16[320,1281]{1,0:T(8,128)(2,1)S(1)}, bf16[320,1281]{1,0:T(8,128)(2,1)S(1)}, u32[]{:S(2)}, u32[]{:S(2)}) %collective-permute-start.6) | collective-permute-done | bytes 819872 | tf_op jit(solution)/shard_map/ppermute | solution.py:268
  54.4 4.9 %solve.1 = bf16[64,2,640]{2,1,0:T(2,128)(2,1)S(1)} custom-call(s32[1]{0:T(128)S(6)} %copy.13.low_ref, s32[1]{0:T(128)} %bitcast.lev_ref, f32[2,8,128]{2,1,0:T(8,128)S(1)} %get-tuple-element.12.level_ref, bf16[8,32,320]{2,1,0:T(8,128)(2,1)S(1)} %weigh.1.w_ref, f32[8,2,320]{2,1,0:T(2,128)S(1)} %get-tuple-element.13.scale_ref, f32[32,1281]{1,0:T(8,128)S(1)} %far.1.raw_ref, ...), custom_call_target="tpu_custom_call" | custom-call | flops 1888911360 | bytes 7378560 | tf_op jit(solution)/shard_map/solve/pallas_call | solution.py:256
  59.4 19.2 %all_to_all.10.b_ref = bf16[64,2,640]{2,1,0:T(2,128)(2,1)S(1)} all-to-all(bf16[64,2,640]{2,1,0:T(2,128)(2,1)S(1)} %solve.1), channel_id=1, replica_groups=mesh['wave'=64,'lev'=8] {'wave'}, dimensions={0} | all-to-all | bytes 327680 | tf_op jit(solution)/shard_map/all_to_all | solution.py:291
  78.5 1.3 %unpack.1 = bf16[2,4,40,256]{3,2,1,0:T(8,128)(2,1)} custom-call(bf16[64,2,640]{2,1,0:T(2,128)(2,1)S(1)} %all_to_all.10.b_ref), custom_call_target="tpu_custom_call" | custom-call | flops 419758080 | bytes 1311744 | tf_op jit(solution)/shard_map/unpack/pallas_call | solution.py:209
  (6 shorter events, 0.0 us)
Async XLA Ops:
  0.0 11.2 %collective-permute-start = (bf16[320,1281]{1,0:T(8,128)(2,1)}, bf16[320,1281]{1,0:T(8,128)(2,1)}, u32[]{:S(2)}, u32[]{:S(2)}) collective-permute-start(bf16[320,1281]{1,0:T(8,128)(2,1)} %bitcast.4), channel_id=1, source_target_pairs={{0,1},{1,0},{2,3},{3,2},{4,5},{5,4},{6,7},{7,6},{8,9},{9,8},{10,11... | collective-permute-start | bytes 2459528 | tf_op jit(solution)/shard_map/ppermute | solution.py:268
  8.8 20.3 %collective-permute-start.1 = (bf16[320,1281]{1,0:T(8,128)(2,1)}, bf16[320,1281]{1,0:T(8,128)(2,1)S(1)}, u32[]{:S(2)}, u32[]{:S(2)}) collective-permute-start(bf16[320,1281]{1,0:T(8,128)(2,1)} %bitcast.5), channel_id=1, source_target_pairs={{0,2},{1,7},{2,4},{3,1},{4,6},{5,3},{6,0},{7,5},{8,10},{9,15},{10,... | collective-permute-start | bytes 2459528 | tf_op jit(solution)/shard_map/ppermute | solution.py:264
  11.2 34.5 %collective-permute-start.2 = (bf16[320,1281]{1,0:T(8,128)(2,1)}, bf16[320,1281]{1,0:T(8,128)(2,1)S(1)}, u32[]{:S(2)}, u32[]{:S(2)}) collective-permute-start(bf16[320,1281]{1,0:T(8,128)(2,1)} %collective-permute-done.refs_1_), channel_id=1, source_target_pairs={{0,2},{1,7},{2,4},{3,1},{4,6},{5,3},{6,0},{7,5},{8,10},{9,15},{10,... | collective-permute-start | bytes 2459528 | tf_op jit(solution)/shard_map/ppermute | solution.py:264
  13.1 0.9 %copy-start.3 = (bf16[2,4,40,256]{3,2,1,0:T(8,128)(2,1)S(1)}, bf16[2,4,40,256]{3,2,1,0:T(8,128)(2,1)}, u32[]{:S(2)}) copy-start(bf16[2,4,40,256]{3,2,1,0:T(8,128)(2,1)} %x_ref.1) | copy-start | bytes 491524
  15.5 25.7 %all-to-all-start = ((bf16[64,2,640]{2,1,0:T(2,128)(2,1)}), bf16[64,2,640]{2,1,0:T(2,128)(2,1)S(1)}, u32[]{:S(2)}, u32[]{:S(2)}) async-start(bf16[64,2,640]{2,1,0:T(2,128)(2,1)} %pack.1.token_ref), calls=%async_computation | async-start | bytes 327680 | tf_op jit(solution)/shard_map/all_to_all | solution.py:278
  29.0 3.1 %copy-start.4 = (s32[2560]{0:T(1024)S(1)}, s32[2560]{0:T(1024)}, u32[]{:S(2)}) copy-start(s32[2560]{0:T(1024)} %param.8) | copy-start | bytes 30724
  29.1 20.9 %collective-permute-start.5 = (bf16[320,1281]{1,0:T(8,128)(2,1)S(1)}, bf16[320,1281]{1,0:T(8,128)(2,1)S(1)}, u32[]{:S(2)}, u32[]{:S(2)}) collective-permute-start(bf16[320,1281]{1,0:T(8,128)(2,1)S(1)} %pass_on.3.refs_2_), channel_id=1, source_target_pairs={{0,2},{1,7},{2,4},{3,1},{4,6},{5,3},{6,0},{7,5},{8,10},{9,15},{10,... | collective-permute-start | bytes 2459528 | tf_op jit(solution)/shard_map/ppermute | solution.py:264
  32.1 0.7 copy-start
  32.1 0.7 copy-start.1
  41.7 5.9 %copy-start.2 = (bf16[1,1281,320]{1,2,0:T(8,128)(2,1)S(1)}, bf16[1,1281,320]{1,2,0:T(8,128)(2,1)}, u32[]{:S(2)}) copy-start(bf16[1,1281,320]{1,2,0:T(8,128)(2,1)} %param.7) | copy-start | bytes 2459524
  41.7 10.7 %collective-permute-start.3 = (bf16[320,1281]{1,0:T(8,128)(2,1)S(1)}, bf16[320,1281]{1,0:T(8,128)(2,1)S(1)}, u32[]{:S(2)}, u32[]{:S(2)}) collective-permute-start(bf16[320,1281]{1,0:T(8,128)(2,1)S(1)} %pass_on.3.refs_2_), channel_id=1, source_target_pairs={{0,1},{1,0},{2,3},{3,2},{4,5},{5,4},{6,7},{7,6},{8,9},{9,8},{10,11... | collective-permute-start | bytes 2459528 | tf_op jit(solution)/shard_map/ppermute | solution.py:268
  45.7 6.7 %collective-permute-start.4 = (bf16[320,1281]{1,0:T(8,128)(2,1)S(1)}, bf16[320,1281]{1,0:T(8,128)(2,1)S(1)}, u32[]{:S(2)}, u32[]{:S(2)}) collective-permute-start(bf16[320,1281]{1,0:T(8,128)(2,1)S(1)} %pass_on.4.refs_3_), channel_id=1, source_target_pairs={{0,1},{1,0},{2,3},{3,2},{4,5},{5,4},{6,7},{7,6},{8,9},{9,8},{10,11... | collective-permute-start | bytes 2459528 | tf_op jit(solution)/shard_map/ppermute | solution.py:268
  49.9 4.5 %collective-permute-start.6 = (bf16[320,1281]{1,0:T(8,128)(2,1)S(1)}, bf16[320,1281]{1,0:T(8,128)(2,1)S(1)}, u32[]{:S(2)}, u32[]{:S(2)}) collective-permute-start(bf16[320,1281]{1,0:T(8,128)(2,1)S(1)} %pass_on.5.refs_2_.refs_6_), channel_id=1, source_target_pairs={{0,1},{1,0},{2,3},{3,2},{4,5},{5,4},{6,7},{7,6},{8,9},{9,8},{10,11... | collective-permute-start | bytes 2459528 | tf_op jit(solution)/shard_map/ppermute | solution.py:268

commit v3 on v2

--- a/solution.py
+++ b/solution.py
@@ -19,6 +19,7 @@
 HALF = 640
 NEAR = 8 * 10**9
 NEARS = 4
+FARS = 3
 
 NT = (((1,), (1,)), ((), ()))
 NN = (((1,), (0,)), ((), ()))
@@ -138,21 +139,24 @@
 
 
 def near_kernel(lev_ref, w_ref, *refs):
-    tabs, raw_ref, kept_refs, sems = refs[:NEARS], refs[NEARS], refs[NEARS + 1:-1], refs[-1]
-    copies = [pltpu.make_async_copy(tabs[n], kept_refs[n], sems.at[n]) for n in range(NEARS)]
+    tabs, raw_ref, turned, held, sems = refs[:NEARS], refs[NEARS], refs[NEARS + 1:2 * NEARS + 1], refs[-2], refs[-1]
+    copies = [pltpu.make_async_copy(tabs[n], held.at[n], sems.at[n]) for n in range(NEARS)]
     for copy in copies:
         copy.start()
     slabs = slab_order(lev_ref[0])
     raw = None
     for n in range(NEARS):
         copies[n].wait()
-        raw = add_up(raw, w_ref, slabs[n:n + 1], [kept_refs[n]])
+        raw = add_up(raw, w_ref, slabs[n:n + 1], [held.at[n]])
+        turned[n][...] = held[n].T
     raw_ref[...] = raw
 
 
 def far_kernel(lev_ref, w_ref, raw_ref, *refs):
-    *tabs, total_ref = refs
-    total_ref[...] = add_up(raw_ref[...], w_ref, slab_order(lev_ref[0])[4:], tabs)
+    tabs, total_ref, turned = refs[:FARS], refs[FARS], refs[FARS + 1:]
+    total_ref[...] = add_up(raw_ref[...], w_ref, slab_order(lev_ref[0])[NEARS:], tabs)
+    for tab, turn in zip(tabs, turned):
+        turn[...] = tab[...].T
 
 
 def pass_kernel(token_ref, tab_ref, same_ref):
@@ -177,8 +181,9 @@
     expanded = jnp.concatenate([jnp.where(first, spec, 0.0), jnp.where(first, 0.0, spec)], axis=0).astype(jnp.bfloat16)
     spread = spread_rows()
     group = own_group()
-    for slab, tab in zip(slabs, tabs):
-        rows = jnp.where(members(scale_ref[slab]) > 0.0, mul(expanded, tab[...], NT), 0.0)
+    for n, slab in enumerate(slabs):
+        rows = mul(expanded, tabs[n][...], NN if n < NEARS + FARS else NT)
+        rows = jnp.where(members(scale_ref[slab]) > 0.0, rows, 0.0)
         rows = jnp.where(group, jnp.concatenate([rows] * 4, axis=0), 0.0).astype(jnp.bfloat16)
         block = mul(spread, rows, NT)
         place = pl.ds(pl.multiple_of(slab * SLABS, SLABS), SLABS)
@@ -238,17 +243,22 @@
 RAW = jax.ShapeDtypeStruct((COLS, KP), jnp.float32)
 
 
+TURNED = jax.ShapeDtypeStruct((KP, SLAB), jnp.bfloat16)
+
+
 def near(lev, w, tabs):
     return pl.pallas_call(
-        near_kernel, out_shape=(RAW,) + tuple(like(t) for t in tabs), in_specs=[SMEM, VMEM] + [ANY] * NEARS,
-        out_specs=(VMEM,) * (1 + NEARS), scratch_shapes=[pltpu.SemaphoreType.DMA((NEARS,))],
-        compiler_params=params(8), cost_estimate=pl.CostEstimate(flops=NEAR, bytes_accessed=0, transcendentals=0),
+        near_kernel, out_shape=(RAW,) + (TURNED,) * NEARS, in_specs=[SMEM, VMEM] + [ANY] * NEARS,
+        out_specs=(VMEM,) * (1 + NEARS),
+        scratch_shapes=[pltpu.VMEM((NEARS, SLAB, KP), jnp.bfloat16), pltpu.SemaphoreType.DMA((NEARS,))],
+        compiler_params=params(12), cost_estimate=pl.CostEstimate(flops=NEAR, bytes_accessed=0, transcendentals=0),
         name="near")(lev, w, *tabs)
 
 
 def far(lev, w, raw, tabs):
     return pl.pallas_call(
-        far_kernel, out_shape=RAW, in_specs=[SMEM] + [VMEM] * (2 + len(tabs)), out_specs=VMEM,
+        far_kernel, out_shape=(RAW,) + (TURNED,) * FARS, in_specs=[SMEM] + [VMEM] * (2 + FARS),
+        out_specs=(VMEM,) * (1 + FARS),
         compiler_params=params(8), cost_estimate=cost(COLS, 3 * SLAB, KP), name="far")(lev, w, raw, *tabs)
 
 
@@ -284,9 +294,9 @@
     weighted = weigh(moved, scale)
     raw, *tabs = near(lev, weighted, [own, twin, first, second])
     third = pass_on(raw, third)
-    tabs += cores + [third]
-    raw = far(lev, weighted, raw, tabs[NEARS:])
-    tabs += [other_core(third)]
+    last = other_core(third)
+    raw, *more = far(lev, weighted, raw, cores + [third])
+    tabs += more + [last]
     result = solve(pair_low, lev, level, weighted, scale, raw, tabs)
     back = lax.all_to_all(result, "wave", split_axis=0, concat_axis=0, tiled=True)
     return unpack(back)

time: 80.5 us -> 79.2 us (0.984)
    pallas_call x1, Pallas kernels: 4.94 us -> 3.59 us  [solve(): pl.pallas_call(solve_kernel, out_shape=chunks(), in_specs=[SMEM] * 2 + [V...]
  transfers between devices with their start and end apart: 8 -> 8, of which waited for: 3 -> 3; matrix products, arithmetic and copies ran while one was open for 0% -> 0% of each run, Pallas kernels for 7% -> 8%
where the time goes in v3:
time: 79.2 us; the launch traced here: 78.5 us
  starting transfers between devices  36.7 us (46%)
  blocking collectives  19 us (24%)
  Pallas kernels  11.1 us (14%)
  waiting for transfers between devices  9.22 us (12%)
  local copies, waits for them, and re-layouts  1.59 us (2%)
  between operations  0.88 us (1%)
    all_to_all x1, blocking collectives, local(): lax.all_to_all(result, 'wave', split_axis=0, concat_axis=0, tiled=True)  19 us
    ppermute x4, starting transfers between devices, other_core(): return lax.ppermute(array, 'lev', [(d, d ^ 1) for d in range(SLABS)])  17 us
    all_to_all x1, starting transfers between devices, local(): lax.all_to_all(sent, 'wave', split_axis=0, concat_axis=0, tiled=True)  13.5 us
    all_to_all x1, waiting for transfers between devices, local(): lax.all_to_all(sent, 'wave', split_axis=0, concat_axis=0, tiled=True)  7.68 us
    ppermute x3, starting transfers between devices, along_x(): lax.ppermute(array, 'lev', [(d, (d + 2 - 4 * (d % 2)) % SLABS) for d in r...  6.2 us
    pallas_call x1, Pallas kernels, solve(): pl.pallas_call(solve_kernel, out_shape=chunks(), in_specs=[SMEM] * 2 + [V...  3.59 us
    pallas_call x1, Pallas kernels, near(): pl.pallas_call(near_kernel, out_shape=(RAW,) + (TURNED,) * NEARS, in_spec...  2.54 us
  transfers between devices with their start and end apart: 8, of which 3 were waited for; matrix products, arithmetic and copies ran while one was open for 0% of the time, Pallas kernels for 8%

profile of v3, /device:TPU:1, one launch (start us, length us, event | category | flops | bytes accessed | tf_op | source)
XLA Modules:
  0.0 78.5 jit_solution(17949621607411485983)
XLA Ops:
  0.0 8.8 %collective-permute-start = (bf16[320,1281]{1,0:T(8,128)(2,1)}, bf16[320,1281]{1,0:T(8,128)(2,1)}, u32[]{:S(2)}, u32[]{:S(2)}) collective-permute-start(bf16[320,1281]{1,0:T(8,128)(2,1)} %bitcast.4), channel_id=1, source_target_pairs={{0,1},{1,0},{2,3},{3,2},{4,5},{5,4},{6,7},{7,6},{8,9},{9,8},{10,11... | collective-permute-start | bytes 2459528 | tf_op jit(solution)/shard_map/ppermute | solution.py:278
  8.8 1.9 %collective-permute-start.1 = (bf16[320,1281]{1,0:T(8,128)(2,1)}, bf16[320,1281]{1,0:T(8,128)(2,1)S(1)}, u32[]{:S(2)}, u32[]{:S(2)}) collective-permute-start(bf16[320,1281]{1,0:T(8,128)(2,1)} %bitcast.5), channel_id=1, source_target_pairs={{0,2},{1,7},{2,4},{3,1},{4,6},{5,3},{6,0},{7,5},{8,10},{9,15},{10,... | collective-permute-start | bytes 2459528 | tf_op jit(solution)/shard_map/ppermute | solution.py:274
  10.7 0.5 collective-permute-done.refs_1_
  11.2 1.9 %collective-permute-start.2 = (bf16[320,1281]{1,0:T(8,128)(2,1)}, bf16[320,1281]{1,0:T(8,128)(2,1)S(1)}, u32[]{:S(2)}, u32[]{:S(2)}) collective-permute-start(bf16[320,1281]{1,0:T(8,128)(2,1)} %collective-permute-done.refs_1_), channel_id=1, source_target_pairs={{0,2},{1,7},{2,4},{3,1},{4,6},{5,3},{6,0},{7,5},{8,10},{9,15},{10,... | collective-permute-start | bytes 2459528 | tf_op jit(solution)/shard_map/ppermute | solution.py:274
  13.1 0.9 %copy-done.3 = bf16[2,4,40,256]{3,2,1,0:T(8,128)(2,1)S(1)} copy-done((bf16[2,4,40,256]{3,2,1,0:T(8,128)(2,1)S(1)}, bf16[2,4,40,256]{3,2,1,0:T(8,128)(2,1)}, u32[]{:S(2)}) %copy-start.3) | copy-done | bytes 163864
  14.0 1.5 %pack.1.token_ref = bf16[64,2,640]{2,1,0:T(2,128)(2,1)} custom-call(bf16[2,4,40,256]{3,2,1,0:T(8,128)(2,1)S(1)} %copy-done.3), custom_call_target="tpu_custom_call" | custom-call | flops 419758080 | bytes 1639680 | tf_op jit(solution)/shard_map/pack/pallas_call | solution.py:209
  15.5 13.5 %all-to-all-start = ((bf16[64,2,640]{2,1,0:T(2,128)(2,1)}), bf16[64,2,640]{2,1,0:T(2,128)(2,1)S(1)}, u32[]{:S(2)}, u32[]{:S(2)}) async-start(bf16[64,2,640]{2,1,0:T(2,128)(2,1)} %pack.1.token_ref), calls=%async_computation | async-start | bytes 327680 | tf_op jit(solution)/shard_map/all_to_all | solution.py:288
  29.0 0.0 collective-permute-done.1.tab_ref
  29.0 0.0 copy-start.4
  29.1 2.4 %collective-permute-start.5 = (bf16[320,1281]{1,0:T(8,128)(2,1)S(1)}, bf16[320,1281]{1,0:T(8,128)(2,1)S(1)}, u32[]{:S(2)}, u32[]{:S(2)}) collective-permute-start(bf16[320,1281]{1,0:T(8,128)(2,1)S(1)} %pass_on.3.refs_2_), channel_id=1, source_target_pairs={{0,2},{1,7},{2,4},{3,1},{4,6},{5,3},{6,0},{7,5},{8,10},{9,15},{10,... | collective-permute-start | bytes 2459528 | tf_op jit(solution)/shard_map/ppermute | solution.py:274
  32.1 0.0 copy-start
  32.1 0.0 copy-start.1
  32.1 0.6 copy-done
  32.8 0.0 copy-done.1
  32.8 0.8 coef.1
  33.6 7.7 %all-to-all-done.y_ref = bf16[64,2,640]{2,1,0:T(2,128)(2,1)S(1)} async-done(((bf16[64,2,640]{2,1,0:T(2,128)(2,1)}), bf16[64,2,640]{2,1,0:T(2,128)(2,1)S(1)}, u32[]{:S(2)}, u32[]{:S(2)}) %all-to-all-start) | async-done | bytes 163872 | tf_op jit(solution)/shard_map/all_to_all | solution.py:288
  41.2 0.4 weigh.1.w_ref
  41.7 0.0 copy-start.2
  41.7 3.9 %collective-permute-start.3 = (bf16[320,1281]{1,0:T(8,128)(2,1)S(1)}, bf16[320,1281]{1,0:T(8,128)(2,1)S(1)}, u32[]{:S(2)}, u32[]{:S(2)}) collective-permute-start(bf16[320,1281]{1,0:T(8,128)(2,1)S(1)} %pass_on.3.refs_2_), channel_id=1, source_target_pairs={{0,1},{1,0},{2,3},{3,2},{4,5},{5,4},{6,7},{7,6},{8,9},{9,8},{10,11... | collective-permute-start | bytes 2459528 | tf_op jit(solution)/shard_map/ppermute | solution.py:278
  45.7 0.0 collective-permute-done.2.tab_ref
  45.7 1.9 %collective-permute-start.4 = (bf16[320,1281]{1,0:T(8,128)(2,1)S(1)}, bf16[320,1281]{1,0:T(8,128)(2,1)S(1)}, u32[]{:S(2)}, u32[]{:S(2)}) collective-permute-start(bf16[320,1281]{1,0:T(8,128)(2,1)S(1)} %pass_on.4.refs_3_), channel_id=1, source_target_pairs={{0,1},{1,0},{2,3},{3,2},{4,5},{5,4},{6,7},{7,6},{8,9},{9,8},{10,11... | collective-permute-start | bytes 2459528 | tf_op jit(solution)/shard_map/ppermute | solution.py:278
  47.6 0.0 copy-done.2
  47.6 2.5 %near.1 = (f32[32,1281]{1,0:T(8,128)S(1)}, bf16[1281,320]{1,0:T(8,128)(2,1)S(1)}, bf16[1281,320]{1,0:T(8,128)(2,1)S(1)}, bf16[1281,320]{1,0:T(8,128)(2,1)S(1)}, bf16[1281,320]{1,0:T(8,128)(2,1)S(1)}) custom-call(s32[1]{0:T(128)} %bitcast.lev_ref, bf16[8,32,320]{2,1,0:T(8,128)(2,1)S(1)} %weigh.1.w_ref, bf16[320,1281]{1,0:T(8,128)(2,1)S(1)} %bitcast.6, ...), custom_call_target="tpu_custom_call" | custom-call | flops 8000000000 | tf_op jit(solution)/shard_map/near/pallas_call | solution.py:250
  50.2 0.0 collective-permute-done.5.tab_ref
  50.2 2.4 %collective-permute-start.6 = (bf16[320,1281]{1,0:T(8,128)(2,1)S(1)}, bf16[320,1281]{1,0:T(8,128)(2,1)S(1)}, u32[]{:S(2)}, u32[]{:S(2)}) collective-permute-start(bf16[320,1281]{1,0:T(8,128)(2,1)S(1)} %pass_on.5.refs_2_), channel_id=1, source_target_pairs={{0,1},{1,0},{2,3},{3,2},{4,5},{5,4},{6,7},{7,6},{8,9},{9,8},{10,11... | collective-permute-start | bytes 2459528 | tf_op jit(solution)/shard_map/ppermute | solution.py:278
  52.6 0.0 collective-permute-done.3.refs_0_
  52.6 0.0 collective-permute-done.4.refs_1_
  52.6 1.0 %far.1 = (f32[32,1281]{1,0:T(8,128)S(1)}, bf16[1281,320]{1,0:T(8,128)(2,1)S(1)}, bf16[1281,320]{1,0:T(8,128)(2,1)S(1)}, bf16[1281,320]{1,0:T(8,128)(2,1)S(1)}) custom-call(s32[1]{0:T(128)} %bitcast.lev_ref, bf16[8,32,320]{2,1,0:T(8,128)(2,1)S(1)} %weigh.1.w_ref, f32[32,1281]{1,0:T(8,128)S(1)} %get-tuple-element.18.token_ref.raw_ref, ...), custom_call_target="tpu_custom_call" | custom-call | flops 629637120 | bytes 2459520 | tf_op jit(solution)/shard_map/far/pallas_call | solution.py:259
  53.6 1.1 %collective-permute-done.6.refs_7_ = bf16[320,1281]{1,0:T(8,128)(2,1)S(1)} collective-permute-done((bf16[320,1281]{1,0:T(8,128)(2,1)S(1)}, bf16[320,1281]{1,0:T(8,128)(2,1)S(1)}, u32[]{:S(2)}, u32[]{:S(2)}) %collective-permute-start.6) | collective-permute-done | bytes 819872 | tf_op jit(solution)/shard_map/ppermute | solution.py:278
  54.6 3.6 %solve.1 = bf16[64,2,640]{2,1,0:T(2,128)(2,1)S(1)} custom-call(s32[1]{0:T(128)S(6)} %copy.13.low_ref, s32[1]{0:T(128)} %bitcast.lev_ref, f32[2,8,128]{2,1,0:T(8,128)S(1)} %get-tuple-element.16.level_ref, bf16[8,32,320]{2,1,0:T(8,128)(2,1)S(1)} %weigh.1.w_ref, f32[8,2,320]{2,1,0:T(2,128)S(1)} %get-tuple-element.17.scale_ref, ...), custom_call_target="tpu_custom_call" | custom-call | flops 1888911360 | bytes 7378560 | tf_op jit(solution)/shard_map/solve/pallas_call | solution.py:266
  58.2 19.0 %all_to_all.10.b_ref = bf16[64,2,640]{2,1,0:T(2,128)(2,1)S(1)} all-to-all(bf16[64,2,640]{2,1,0:T(2,128)(2,1)S(1)} %solve.1), channel_id=1, replica_groups=mesh['wave'=64,'lev'=8] {'wave'}, dimensions={0} | all-to-all | bytes 327680 | tf_op jit(solution)/shard_map/all_to_all | solution.py:301
  77.2 1.3 %unpack.1 = bf16[2,4,40,256]{3,2,1,0:T(8,128)(2,1)} custom-call(bf16[64,2,640]{2,1,0:T(2,128)(2,1)S(1)} %all_to_all.10.b_ref), custom_call_target="tpu_custom_call" | custom-call | flops 419758080 | bytes 1311744 | tf_op jit(solution)/shard_map/unpack/pallas_call | solution.py:214
  (6 shorter events, 0.0 us)
Async XLA Ops:
  0.0 11.2 %collective-permute-start = (bf16[320,1281]{1,0:T(8,128)(2,1)}, bf16[320,1281]{1,0:T(8,128)(2,1)}, u32[]{:S(2)}, u32[]{:S(2)}) collective-permute-start(bf16[320,1281]{1,0:T(8,128)(2,1)} %bitcast.4), channel_id=1, source_target_pairs={{0,1},{1,0},{2,3},{3,2},{4,5},{5,4},{6,7},{7,6},{8,9},{9,8},{10,11... | collective-permute-start | bytes 2459528 | tf_op jit(solution)/shard_map/ppermute | solution.py:278
  8.8 20.3 %collective-permute-start.1 = (bf16[320,1281]{1,0:T(8,128)(2,1)}, bf16[320,1281]{1,0:T(8,128)(2,1)S(1)}, u32[]{:S(2)}, u32[]{:S(2)}) collective-permute-start(bf16[320,1281]{1,0:T(8,128)(2,1)} %bitcast.5), channel_id=1, source_target_pairs={{0,2},{1,7},{2,4},{3,1},{4,6},{5,3},{6,0},{7,5},{8,10},{9,15},{10,... | collective-permute-start | bytes 2459528 | tf_op jit(solution)/shard_map/ppermute | solution.py:274
  11.2 34.5 %collective-permute-start.2 = (bf16[320,1281]{1,0:T(8,128)(2,1)}, bf16[320,1281]{1,0:T(8,128)(2,1)S(1)}, u32[]{:S(2)}, u32[]{:S(2)}) collective-permute-start(bf16[320,1281]{1,0:T(8,128)(2,1)} %collective-permute-done.refs_1_), channel_id=1, source_target_pairs={{0,2},{1,7},{2,4},{3,1},{4,6},{5,3},{6,0},{7,5},{8,10},{9,15},{10,... | collective-permute-start | bytes 2459528 | tf_op jit(solution)/shard_map/ppermute | solution.py:274
  13.1 0.9 %copy-start.3 = (bf16[2,4,40,256]{3,2,1,0:T(8,128)(2,1)S(1)}, bf16[2,4,40,256]{3,2,1,0:T(8,128)(2,1)}, u32[]{:S(2)}) copy-start(bf16[2,4,40,256]{3,2,1,0:T(8,128)(2,1)} %x_ref.1) | copy-start | bytes 491524
  15.5 25.7 %all-to-all-start = ((bf16[64,2,640]{2,1,0:T(2,128)(2,1)}), bf16[64,2,640]{2,1,0:T(2,128)(2,1)S(1)}, u32[]{:S(2)}, u32[]{:S(2)}) async-start(bf16[64,2,640]{2,1,0:T(2,128)(2,1)} %pack.1.token_ref), calls=%async_computation | async-start | bytes 327680 | tf_op jit(solution)/shard_map/all_to_all | solution.py:288
  29.0 3.0 %copy-start.4 = (s32[2560]{0:T(1024)S(1)}, s32[2560]{0:T(1024)}, u32[]{:S(2)}) copy-start(s32[2560]{0:T(1024)} %param.8) | copy-start | bytes 30724
  29.1 21.1 %collective-permute-start.5 = (bf16[320,1281]{1,0:T(8,128)(2,1)S(1)}, bf16[320,1281]{1,0:T(8,128)(2,1)S(1)}, u32[]{:S(2)}, u32[]{:S(2)}) collective-permute-start(bf16[320,1281]{1,0:T(8,128)(2,1)S(1)} %pass_on.3.refs_2_), channel_id=1, source_target_pairs={{0,2},{1,7},{2,4},{3,1},{4,6},{5,3},{6,0},{7,5},{8,10},{9,15},{10,... | collective-permute-start | bytes 2459528 | tf_op jit(solution)/shard_map/ppermute | solution.py:274
  32.1 0.7 copy-start
  32.1 0.7 copy-start.1
  41.7 5.9 %copy-start.2 = (bf16[1,1281,320]{1,2,0:T(8,128)(2,1)S(1)}, bf16[1,1281,320]{1,2,0:T(8,128)(2,1)}, u32[]{:S(2)}) copy-start(bf16[1,1281,320]{1,2,0:T(8,128)(2,1)} %param.7) | copy-start | bytes 2459524
  41.7 10.9 %collective-permute-start.3 = (bf16[320,1281]{1,0:T(8,128)(2,1)S(1)}, bf16[320,1281]{1,0:T(8,128)(2,1)S(1)}, u32[]{:S(2)}, u32[]{:S(2)}) collective-permute-start(bf16[320,1281]{1,0:T(8,128)(2,1)S(1)} %pass_on.3.refs_2_), channel_id=1, source_target_pairs={{0,1},{1,0},{2,3},{3,2},{4,5},{5,4},{6,7},{7,6},{8,9},{9,8},{10,11... | collective-permute-start | bytes 2459528 | tf_op jit(solution)/shard_map/ppermute | solution.py:278
  45.7 6.9 %collective-permute-start.4 = (bf16[320,1281]{1,0:T(8,128)(2,1)S(1)}, bf16[320,1281]{1,0:T(8,128)(2,1)S(1)}, u32[]{:S(2)}, u32[]{:S(2)}) collective-permute-start(bf16[320,1281]{1,0:T(8,128)(2,1)S(1)} %pass_on.4.refs_3_), channel_id=1, source_target_pairs={{0,1},{1,0},{2,3},{3,2},{4,5},{5,4},{6,7},{7,6},{8,9},{9,8},{10,11... | collective-permute-start | bytes 2459528 | tf_op jit(solution)/shard_map/ppermute | solution.py:278
  50.2 4.5 %collective-permute-start.6 = (bf16[320,1281]{1,0:T(8,128)(2,1)S(1)}, bf16[320,1281]{1,0:T(8,128)(2,1)S(1)}, u32[]{:S(2)}, u32[]{:S(2)}) collective-permute-start(bf16[320,1281]{1,0:T(8,128)(2,1)S(1)} %pass_on.5.refs_2_), channel_id=1, source_target_pairs={{0,1},{1,0},{2,3},{3,2},{4,5},{5,4},{6,7},{7,6},{8,9},{9,8},{10,11... | collective-permute-start | bytes 2459528 | tf_op jit(solution)/shard_map/ppermute | solution.py:278

commit v4 on v3

--- a/solution.py
+++ b/solution.py
@@ -17,9 +17,9 @@
 STEPS = R // 4
 COLS = 32
 HALF = 640
-NEAR = 8 * 10**9
-NEARS = 4
-FARS = 3
+NEAR = 73 * 10**8
+NEARS = 3
+FARS = 4
 
 NT = (((1,), (1,)), ((), ()))
 NN = (((1,), (0,)), ((), ()))
@@ -58,9 +58,17 @@
     return ((lane >> 4) & 1) * 2 + (lane & 1)
 
 
-def pack_kernel(x_ref, o_ref):
-    x = x_ref[...].astype(jnp.float32).reshape(F * V * R, 4 * PAIRS).astype(jnp.bfloat16)
+def pack_kernel(x_ref, tab_ref, o_ref, copy_ref, held_x, held_tab, sems):
+    get_x = pltpu.make_async_copy(x_ref, held_x, sems.at[0])
+    get_tab = pltpu.make_async_copy(tab_ref, held_tab, sems.at[1])
+    put_tab = pltpu.make_async_copy(held_tab, copy_ref, sems.at[2])
+    get_x.start()
+    get_tab.start()
+    get_x.wait()
+    x = held_x[...].astype(jnp.float32).reshape(F * V * R, 4 * PAIRS).astype(jnp.bfloat16)
     turned = mul(by_member(), x, NT).astype(jnp.bfloat16)
+    get_tab.wait()
+    put_tab.start()
     placed = mul(turned, by_place(), NN)
     part = lane_part((PAIRS, STEPS * 128))
     out = placed[:PAIRS]
@@ -68,6 +76,7 @@
         out = jnp.where(part == q, placed[q * PAIRS:(q + 1) * PAIRS], out)
     halves = jnp.stack([out[:, :HALF], out[:, HALF:]], axis=0)
     o_ref[...] = jnp.swapaxes(halves, 0, 1).astype(jnp.bfloat16)
+    put_tab.wait()
 
 
 def unpack_kernel(b_ref, o_ref):
@@ -127,8 +136,8 @@
 
 def slab_order(lev):
     way = 2 - 4 * (lev & 1)
-    behind, ahead, far = (lev - way) & 7, (lev + way) & 7, (lev + 4) & 7
-    return [lev, lev ^ 1, behind, behind ^ 1, ahead ^ 1, ahead, far, far ^ 1]
+    behind, ahead, far = (lev - way) & 7, (lev + way) & 7, lev ^ 4
+    return [lev, behind, ahead, lev ^ 1, ahead ^ 1, behind ^ 1, far, far ^ 1]
 
 
 def add_up(raw, w_ref, slabs, tabs):
@@ -139,16 +148,17 @@
 
 
 def near_kernel(lev_ref, w_ref, *refs):
-    tabs, raw_ref, turned, held, sems = refs[:NEARS], refs[NEARS], refs[NEARS + 1:2 * NEARS + 1], refs[-2], refs[-1]
-    copies = [pltpu.make_async_copy(tabs[n], held.at[n], sems.at[n]) for n in range(NEARS)]
+    tabs, raw_ref, turned, same_ref, held, sems = refs[:NEARS], refs[NEARS], refs[NEARS + 1:-3], *refs[-3:]
+    places = [same_ref] + [held.at[n] for n in range(NEARS - 1)]
+    copies = [pltpu.make_async_copy(tabs[n], places[n], sems.at[n]) for n in range(NEARS)]
     for copy in copies:
         copy.start()
     slabs = slab_order(lev_ref[0])
     raw = None
     for n in range(NEARS):
         copies[n].wait()
-        raw = add_up(raw, w_ref, slabs[n:n + 1], [held.at[n]])
-        turned[n][...] = held[n].T
+        raw = add_up(raw, w_ref, slabs[n:n + 1], places[n:n + 1])
+        turned[n][...] = places[n][...].T
     raw_ref[...] = raw
 
 
@@ -205,9 +215,11 @@
     return jax.ShapeDtypeStruct((PAIRS, 2, HALF), jnp.bfloat16)
 
 
-def pack(x):
-    return pl.pallas_call(pack_kernel, out_shape=chunks(), in_specs=[VMEM], out_specs=VMEM,
-                          compiler_params=params(12), cost_estimate=cost(PAIRS * 4, SLAB, 2 * KP), name="pack")(x)
+def pack(x, tab):
+    return pl.pallas_call(
+        pack_kernel, out_shape=(chunks(), like(tab)), in_specs=[ANY, ANY], out_specs=(VMEM, ANY),
+        scratch_shapes=[pltpu.VMEM(x.shape, x.dtype), pltpu.VMEM(tab.shape, tab.dtype), pltpu.SemaphoreType.DMA((3,))],
+        compiler_params=params(60), cost_estimate=cost(PAIRS * 4, SLAB, 2 * KP), name="pack")(x, tab)
 
 
 def unpack(b):
@@ -248,9 +260,9 @@
 
 def near(lev, w, tabs):
     return pl.pallas_call(
-        near_kernel, out_shape=(RAW,) + (TURNED,) * NEARS, in_specs=[SMEM, VMEM] + [ANY] * NEARS,
-        out_specs=(VMEM,) * (1 + NEARS),
-        scratch_shapes=[pltpu.VMEM((NEARS, SLAB, KP), jnp.bfloat16), pltpu.SemaphoreType.DMA((NEARS,))],
+        near_kernel, out_shape=(RAW,) + (TURNED,) * NEARS + (like(tabs[0]),),
+        in_specs=[SMEM, VMEM] + [ANY] * NEARS, out_specs=(VMEM,) * (2 + NEARS),
+        scratch_shapes=[pltpu.VMEM((NEARS - 1, SLAB, KP), jnp.bfloat16), pltpu.SemaphoreType.DMA((NEARS,))],
         compiler_params=params(12), cost_estimate=pl.CostEstimate(flops=NEAR, bytes_accessed=0, transcendentals=0),
         name="near")(lev, w, *tabs)
 
@@ -259,7 +271,7 @@
     return pl.pallas_call(
         far_kernel, out_shape=(RAW,) + (TURNED,) * FARS, in_specs=[SMEM] + [VMEM] * (2 + FARS),
         out_specs=(VMEM,) * (1 + FARS),
-        compiler_params=params(8), cost_estimate=cost(COLS, 3 * SLAB, KP), name="far")(lev, w, raw, *tabs)
+        compiler_params=params(8), cost_estimate=cost(COLS, 4 * SLAB, KP), name="far")(lev, w, raw, *tabs)
 
 
 def solve(low, lev, level, w, scale, raw, tabs):
@@ -270,8 +282,8 @@
         name="solve")(low, lev, level, w, scale, raw, *tabs)
 
 
-def along_x(array):
-    return lax.ppermute(array, "lev", [(d, (d + 2 - 4 * (d % 2)) % SLABS) for d in range(SLABS)])
+def along_x(array, step):
+    return lax.ppermute(array, "lev", [(d, (d + 2 * step * (1 - 2 * (d % 2))) % SLABS) for d in range(SLABS)])
 
 
 def other_core(array):
@@ -281,21 +293,20 @@
 def local(fourier_in, table, points, pair_low, gamma, beta):
     lev = lax.axis_index("lev").astype(jnp.int32).reshape(1)
     own = jnp.swapaxes(table, 1, 2)[0]
-    twin = other_core(own)
-    first = along_x(own)
-    second = along_x(twin)
-    sent = pack(fourier_in)
+    first = along_x(own, 1)
+    sent, own = pack(fourier_in, own)
+    second = along_x(own, -1)
     moved = lax.all_to_all(sent, "wave", split_axis=0, concat_axis=0, tiled=True)
     first = pass_on(sent, first)
-    third = along_x(first)
+    third = along_x(first, 1)
     second = pass_on(sent, second)
     cores = [other_core(first), other_core(second)]
     scale, level = coef(pair_low, lev, gamma, beta, points.reshape(1, NLAT))
     weighted = weigh(moved, scale)
-    raw, *tabs = near(lev, weighted, [own, twin, first, second])
+    raw, *tabs, own = near(lev, weighted, [own, first, second])
     third = pass_on(raw, third)
     last = other_core(third)
-    raw, *more = far(lev, weighted, raw, cores + [third])
+    raw, *more = far(lev, weighted, raw, [other_core(own)] + cores + [third])
     tabs += more + [last]
     result = solve(pair_low, lev, level, weighted, scale, raw, tabs)
     back = lax.all_to_all(result, "wave", split_axis=0, concat_axis=0, tiled=True)

time: 79.2 us -> 78.1 us (0.986)
  waiting for transfers between devices: 9.22 us -> 6.21 us
  starting transfers between devices: 36.7 us -> 39.2 us
  blocking collectives: 19 us -> 17.4 us
  Pallas kernels: 11.1 us -> 11.9 us
    ppermute x4, starting transfers between devices: 17 us -> 11.1 us  [other_core(): return lax.ppermute(array, 'lev', [(d, d ^ 1) for d in range(SLABS)])]
    ppermute x3, starting transfers between devices: 6.2 us -> 11.7 us  [along_x(): lax.ppermute(array, 'lev', [(d, (d + 2 * step * (1 - 2 * (d % 2))) % SLAB...]
    all_to_all x1, starting transfers between devices: 13.5 us -> 16.5 us  [local(): lax.all_to_all(sent, 'wave', split_axis=0, concat_axis=0, tiled=True)]
    all_to_all x1, waiting for transfers between devices: 7.68 us -> 5.04 us  [local(): lax.all_to_all(sent, 'wave', split_axis=0, concat_axis=0, tiled=True)]
    all_to_all x1, blocking collectives: 19 us -> 17.4 us  [local(): lax.all_to_all(result, 'wave', split_axis=0, concat_axis=0, tiled=True)]
  transfers between devices with their start and end apart: 8 -> 8, of which waited for: 3 -> 3; matrix products, arithmetic and copies ran while one was open for 0% -> 0% of each run, Pallas kernels for 8% -> 9%
where the time goes in v4:
time: 78.1 us; the launch traced here: 77.4 us
  starting transfers between devices  39.2 us (50%)
  blocking collectives  17.4 us (22%)
  Pallas kernels  11.9 us (15%)
  waiting for transfers between devices  6.21 us (8%)
  local copies, waits for them, and re-layouts  1.83 us (2%)
  between operations  0.89 us (1%)
    all_to_all x1, blocking collectives, local(): lax.all_to_all(result, 'wave', split_axis=0, concat_axis=0, tiled=True)  17.4 us
    all_to_all x1, starting transfers between devices, local(): lax.all_to_all(sent, 'wave', split_axis=0, concat_axis=0, tiled=True)  16.5 us
    ppermute x3, starting transfers between devices, along_x(): lax.ppermute(array, 'lev', [(d, (d + 2 * step * (1 - 2 * (d % 2))) % SLAB...  11.7 us
    ppermute x4, starting transfers between devices, other_core(): return lax.ppermute(array, 'lev', [(d, d ^ 1) for d in range(SLABS)])  11.1 us
    all_to_all x1, waiting for transfers between devices, local(): lax.all_to_all(sent, 'wave', split_axis=0, concat_axis=0, tiled=True)  5.04 us
    pallas_call x1, Pallas kernels, solve(): pl.pallas_call(solve_kernel, out_shape=chunks(), in_specs=[SMEM] * 2 + [V...  3.59 us
    pallas_call x1, Pallas kernels, pack(): pl.pallas_call(pack_kernel, out_shape=(chunks(), like(tab)), in_specs=[AN...  2.87 us
    unnamed x10, local copies, waits for them, and re-layouts  1.82 us
  transfers between devices with their start and end apart: 8, of which 3 were waited for; matrix products, arithmetic and copies ran while one was open for 0% of the time, Pallas kernels for 9%

profile of v4, /device:TPU:1, one launch (start us, length us, event | category | flops | bytes accessed | tf_op | source)
XLA Modules:
  0.0 77.4 jit_solution(1840383520440263033)
XLA Ops:
  0.0 5.2 %collective-permute-start = (bf16[320,1281]{1,0:T(8,128)(2,1)}, bf16[320,1281]{1,0:T(8,128)(2,1)S(1)}, u32[]{:S(2)}, u32[]{:S(2)}) collective-permute-start(bf16[320,1281]{1,0:T(8,128)(2,1)} %bitcast.4), channel_id=1, source_target_pairs={{0,2},{1,7},{2,4},{3,1},{4,6},{5,3},{6,0},{7,5},{8,10},{9,15},{10,... | collective-permute-start | bytes 2459528 | tf_op jit(solution)/shard_map/ppermute | solution.py:286
  5.2 2.9 %pack.1 = (bf16[64,2,640]{2,1,0:T(2,128)(2,1)}, bf16[320,1281]{1,0:T(8,128)(2,1)}) custom-call(bf16[2,4,40,256]{3,2,1,0:T(8,128)(2,1)} %x_ref.1, bf16[320,1281]{1,0:T(8,128)(2,1)} %bitcast.5), custom_call_target="tpu_custom_call" | custom-call | flops 419758080 | bytes 1639680 | tf_op jit(solution)/shard_map/pack/pallas_call | solution.py:219
  8.1 1.9 %collective-permute-start.1 = (bf16[320,1281]{1,0:T(8,128)(2,1)}, bf16[320,1281]{1,0:T(8,128)(2,1)S(1)}, u32[]{:S(2)}, u32[]{:S(2)}) collective-permute-start(bf16[320,1281]{1,0:T(8,128)(2,1)} %get-tuple-element.22.refs_0_), channel_id=1, source_target_pairs={{0,6},{1,3},{2,0},{3,5},{4,2},{5,7},{6,4},{7,1},{8,14},{9,11},{10,... | collective-permute-start | bytes 2459528 | tf_op jit(solution)/shard_map/ppermute | solution.py:286
  10.0 0.0 copy-start
  10.0 16.5 %all-to-all-start = ((bf16[64,2,640]{2,1,0:T(2,128)(2,1)}), bf16[64,2,640]{2,1,0:T(2,128)(2,1)S(1)}, u32[]{:S(2)}, u32[]{:S(2)}) async-start(bf16[64,2,640]{2,1,0:T(2,128)(2,1)} %get-tuple-element.20.token_ref), calls=%async_computation | async-start | bytes 327680 | tf_op jit(solution)/shard_map/all_to_all | solution.py:299
  26.5 0.0 collective-permute-done.tab_ref
  26.5 0.0 copy-done
  26.5 0.0 copy-start.4
  26.5 4.6 %collective-permute-start.5 = (bf16[320,1281]{1,0:T(8,128)(2,1)S(1)}, bf16[320,1281]{1,0:T(8,128)(2,1)S(1)}, u32[]{:S(2)}, u32[]{:S(2)}) collective-permute-start(bf16[320,1281]{1,0:T(8,128)(2,1)S(1)} %pass_on.3.refs_1_), channel_id=1, source_target_pairs={{0,2},{1,7},{2,4},{3,1},{4,6},{5,3},{6,0},{7,5},{8,10},{9,15},{10,... | collective-permute-start | bytes 2459528 | tf_op jit(solution)/shard_map/ppermute | solution.py:286
  31.8 0.0 copy-start.1
  31.8 0.0 copy-start.2
  31.8 0.6 copy-done.1
  32.5 0.0 copy-done.2
  32.5 0.8 coef.1
  33.2 5.0 %all-to-all-done.y_ref = bf16[64,2,640]{2,1,0:T(2,128)(2,1)S(1)} async-done(((bf16[64,2,640]{2,1,0:T(2,128)(2,1)}), bf16[64,2,640]{2,1,0:T(2,128)(2,1)S(1)}, u32[]{:S(2)}, u32[]{:S(2)}) %all-to-all-start) | async-done | bytes 163872 | tf_op jit(solution)/shard_map/all_to_all | solution.py:299
  38.3 0.4 weigh.1.w_ref
  38.7 0.0 collective-permute-done.1.tab_ref
  38.8 1.1 %copy-done.3 = bf16[320,1281]{1,0:T(8,128)(2,1)S(1)} copy-done((bf16[320,1281]{1,0:T(8,128)(2,1)S(1)}, bf16[320,1281]{1,0:T(8,128)(2,1)}, u32[]{:S(2)}) %copy-start.3) | copy-done | bytes 819864
  39.9 1.7 %near.1 = (f32[32,1281]{1,0:T(8,128)S(1)}, bf16[1281,320]{1,0:T(8,128)(2,1)S(1)}, bf16[1281,320]{1,0:T(8,128)(2,1)S(1)}, bf16[1281,320]{1,0:T(8,128)(2,1)S(1)}, bf16[320,1281]{1,0:T(8,128)(2,1)S(1)}) custom-call(s32[1]{0:T(128)} %bitcast.lev_ref, bf16[8,32,320]{2,1,0:T(8,128)(2,1)S(1)} %weigh.1.w_ref, bf16[320,1281]{1,0:T(8,128)(2,1)S(1)} %copy-done.3, ...), custom_call_target="tpu_custom_call" | custom-call | flops 7299999744 | tf_op jit(solution)/shard_map/near/pallas_call | solution.py:262
  41.6 4.8 %collective-permute-start.2 = (bf16[320,1281]{1,0:T(8,128)(2,1)S(1)}, bf16[320,1281]{1,0:T(8,128)(2,1)S(1)}, u32[]{:S(2)}, u32[]{:S(2)}) collective-permute-start(bf16[320,1281]{1,0:T(8,128)(2,1)S(1)} %get-tuple-element.24), channel_id=1, source_target_pairs={{0,1},{1,0},{2,3},{3,2},{4,5},{5,4},{6,7},{7,6},{8,9},{9,8},{10,11... | collective-permute-start | bytes 2459528 | tf_op jit(solution)/shard_map/ppermute | solution.py:290
  46.4 1.9 %collective-permute-start.3 = (bf16[320,1281]{1,0:T(8,128)(2,1)S(1)}, bf16[320,1281]{1,0:T(8,128)(2,1)S(1)}, u32[]{:S(2)}, u32[]{:S(2)}) collective-permute-start(bf16[320,1281]{1,0:T(8,128)(2,1)S(1)} %pass_on.3.refs_1_), channel_id=1, source_target_pairs={{0,1},{1,0},{2,3},{3,2},{4,5},{5,4},{6,7},{7,6},{8,9},{9,8},{10,11... | collective-permute-start | bytes 2459528 | tf_op jit(solution)/shard_map/ppermute | solution.py:290
  48.4 2.4 %collective-permute-start.4 = (bf16[320,1281]{1,0:T(8,128)(2,1)S(1)}, bf16[320,1281]{1,0:T(8,128)(2,1)S(1)}, u32[]{:S(2)}, u32[]{:S(2)}) collective-permute-start(bf16[320,1281]{1,0:T(8,128)(2,1)S(1)} %pass_on.4.refs_2_), channel_id=1, source_target_pairs={{0,1},{1,0},{2,3},{3,2},{4,5},{5,4},{6,7},{7,6},{8,9},{9,8},{10,11... | collective-permute-start | bytes 2459528 | tf_op jit(solution)/shard_map/ppermute | solution.py:290
  50.8 0.0 collective-permute-done.5.tab_ref
  50.8 1.9 %collective-permute-start.6 = (bf16[320,1281]{1,0:T(8,128)(2,1)S(1)}, bf16[320,1281]{1,0:T(8,128)(2,1)S(1)}, u32[]{:S(2)}, u32[]{:S(2)}) collective-permute-start(bf16[320,1281]{1,0:T(8,128)(2,1)S(1)} %pass_on.5.refs_3_), channel_id=1, source_target_pairs={{0,1},{1,0},{2,3},{3,2},{4,5},{5,4},{6,7},{7,6},{8,9},{9,8},{10,11... | collective-permute-start | bytes 2459528 | tf_op jit(solution)/shard_map/ppermute | solution.py:290
  52.7 0.0 collective-permute-done.2.refs_0_
  52.7 0.0 collective-permute-done.3.refs_1_
  52.7 0.1 collective-permute-done.4.refs_2_
  52.8 1.2 %far.1 = (f32[32,1281]{1,0:T(8,128)S(1)}, bf16[1281,320]{1,0:T(8,128)(2,1)S(1)}, bf16[1281,320]{1,0:T(8,128)(2,1)S(1)}, bf16[1281,320]{1,0:T(8,128)(2,1)S(1)}, bf16[1281,320]{1,0:T(8,128)(2,1)S(1)}) custom-call(s32[1]{0:T(128)} %bitcast.lev_ref, bf16[8,32,320]{2,1,0:T(8,128)(2,1)S(1)} %weigh.1.w_ref, f32[32,1281]{1,0:T(8,128)S(1)} %get-tuple-element.23.token_ref.raw_ref, ...), custom_call_target="tpu_custom_call" | custom-call | flops 839516160 | bytes 3279360 | tf_op jit(solution)/shard_map/far/pallas_call | solution.py:271
  54.1 1.1 %collective-permute-done.6.refs_7_ = bf16[320,1281]{1,0:T(8,128)(2,1)S(1)} collective-permute-done((bf16[320,1281]{1,0:T(8,128)(2,1)S(1)}, bf16[320,1281]{1,0:T(8,128)(2,1)S(1)}, u32[]{:S(2)}, u32[]{:S(2)}) %collective-permute-start.6) | collective-permute-done | bytes 819872 | tf_op jit(solution)/shard_map/ppermute | solution.py:290
  55.1 3.6 %solve.1 = bf16[64,2,640]{2,1,0:T(2,128)(2,1)S(1)} custom-call(s32[1]{0:T(128)S(6)} %copy.13.low_ref, s32[1]{0:T(128)} %bitcast.lev_ref, f32[2,8,128]{2,1,0:T(8,128)S(1)} %get-tuple-element.19.level_ref, bf16[8,32,320]{2,1,0:T(8,128)(2,1)S(1)} %weigh.1.w_ref, f32[8,2,320]{2,1,0:T(2,128)S(1)} %get-tuple-element.21.scale_ref, ...), custom_call_target="tpu_custom_call" | custom-call | flops 1888911360 | bytes 7378560 | tf_op jit(solution)/shard_map/solve/pallas_call | solution.py:278
  58.7 17.4 %all_to_all.10.b_ref = bf16[64,2,640]{2,1,0:T(2,128)(2,1)S(1)} all-to-all(bf16[64,2,640]{2,1,0:T(2,128)(2,1)S(1)} %solve.1), channel_id=1, replica_groups=mesh['wave'=64,'lev'=8] {'wave'}, dimensions={0} | all-to-all | bytes 327680 | tf_op jit(solution)/shard_map/all_to_all | solution.py:312
  76.1 1.3 %unpack.1 = bf16[2,4,40,256]{3,2,1,0:T(8,128)(2,1)} custom-call(bf16[64,2,640]{2,1,0:T(2,128)(2,1)S(1)} %all_to_all.10.b_ref), custom_call_target="tpu_custom_call" | custom-call | flops 419758080 | bytes 1311744 | tf_op jit(solution)/shard_map/unpack/pallas_call | solution.py:226
  (6 shorter events, 0.0 us)
Async XLA Ops:
  0.0 26.5 %collective-permute-start = (bf16[320,1281]{1,0:T(8,128)(2,1)}, bf16[320,1281]{1,0:T(8,128)(2,1)S(1)}, u32[]{:S(2)}, u32[]{:S(2)}) collective-permute-start(bf16[320,1281]{1,0:T(8,128)(2,1)} %bitcast.4), channel_id=1, source_target_pairs={{0,2},{1,7},{2,4},{3,1},{4,6},{5,3},{6,0},{7,5},{8,10},{9,15},{10,... | collective-permute-start | bytes 2459528 | tf_op jit(solution)/shard_map/ppermute | solution.py:286
  8.1 30.6 %collective-permute-start.1 = (bf16[320,1281]{1,0:T(8,128)(2,1)}, bf16[320,1281]{1,0:T(8,128)(2,1)S(1)}, u32[]{:S(2)}, u32[]{:S(2)}) collective-permute-start(bf16[320,1281]{1,0:T(8,128)(2,1)} %get-tuple-element.22.refs_0_), channel_id=1, source_target_pairs={{0,6},{1,3},{2,0},{3,5},{4,2},{5,7},{6,4},{7,1},{8,14},{9,11},{10,... | collective-permute-start | bytes 2459528 | tf_op jit(solution)/shard_map/ppermute | solution.py:286
  10.0 16.5 %copy-start = (bf16[64,2,640]{2,1,0:T(2,128)(2,1)S(1)}, bf16[64,2,640]{2,1,0:T(2,128)(2,1)}, u32[]{:S(2)}) copy-start(bf16[64,2,640]{2,1,0:T(2,128)(2,1)} %get-tuple-element.20.token_ref) | copy-start | bytes 491524
  10.0 28.2 %all-to-all-start = ((bf16[64,2,640]{2,1,0:T(2,128)(2,1)}), bf16[64,2,640]{2,1,0:T(2,128)(2,1)S(1)}, u32[]{:S(2)}, u32[]{:S(2)}) async-start(bf16[64,2,640]{2,1,0:T(2,128)(2,1)} %get-tuple-element.20.token_ref), calls=%async_computation | async-start | bytes 327680 | tf_op jit(solution)/shard_map/all_to_all | solution.py:299
  26.5 5.3 %copy-start.4 = (s32[2560]{0:T(1024)S(1)}, s32[2560]{0:T(1024)}, u32[]{:S(2)}) copy-start(s32[2560]{0:T(1024)} %param.8) | copy-start | bytes 30724
  26.5 24.2 %collective-permute-start.5 = (bf16[320,1281]{1,0:T(8,128)(2,1)S(1)}, bf16[320,1281]{1,0:T(8,128)(2,1)S(1)}, u32[]{:S(2)}, u32[]{:S(2)}) collective-permute-start(bf16[320,1281]{1,0:T(8,128)(2,1)S(1)} %pass_on.3.refs_1_), channel_id=1, source_target_pairs={{0,2},{1,7},{2,4},{3,1},{4,6},{5,3},{6,0},{7,5},{8,10},{9,15},{10,... | collective-permute-start | bytes 2459528 | tf_op jit(solution)/shard_map/ppermute | solution.py:286
  31.8 0.7 copy-start.1
  31.8 0.7 copy-start.2
  38.7 1.2 %copy-start.3 = (bf16[320,1281]{1,0:T(8,128)(2,1)S(1)}, bf16[320,1281]{1,0:T(8,128)(2,1)}, u32[]{:S(2)}) copy-start(bf16[320,1281]{1,0:T(8,128)(2,1)} %get-tuple-element.22.refs_0_) | copy-start | bytes 2459524
  41.6 11.1 %collective-permute-start.2 = (bf16[320,1281]{1,0:T(8,128)(2,1)S(1)}, bf16[320,1281]{1,0:T(8,128)(2,1)S(1)}, u32[]{:S(2)}, u32[]{:S(2)}) collective-permute-start(bf16[320,1281]{1,0:T(8,128)(2,1)S(1)} %get-tuple-element.24), channel_id=1, source_target_pairs={{0,1},{1,0},{2,3},{3,2},{4,5},{5,4},{6,7},{7,6},{8,9},{9,8},{10,11... | collective-permute-start | bytes 2459528 | tf_op jit(solution)/shard_map/ppermute | solution.py:290
  46.4 6.3 %collective-permute-start.3 = (bf16[320,1281]{1,0:T(8,128)(2,1)S(1)}, bf16[320,1281]{1,0:T(8,128)(2,1)S(1)}, u32[]{:S(2)}, u32[]{:S(2)}) collective-permute-start(bf16[320,1281]{1,0:T(8,128)(2,1)S(1)} %pass_on.3.refs_1_), channel_id=1, source_target_pairs={{0,1},{1,0},{2,3},{3,2},{4,5},{5,4},{6,7},{7,6},{8,9},{9,8},{10,11... | collective-permute-start | bytes 2459528 | tf_op jit(solution)/shard_map/ppermute | solution.py:290
  48.4 4.5 %collective-permute-start.4 = (bf16[320,1281]{1,0:T(8,128)(2,1)S(1)}, bf16[320,1281]{1,0:T(8,128)(2,1)S(1)}, u32[]{:S(2)}, u32[]{:S(2)}) collective-permute-start(bf16[320,1281]{1,0:T(8,128)(2,1)S(1)} %pass_on.4.refs_2_), channel_id=1, source_target_pairs={{0,1},{1,0},{2,3},{3,2},{4,5},{5,4},{6,7},{7,6},{8,9},{9,8},{10,11... | collective-permute-start | bytes 2459528 | tf_op jit(solution)/shard_map/ppermute | solution.py:290
  50.8 4.3 %collective-permute-start.6 = (bf16[320,1281]{1,0:T(8,128)(2,1)S(1)}, bf16[320,1281]{1,0:T(8,128)(2,1)S(1)}, u32[]{:S(2)}, u32[]{:S(2)}) collective-permute-start(bf16[320,1281]{1,0:T(8,128)(2,1)S(1)} %pass_on.5.refs_3_), channel_id=1, source_target_pairs={{0,1},{1,0},{2,3},{3,2},{4,5},{5,4},{6,7},{7,6},{8,9},{9,8},{10,11... | collective-permute-start | bytes 2459528 | tf_op jit(solution)/shard_map/ppermute | solution.py:290

commit v5 on v4

--- a/solution.py
+++ b/solution.py
@@ -95,11 +95,17 @@
     return ones_where((gap >= 0) & (gap < 4))
 
 
+def place_rows():
+    lane = iota((1, 512), 1)
+    row = (lane & 7) * R + 4 * ((lane >> 3) & 15) + (lane >> 7)
+    return ones_where((iota((SLAB, 512), 0) == row) & (((lane >> 3) & 15) < STEPS))
+
+
 def own_group():
     return (iota((4 * COLS, SLAB), 0) >> 5) == (iota((4 * COLS, SLAB), 1) & 3)
 
 
-def coef_kernel(low_ref, lev_ref, gamma_ref, beta_ref, points_ref, scale_ref, level_ref):
+def coef_kernel(low_ref, lev_ref, gamma_ref, beta_ref, points_ref, token_ref, scale_ref, level_ref):
     low = low_ref[0]
     points = jnp.concatenate([points_ref[:, s * SLAB:(s + 1) * SLAB] for s in range(SLABS)], axis=0)
     pts = points.astype(jnp.float32)
@@ -189,13 +195,14 @@
     solved = (drive - bval * eig * mass) / (1.0 + gval * eig)
     spec = jnp.concatenate([solved, mass + bval * solved], axis=0)
     expanded = jnp.concatenate([jnp.where(first, spec, 0.0), jnp.where(first, 0.0, spec)], axis=0).astype(jnp.bfloat16)
-    spread = spread_rows()
-    group = own_group()
+    rows = []
     for n, slab in enumerate(slabs):
-        rows = mul(expanded, tabs[n][...], NN if n < NEARS + FARS else NT)
-        rows = jnp.where(members(scale_ref[slab]) > 0.0, rows, 0.0)
-        rows = jnp.where(group, jnp.concatenate([rows] * 4, axis=0), 0.0).astype(jnp.bfloat16)
-        block = mul(spread, rows, NT)
+        part = mul(expanded, tabs[n][...], NN if n < NEARS + FARS else NT)
+        rows.append(jnp.where(members(scale_ref[slab]) > 0.0, part, 0.0).astype(jnp.bfloat16))
+    placed = mul(jnp.concatenate(rows, axis=0), place_rows(), NN)
+    for n, slab in enumerate(slabs):
+        part = placed[n * COLS:(n + 1) * COLS]
+        block = jnp.concatenate([part[:, g * 128:(g + 1) * 128] for g in range(4)], axis=0).T
         place = pl.ds(pl.multiple_of(slab * SLABS, SLABS), SLABS)
         for j in range(STEPS):
             out_ref[j // 5, place, (j % 5) * 128:(j % 5 + 1) * 128] = block[j * SLABS:(j + 1) * SLABS]
@@ -228,12 +235,12 @@
                           name="unpack")(b)
 
 
-def coef(low, lev, gamma, beta, points):
+def coef(low, lev, gamma, beta, points, token):
     return pl.pallas_call(
         coef_kernel, out_shape=(jax.ShapeDtypeStruct((SLABS, 2, SLAB), jnp.float32),
                                 jax.ShapeDtypeStruct((2, SLABS, 128), jnp.float32)),
-        in_specs=[SMEM] * 4 + [VMEM], out_specs=(VMEM,) * 2, compiler_params=params(8),
-        name="coef")(low, lev, gamma, beta, points)
+        in_specs=[SMEM] * 4 + [VMEM, ANY], out_specs=(VMEM,) * 2, compiler_params=params(8),
+        name="coef")(low, lev, gamma, beta, points, token)
 
 
 def like(tab):
@@ -294,14 +301,14 @@
     lev = lax.axis_index("lev").astype(jnp.int32).reshape(1)
     own = jnp.swapaxes(table, 1, 2)[0]
     first = along_x(own, 1)
-    sent, own = pack(fourier_in, own)
-    second = along_x(own, -1)
+    sent, copied = pack(fourier_in, own)
+    second = along_x(copied, -1)
     moved = lax.all_to_all(sent, "wave", split_axis=0, concat_axis=0, tiled=True)
-    first = pass_on(sent, first)
+    scale, level = coef(pair_low, lev, gamma, beta, points.reshape(1, NLAT), sent)
+    first = pass_on(level, first)
     third = along_x(first, 1)
     second = pass_on(sent, second)
     cores = [other_core(first), other_core(second)]
-    scale, level = coef(pair_low, lev, gamma, beta, points.reshape(1, NLAT))
     weighted = weigh(moved, scale)
     raw, *tabs, own = near(lev, weighted, [own, first, second])
     third = pass_on(raw, third)

time: 78.1 us -> 78.8 us (level)
  blocking collectives: 17.4 us -> 19.5 us
  Pallas kernels: 11.9 us -> 10.6 us
    all_to_all x1, blocking collectives: 17.4 us -> 19.5 us  [local(): lax.all_to_all(result, 'wave', split_axis=0, concat_axis=0, tiled=True)]
    pallas_call x1, Pallas kernels: 3.59 us -> 2.24 us  [solve(): pl.pallas_call(solve_kernel, out_shape=chunks(), in_specs=[SMEM] * 2 + [V...]
where the time goes in v5:
time: 78.8 us; the launch traced here: 78.2 us
  starting transfers between devices  39.2 us (50%)
  blocking collectives  19.5 us (25%)
  Pallas kernels  10.6 us (13%)
  waiting for transfers between devices  6.23 us (8%)
  local copies, waits for them, and re-layouts  1.82 us (2%)
  between operations  0.89 us (1%)
    all_to_all x1, blocking collectives, local(): lax.all_to_all(result, 'wave', split_axis=0, concat_axis=0, tiled=True)  19.5 us
    all_to_all x1, starting transfers between devices, local(): lax.all_to_all(sent, 'wave', split_axis=0, concat_axis=0, tiled=True)  16.4 us
    ppermute x3, starting transfers between devices, along_x(): lax.ppermute(array, 'lev', [(d, (d + 2 * step * (1 - 2 * (d % 2))) % SLAB...  11.7 us
    ppermute x4, starting transfers between devices, other_core(): return lax.ppermute(array, 'lev', [(d, d ^ 1) for d in range(SLABS)])  11.1 us
    all_to_all x1, waiting for transfers between devices, local(): lax.all_to_all(sent, 'wave', split_axis=0, concat_axis=0, tiled=True)  5.06 us
    pallas_call x1, Pallas kernels, pack(): pl.pallas_call(pack_kernel, out_shape=(chunks(), like(tab)), in_specs=[AN...  2.88 us
    pallas_call x1, Pallas kernels, solve(): pl.pallas_call(solve_kernel, out_shape=chunks(), in_specs=[SMEM] * 2 + [V...  2.24 us
    unnamed x10, local copies, waits for them, and re-layouts  1.81 us
  transfers between devices with their start and end apart: 8, of which 3 were waited for; matrix products, arithmetic and copies ran while one was open for 0% of the time, Pallas kernels for 9%

profile of v5, /device:TPU:1, one launch (start us, length us, event | category | flops | bytes accessed | tf_op | source)
XLA Modules:
  0.0 78.2 jit_solution(2344611655259066724)
XLA Ops:
  0.0 5.2 %collective-permute-start = (bf16[320,1281]{1,0:T(8,128)(2,1)}, bf16[320,1281]{1,0:T(8,128)(2,1)S(1)}, u32[]{:S(2)}, u32[]{:S(2)}) collective-permute-start(bf16[320,1281]{1,0:T(8,128)(2,1)} %bitcast.4), channel_id=1, source_target_pairs={{0,2},{1,7},{2,4},{3,1},{4,6},{5,3},{6,0},{7,5},{8,10},{9,15},{10,... | collective-permute-start | bytes 2459528 | tf_op jit(solution)/shard_map/ppermute | solution.py:293
  5.2 2.9 %pack.1 = (bf16[64,2,640]{2,1,0:T(2,128)(2,1)}, bf16[320,1281]{1,0:T(8,128)(2,1)}) custom-call(bf16[2,4,40,256]{3,2,1,0:T(8,128)(2,1)} %x_ref.1, bf16[320,1281]{1,0:T(8,128)(2,1)} %bitcast.5), custom_call_target="tpu_custom_call" | custom-call | flops 419758080 | bytes 1639680 | tf_op jit(solution)/shard_map/pack/pallas_call | solution.py:226
  8.1 1.9 %collective-permute-start.1 = (bf16[320,1281]{1,0:T(8,128)(2,1)}, bf16[320,1281]{1,0:T(8,128)(2,1)S(1)}, u32[]{:S(2)}, u32[]{:S(2)}) collective-permute-start(bf16[320,1281]{1,0:T(8,128)(2,1)} %get-tuple-element.22), channel_id=1, source_target_pairs={{0,6},{1,3},{2,0},{3,5},{4,2},{5,7},{6,4},{7,1},{8,14},{9,11},{10,... | collective-permute-start | bytes 2459528 | tf_op jit(solution)/shard_map/ppermute | solution.py:293
  10.0 0.0 copy-start.4
  10.0 0.0 copy-start
  10.1 16.4 %all-to-all-start = ((bf16[64,2,640]{2,1,0:T(2,128)(2,1)}), bf16[64,2,640]{2,1,0:T(2,128)(2,1)S(1)}, u32[]{:S(2)}, u32[]{:S(2)}) async-start(bf16[64,2,640]{2,1,0:T(2,128)(2,1)} %get-tuple-element.19.token_ref), calls=%async_computation | async-start | bytes 327680 | tf_op jit(solution)/shard_map/all_to_all | solution.py:306
  27.2 0.0 copy-start.1
  27.2 0.0 copy-start.2
  27.2 0.6 copy-done.1
  27.8 0.0 copy-done.2
  27.9 0.8 coef.1
  28.6 0.0 collective-permute-done.tab_ref
  28.6 4.6 %collective-permute-start.5 = (bf16[320,1281]{1,0:T(8,128)(2,1)S(1)}, bf16[320,1281]{1,0:T(8,128)(2,1)S(1)}, u32[]{:S(2)}, u32[]{:S(2)}) collective-permute-start(bf16[320,1281]{1,0:T(8,128)(2,1)S(1)} %pass_on.3.refs_1_), channel_id=1, source_target_pairs={{0,2},{1,7},{2,4},{3,1},{4,6},{5,3},{6,0},{7,5},{8,10},{9,15},{10,... | collective-permute-start | bytes 2459528 | tf_op jit(solution)/shard_map/ppermute | solution.py:293
  33.2 5.1 %all-to-all-done.y_ref = bf16[64,2,640]{2,1,0:T(2,128)(2,1)S(1)} async-done(((bf16[64,2,640]{2,1,0:T(2,128)(2,1)}), bf16[64,2,640]{2,1,0:T(2,128)(2,1)S(1)}, u32[]{:S(2)}, u32[]{:S(2)}) %all-to-all-start) | async-done | bytes 163872 | tf_op jit(solution)/shard_map/all_to_all | solution.py:306
  38.3 0.4 weigh.1.w_ref
  38.7 0.0 copy-start.3
  38.7 0.0 collective-permute-done.1.tab_ref
  38.8 1.1 %copy-done.3 = bf16[1,1281,320]{1,2,0:T(8,128)(2,1)S(1)} copy-done((bf16[1,1281,320]{1,2,0:T(8,128)(2,1)S(1)}, bf16[1,1281,320]{1,2,0:T(8,128)(2,1)}, u32[]{:S(2)}) %copy-start.3) | copy-done | bytes 819864
  39.9 1.7 %near.1 = (f32[32,1281]{1,0:T(8,128)S(1)}, bf16[1281,320]{1,0:T(8,128)(2,1)S(1)}, bf16[1281,320]{1,0:T(8,128)(2,1)S(1)}, bf16[1281,320]{1,0:T(8,128)(2,1)S(1)}, bf16[320,1281]{1,0:T(8,128)(2,1)S(1)}) custom-call(s32[1]{0:T(128)} %bitcast.lev_ref, bf16[8,32,320]{2,1,0:T(8,128)(2,1)S(1)} %weigh.1.w_ref, bf16[320,1281]{1,0:T(8,128)(2,1)S(1)} %bitcast.6, ...), custom_call_target="tpu_custom_call" | custom-call | flops 7299999744 | tf_op jit(solution)/shard_map/near/pallas_call | solution.py:269
  41.6 4.8 %collective-permute-start.2 = (bf16[320,1281]{1,0:T(8,128)(2,1)S(1)}, bf16[320,1281]{1,0:T(8,128)(2,1)S(1)}, u32[]{:S(2)}, u32[]{:S(2)}) collective-permute-start(bf16[320,1281]{1,0:T(8,128)(2,1)S(1)} %get-tuple-element.24), channel_id=1, source_target_pairs={{0,1},{1,0},{2,3},{3,2},{4,5},{5,4},{6,7},{7,6},{8,9},{9,8},{10,11... | collective-permute-start | bytes 2459528 | tf_op jit(solution)/shard_map/ppermute | solution.py:297
  46.4 1.9 %collective-permute-start.3 = (bf16[320,1281]{1,0:T(8,128)(2,1)S(1)}, bf16[320,1281]{1,0:T(8,128)(2,1)S(1)}, u32[]{:S(2)}, u32[]{:S(2)}) collective-permute-start(bf16[320,1281]{1,0:T(8,128)(2,1)S(1)} %pass_on.3.refs_1_), channel_id=1, source_target_pairs={{0,1},{1,0},{2,3},{3,2},{4,5},{5,4},{6,7},{7,6},{8,9},{9,8},{10,11... | collective-permute-start | bytes 2459528 | tf_op jit(solution)/shard_map/ppermute | solution.py:297
  48.4 2.4 %collective-permute-start.4 = (bf16[320,1281]{1,0:T(8,128)(2,1)S(1)}, bf16[320,1281]{1,0:T(8,128)(2,1)S(1)}, u32[]{:S(2)}, u32[]{:S(2)}) collective-permute-start(bf16[320,1281]{1,0:T(8,128)(2,1)S(1)} %pass_on.4.refs_2_), channel_id=1, source_target_pairs={{0,1},{1,0},{2,3},{3,2},{4,5},{5,4},{6,7},{7,6},{8,9},{9,8},{10,11... | collective-permute-start | bytes 2459528 | tf_op jit(solution)/shard_map/ppermute | solution.py:297
  50.8 0.0 collective-permute-done.5.tab_ref
  50.8 1.9 %collective-permute-start.6 = (bf16[320,1281]{1,0:T(8,128)(2,1)S(1)}, bf16[320,1281]{1,0:T(8,128)(2,1)S(1)}, u32[]{:S(2)}, u32[]{:S(2)}) collective-permute-start(bf16[320,1281]{1,0:T(8,128)(2,1)S(1)} %pass_on.5.refs_3_), channel_id=1, source_target_pairs={{0,1},{1,0},{2,3},{3,2},{4,5},{5,4},{6,7},{7,6},{8,9},{9,8},{10,11... | collective-permute-start | bytes 2459528 | tf_op jit(solution)/shard_map/ppermute | solution.py:297
  52.7 0.0 collective-permute-done.2.refs_0_
  52.7 0.0 collective-permute-done.3.refs_1_
  52.8 0.1 collective-permute-done.4.refs_2_
  52.8 1.2 %far.1 = (f32[32,1281]{1,0:T(8,128)S(1)}, bf16[1281,320]{1,0:T(8,128)(2,1)S(1)}, bf16[1281,320]{1,0:T(8,128)(2,1)S(1)}, bf16[1281,320]{1,0:T(8,128)(2,1)S(1)}, bf16[1281,320]{1,0:T(8,128)(2,1)S(1)}) custom-call(s32[1]{0:T(128)} %bitcast.lev_ref, bf16[8,32,320]{2,1,0:T(8,128)(2,1)S(1)} %weigh.1.w_ref, f32[32,1281]{1,0:T(8,128)S(1)} %get-tuple-element.23.token_ref.raw_ref, ...), custom_call_target="tpu_custom_call" | custom-call | flops 839516160 | bytes 3279360 | tf_op jit(solution)/shard_map/far/pallas_call | solution.py:278
  54.1 1.1 %collective-permute-done.6.refs_7_ = bf16[320,1281]{1,0:T(8,128)(2,1)S(1)} collective-permute-done((bf16[320,1281]{1,0:T(8,128)(2,1)S(1)}, bf16[320,1281]{1,0:T(8,128)(2,1)S(1)}, u32[]{:S(2)}, u32[]{:S(2)}) %collective-permute-start.6) | collective-permute-done | bytes 819872 | tf_op jit(solution)/shard_map/ppermute | solution.py:297
  55.2 2.2 %solve.1 = bf16[64,2,640]{2,1,0:T(2,128)(2,1)S(1)} custom-call(s32[1]{0:T(128)S(6)} %copy.13.low_ref, s32[1]{0:T(128)} %bitcast.lev_ref, f32[2,8,128]{2,1,0:T(8,128)S(1)} %get-tuple-element.20.token_ref.level_ref, bf16[8,32,320]{2,1,0:T(8,128)(2,1)S(1)} %weigh.1.w_ref, f32[8,2,320]{2,1,0:T(2,128)S(1)} %get-tuple-element.21.scale_ref, ...), custom_call_target="tpu_custom_call" | custom-call | flops 1888911360 | bytes 7378560 | tf_op jit(solution)/shard_map/solve/pallas_call | solution.py:285
  57.4 19.5 %all_to_all.10.b_ref = bf16[64,2,640]{2,1,0:T(2,128)(2,1)S(1)} all-to-all(bf16[64,2,640]{2,1,0:T(2,128)(2,1)S(1)} %solve.1), channel_id=1, replica_groups=mesh['wave'=64,'lev'=8] {'wave'}, dimensions={0} | all-to-all | bytes 327680 | tf_op jit(solution)/shard_map/all_to_all | solution.py:319
  76.9 1.3 %unpack.1 = bf16[2,4,40,256]{3,2,1,0:T(8,128)(2,1)} custom-call(bf16[64,2,640]{2,1,0:T(2,128)(2,1)S(1)} %all_to_all.10.b_ref), custom_call_target="tpu_custom_call" | custom-call | flops 419758080 | bytes 1311744 | tf_op jit(solution)/shard_map/unpack/pallas_call | solution.py:233
  (6 shorter events, 0.0 us)
Async XLA Ops:
  0.0 28.6 %collective-permute-start = (bf16[320,1281]{1,0:T(8,128)(2,1)}, bf16[320,1281]{1,0:T(8,128)(2,1)S(1)}, u32[]{:S(2)}, u32[]{:S(2)}) collective-permute-start(bf16[320,1281]{1,0:T(8,128)(2,1)} %bitcast.4), channel_id=1, source_target_pairs={{0,2},{1,7},{2,4},{3,1},{4,6},{5,3},{6,0},{7,5},{8,10},{9,15},{10,... | collective-permute-start | bytes 2459528 | tf_op jit(solution)/shard_map/ppermute | solution.py:293
  8.1 30.6 %collective-permute-start.1 = (bf16[320,1281]{1,0:T(8,128)(2,1)}, bf16[320,1281]{1,0:T(8,128)(2,1)S(1)}, u32[]{:S(2)}, u32[]{:S(2)}) collective-permute-start(bf16[320,1281]{1,0:T(8,128)(2,1)} %get-tuple-element.22), channel_id=1, source_target_pairs={{0,6},{1,3},{2,0},{3,5},{4,2},{5,7},{6,4},{7,1},{8,14},{9,11},{10,... | collective-permute-start | bytes 2459528 | tf_op jit(solution)/shard_map/ppermute | solution.py:293
  10.0 17.1 %copy-start.4 = (s32[2560]{0:T(1024)S(1)}, s32[2560]{0:T(1024)}, u32[]{:S(2)}) copy-start(s32[2560]{0:T(1024)} %param.8) | copy-start | bytes 30724
  10.0 17.2 %copy-start = (bf16[64,2,640]{2,1,0:T(2,128)(2,1)S(1)}, bf16[64,2,640]{2,1,0:T(2,128)(2,1)}, u32[]{:S(2)}) copy-start(bf16[64,2,640]{2,1,0:T(2,128)(2,1)} %get-tuple-element.19.token_ref) | copy-start | bytes 491524
  10.1 28.2 %all-to-all-start = ((bf16[64,2,640]{2,1,0:T(2,128)(2,1)}), bf16[64,2,640]{2,1,0:T(2,128)(2,1)S(1)}, u32[]{:S(2)}, u32[]{:S(2)}) async-start(bf16[64,2,640]{2,1,0:T(2,128)(2,1)} %get-tuple-element.19.token_ref), calls=%async_computation | async-start | bytes 327680 | tf_op jit(solution)/shard_map/all_to_all | solution.py:306
  27.2 0.7 copy-start.1
  27.2 0.7 copy-start.2
  28.6 22.2 %collective-permute-start.5 = (bf16[320,1281]{1,0:T(8,128)(2,1)S(1)}, bf16[320,1281]{1,0:T(8,128)(2,1)S(1)}, u32[]{:S(2)}, u32[]{:S(2)}) collective-permute-start(bf16[320,1281]{1,0:T(8,128)(2,1)S(1)} %pass_on.3.refs_1_), channel_id=1, source_target_pairs={{0,2},{1,7},{2,4},{3,1},{4,6},{5,3},{6,0},{7,5},{8,10},{9,15},{10,... | collective-permute-start | bytes 2459528 | tf_op jit(solution)/shard_map/ppermute | solution.py:293
  38.7 1.2 %copy-start.3 = (bf16[1,1281,320]{1,2,0:T(8,128)(2,1)S(1)}, bf16[1,1281,320]{1,2,0:T(8,128)(2,1)}, u32[]{:S(2)}) copy-start(bf16[1,1281,320]{1,2,0:T(8,128)(2,1)} %param.7) | copy-start | bytes 2459524
  41.6 11.1 %collective-permute-start.2 = (bf16[320,1281]{1,0:T(8,128)(2,1)S(1)}, bf16[320,1281]{1,0:T(8,128)(2,1)S(1)}, u32[]{:S(2)}, u32[]{:S(2)}) collective-permute-start(bf16[320,1281]{1,0:T(8,128)(2,1)S(1)} %get-tuple-element.24), channel_id=1, source_target_pairs={{0,1},{1,0},{2,3},{3,2},{4,5},{5,4},{6,7},{7,6},{8,9},{9,8},{10,11... | collective-permute-start | bytes 2459528 | tf_op jit(solution)/shard_map/ppermute | solution.py:297
  46.4 6.3 %collective-permute-start.3 = (bf16[320,1281]{1,0:T(8,128)(2,1)S(1)}, bf16[320,1281]{1,0:T(8,128)(2,1)S(1)}, u32[]{:S(2)}, u32[]{:S(2)}) collective-permute-start(bf16[320,1281]{1,0:T(8,128)(2,1)S(1)} %pass_on.3.refs_1_), channel_id=1, source_target_pairs={{0,1},{1,0},{2,3},{3,2},{4,5},{5,4},{6,7},{7,6},{8,9},{9,8},{10,11... | collective-permute-start | bytes 2459528 | tf_op jit(solution)/shard_map/ppermute | solution.py:297
  48.4 4.5 %collective-permute-start.4 = (bf16[320,1281]{1,0:T(8,128)(2,1)S(1)}, bf16[320,1281]{1,0:T(8,128)(2,1)S(1)}, u32[]{:S(2)}, u32[]{:S(2)}) collective-permute-start(bf16[320,1281]{1,0:T(8,128)(2,1)S(1)} %pass_on.4.refs_2_), channel_id=1, source_target_pairs={{0,1},{1,0},{2,3},{3,2},{4,5},{5,4},{6,7},{7,6},{8,9},{9,8},{10,11... | collective-permute-start | bytes 2459528 | tf_op jit(solution)/shard_map/ppermute | solution.py:297
  50.8 4.3 %collective-permute-start.6 = (bf16[320,1281]{1,0:T(8,128)(2,1)S(1)}, bf16[320,1281]{1,0:T(8,128)(2,1)S(1)}, u32[]{:S(2)}, u32[]{:S(2)}) collective-permute-start(bf16[320,1281]{1,0:T(8,128)(2,1)S(1)} %pass_on.5.refs_3_), channel_id=1, source_target_pairs={{0,1},{1,0},{2,3},{3,2},{4,5},{5,4},{6,7},{7,6},{8,9},{9,8},{10,11... | collective-permute-start | bytes 2459528 | tf_op jit(solution)/shard_map/ppermute | solution.py:297

commit v6 on v5

--- a/solution.py
+++ b/solution.py
@@ -51,6 +51,13 @@
     source = ((lane >> 3) & 1) * V + ((lane >> 1) & 3)
     source = source * R + 4 * (lane >> 7) + ((lane >> 5) & 3)
     return ones_where(iota((F * V * R, STEPS * 128), 0) == source)
+
+
+def by_place_turned():
+    row = iota((STEPS * 128, 1), 0)
+    source = ((row >> 3) & 1) * V + ((row >> 1) & 3)
+    source = source * R + 4 * (row >> 7) + ((row >> 5) & 3)
+    return ones_where(iota((STEPS * 128, F * V * R), 1) == source)
 
 
 def lane_part(shape):
@@ -81,11 +88,11 @@
 
 def unpack_kernel(b_ref, o_ref):
     b = jnp.swapaxes(b_ref[...].astype(jnp.float32), 0, 1)
-    b = jnp.concatenate([b[0], b[1]], axis=1)
-    part = lane_part((PAIRS, STEPS * 128))
-    parts = [jnp.where(part == q, b, 0.0).astype(jnp.bfloat16) for q in range(4)]
-    turned = mul(by_place(), jnp.concatenate(parts, axis=0), NT).astype(jnp.bfloat16)
-    x = mul(turned, by_member(), NN)
+    b = jnp.concatenate([b[0], b[1]], axis=1).astype(jnp.bfloat16)
+    part = lane_part((1, STEPS * 128))
+    parts = [b * ones_where(part == q) for q in range(4)]
+    turned = mul(jnp.concatenate(parts, axis=0), by_place_turned(), NN).astype(jnp.bfloat16)
+    x = mul(turned, by_member(), TN)
     o_ref[...] = x.reshape(F, V, R, 4 * PAIRS).astype(jnp.bfloat16)
 
 

time: 78.8 us -> 79.2 us (level)
  no operation moved by 1% of the time
where the time goes in v6:
time: 79.2 us; the launch traced here: 78.6 us
  starting transfers between devices  39.2 us (49%)
  blocking collectives  19.5 us (25%)
  Pallas kernels  10.9 us (14%)
  waiting for transfers between devices  6.23 us (8%)
  local copies, waits for them, and re-layouts  1.82 us (2%)
  between operations  0.89 us (1%)
    all_to_all x1, blocking collectives, local(): lax.all_to_all(result, 'wave', split_axis=0, concat_axis=0, tiled=True)  19.5 us
    all_to_all x1, starting transfers between devices, local(): lax.all_to_all(sent, 'wave', split_axis=0, concat_axis=0, tiled=True)  16.4 us
    ppermute x3, starting transfers between devices, along_x(): lax.ppermute(array, 'lev', [(d, (d + 2 * step * (1 - 2 * (d % 2))) % SLAB...  11.7 us
    ppermute x4, starting transfers between devices, other_core(): return lax.ppermute(array, 'lev', [(d, d ^ 1) for d in range(SLABS)])  11.1 us
    all_to_all x1, waiting for transfers between devices, local(): lax.all_to_all(sent, 'wave', split_axis=0, concat_axis=0, tiled=True)  5.06 us
    pallas_call x1, Pallas kernels, pack(): pl.pallas_call(pack_kernel, out_shape=(chunks(), like(tab)), in_specs=[AN...  2.88 us
    pallas_call x1, Pallas kernels, solve(): pl.pallas_call(solve_kernel, out_shape=chunks(), in_specs=[SMEM] * 2 + [V...  2.24 us
    unnamed x10, local copies, waits for them, and re-layouts  1.81 us
  transfers between devices with their start and end apart: 8, of which 3 were waited for; matrix products, arithmetic and copies ran while one was open for 0% of the time, Pallas kernels for 9%

profile of v6, /device:TPU:1, one launch (start us, length us, event | category | flops | bytes accessed | tf_op | source)
XLA Modules:
  0.0 78.6 jit_solution(9839409853652677818)
XLA Ops:
  0.0 5.2 %collective-permute-start = (bf16[320,1281]{1,0:T(8,128)(2,1)}, bf16[320,1281]{1,0:T(8,128)(2,1)S(1)}, u32[]{:S(2)}, u32[]{:S(2)}) collective-permute-start(bf16[320,1281]{1,0:T(8,128)(2,1)} %bitcast.4), channel_id=1, source_target_pairs={{0,2},{1,7},{2,4},{3,1},{4,6},{5,3},{6,0},{7,5},{8,10},{9,15},{10,... | collective-permute-start | bytes 2459528 | tf_op jit(solution)/shard_map/ppermute | solution.py:300
  5.2 2.9 %pack.1 = (bf16[64,2,640]{2,1,0:T(2,128)(2,1)}, bf16[320,1281]{1,0:T(8,128)(2,1)}) custom-call(bf16[2,4,40,256]{3,2,1,0:T(8,128)(2,1)} %x_ref.1, bf16[320,1281]{1,0:T(8,128)(2,1)} %bitcast.5), custom_call_target="tpu_custom_call" | custom-call | flops 419758080 | bytes 1639680 | tf_op jit(solution)/shard_map/pack/pallas_call | solution.py:233
  8.1 1.9 %collective-permute-start.1 = (bf16[320,1281]{1,0:T(8,128)(2,1)}, bf16[320,1281]{1,0:T(8,128)(2,1)S(1)}, u32[]{:S(2)}, u32[]{:S(2)}) collective-permute-start(bf16[320,1281]{1,0:T(8,128)(2,1)} %get-tuple-element.22), channel_id=1, source_target_pairs={{0,6},{1,3},{2,0},{3,5},{4,2},{5,7},{6,4},{7,1},{8,14},{9,11},{10,... | collective-permute-start | bytes 2459528 | tf_op jit(solution)/shard_map/ppermute | solution.py:300
  10.0 0.0 copy-start.4
  10.0 0.0 copy-start
  10.1 16.4 %all-to-all-start = ((bf16[64,2,640]{2,1,0:T(2,128)(2,1)}), bf16[64,2,640]{2,1,0:T(2,128)(2,1)S(1)}, u32[]{:S(2)}, u32[]{:S(2)}) async-start(bf16[64,2,640]{2,1,0:T(2,128)(2,1)} %get-tuple-element.19.token_ref), calls=%async_computation | async-start | bytes 327680 | tf_op jit(solution)/shard_map/all_to_all | solution.py:313
  27.2 0.0 copy-start.1
  27.2 0.0 copy-start.2
  27.2 0.6 copy-done.1
  27.8 0.0 copy-done.2
  27.9 0.8 coef.1
  28.6 0.0 collective-permute-done.tab_ref
  28.6 4.6 %collective-permute-start.5 = (bf16[320,1281]{1,0:T(8,128)(2,1)S(1)}, bf16[320,1281]{1,0:T(8,128)(2,1)S(1)}, u32[]{:S(2)}, u32[]{:S(2)}) collective-permute-start(bf16[320,1281]{1,0:T(8,128)(2,1)S(1)} %pass_on.3.refs_1_), channel_id=1, source_target_pairs={{0,2},{1,7},{2,4},{3,1},{4,6},{5,3},{6,0},{7,5},{8,10},{9,15},{10,... | collective-permute-start | bytes 2459528 | tf_op jit(solution)/shard_map/ppermute | solution.py:300
  33.2 5.1 %all-to-all-done.y_ref = bf16[64,2,640]{2,1,0:T(2,128)(2,1)S(1)} async-done(((bf16[64,2,640]{2,1,0:T(2,128)(2,1)}), bf16[64,2,640]{2,1,0:T(2,128)(2,1)S(1)}, u32[]{:S(2)}, u32[]{:S(2)}) %all-to-all-start) | async-done | bytes 163872 | tf_op jit(solution)/shard_map/all_to_all | solution.py:313
  38.3 0.4 weigh.1.w_ref
  38.7 0.0 copy-start.3
  38.7 0.0 collective-permute-done.1.tab_ref
  38.8 1.1 %copy-done.3 = bf16[1,1281,320]{1,2,0:T(8,128)(2,1)S(1)} copy-done((bf16[1,1281,320]{1,2,0:T(8,128)(2,1)S(1)}, bf16[1,1281,320]{1,2,0:T(8,128)(2,1)}, u32[]{:S(2)}) %copy-start.3) | copy-done | bytes 819864
  39.9 1.7 %near.1 = (f32[32,1281]{1,0:T(8,128)S(1)}, bf16[1281,320]{1,0:T(8,128)(2,1)S(1)}, bf16[1281,320]{1,0:T(8,128)(2,1)S(1)}, bf16[1281,320]{1,0:T(8,128)(2,1)S(1)}, bf16[320,1281]{1,0:T(8,128)(2,1)S(1)}) custom-call(s32[1]{0:T(128)} %bitcast.lev_ref, bf16[8,32,320]{2,1,0:T(8,128)(2,1)S(1)} %weigh.1.w_ref, bf16[320,1281]{1,0:T(8,128)(2,1)S(1)} %bitcast.6, ...), custom_call_target="tpu_custom_call" | custom-call | flops 7299999744 | tf_op jit(solution)/shard_map/near/pallas_call | solution.py:276
  41.6 4.8 %collective-permute-start.2 = (bf16[320,1281]{1,0:T(8,128)(2,1)S(1)}, bf16[320,1281]{1,0:T(8,128)(2,1)S(1)}, u32[]{:S(2)}, u32[]{:S(2)}) collective-permute-start(bf16[320,1281]{1,0:T(8,128)(2,1)S(1)} %get-tuple-element.24), channel_id=1, source_target_pairs={{0,1},{1,0},{2,3},{3,2},{4,5},{5,4},{6,7},{7,6},{8,9},{9,8},{10,11... | collective-permute-start | bytes 2459528 | tf_op jit(solution)/shard_map/ppermute | solution.py:304
  46.4 1.9 %collective-permute-start.3 = (bf16[320,1281]{1,0:T(8,128)(2,1)S(1)}, bf16[320,1281]{1,0:T(8,128)(2,1)S(1)}, u32[]{:S(2)}, u32[]{:S(2)}) collective-permute-start(bf16[320,1281]{1,0:T(8,128)(2,1)S(1)} %pass_on.3.refs_1_), channel_id=1, source_target_pairs={{0,1},{1,0},{2,3},{3,2},{4,5},{5,4},{6,7},{7,6},{8,9},{9,8},{10,11... | collective-permute-start | bytes 2459528 | tf_op jit(solution)/shard_map/ppermute | solution.py:304
  48.4 2.4 %collective-permute-start.4 = (bf16[320,1281]{1,0:T(8,128)(2,1)S(1)}, bf16[320,1281]{1,0:T(8,128)(2,1)S(1)}, u32[]{:S(2)}, u32[]{:S(2)}) collective-permute-start(bf16[320,1281]{1,0:T(8,128)(2,1)S(1)} %pass_on.4.refs_2_), channel_id=1, source_target_pairs={{0,1},{1,0},{2,3},{3,2},{4,5},{5,4},{6,7},{7,6},{8,9},{9,8},{10,11... | collective-permute-start | bytes 2459528 | tf_op jit(solution)/shard_map/ppermute | solution.py:304
  50.8 0.0 collective-permute-done.5.tab_ref
  50.8 1.9 %collective-permute-start.6 = (bf16[320,1281]{1,0:T(8,128)(2,1)S(1)}, bf16[320,1281]{1,0:T(8,128)(2,1)S(1)}, u32[]{:S(2)}, u32[]{:S(2)}) collective-permute-start(bf16[320,1281]{1,0:T(8,128)(2,1)S(1)} %pass_on.5.refs_3_), channel_id=1, source_target_pairs={{0,1},{1,0},{2,3},{3,2},{4,5},{5,4},{6,7},{7,6},{8,9},{9,8},{10,11... | collective-permute-start | bytes 2459528 | tf_op jit(solution)/shard_map/ppermute | solution.py:304
  52.7 0.0 collective-permute-done.2.refs_0_
  52.7 0.0 collective-permute-done.3.refs_1_
  52.8 0.1 collective-permute-done.4.refs_2_
  52.8 1.2 %far.1 = (f32[32,1281]{1,0:T(8,128)S(1)}, bf16[1281,320]{1,0:T(8,128)(2,1)S(1)}, bf16[1281,320]{1,0:T(8,128)(2,1)S(1)}, bf16[1281,320]{1,0:T(8,128)(2,1)S(1)}, bf16[1281,320]{1,0:T(8,128)(2,1)S(1)}) custom-call(s32[1]{0:T(128)} %bitcast.lev_ref, bf16[8,32,320]{2,1,0:T(8,128)(2,1)S(1)} %weigh.1.w_ref, f32[32,1281]{1,0:T(8,128)S(1)} %get-tuple-element.23.token_ref.raw_ref, ...), custom_call_target="tpu_custom_call" | custom-call | flops 839516160 | bytes 3279360 | tf_op jit(solution)/shard_map/far/pallas_call | solution.py:285
  54.1 1.1 %collective-permute-done.6.refs_7_ = bf16[320,1281]{1,0:T(8,128)(2,1)S(1)} collective-permute-done((bf16[320,1281]{1,0:T(8,128)(2,1)S(1)}, bf16[320,1281]{1,0:T(8,128)(2,1)S(1)}, u32[]{:S(2)}, u32[]{:S(2)}) %collective-permute-start.6) | collective-permute-done | bytes 819872 | tf_op jit(solution)/shard_map/ppermute | solution.py:304
  55.2 2.2 %solve.1 = bf16[64,2,640]{2,1,0:T(2,128)(2,1)S(1)} custom-call(s32[1]{0:T(128)S(6)} %copy.13.low_ref, s32[1]{0:T(128)} %bitcast.lev_ref, f32[2,8,128]{2,1,0:T(8,128)S(1)} %get-tuple-element.20.token_ref.level_ref, bf16[8,32,320]{2,1,0:T(8,128)(2,1)S(1)} %weigh.1.w_ref, f32[8,2,320]{2,1,0:T(2,128)S(1)} %get-tuple-element.21.scale_ref, ...), custom_call_target="tpu_custom_call" | custom-call | flops 1888911360 | bytes 7378560 | tf_op jit(solution)/shard_map/solve/pallas_call | solution.py:292
  57.4 19.5 %all_to_all.10.b_ref = bf16[64,2,640]{2,1,0:T(2,128)(2,1)S(1)} all-to-all(bf16[64,2,640]{2,1,0:T(2,128)(2,1)S(1)} %solve.1), channel_id=1, replica_groups=mesh['wave'=64,'lev'=8] {'wave'}, dimensions={0} | all-to-all | bytes 327680 | tf_op jit(solution)/shard_map/all_to_all | solution.py:326
  76.9 1.7 %unpack.1 = bf16[2,4,40,256]{3,2,1,0:T(8,128)(2,1)} custom-call(bf16[64,2,640]{2,1,0:T(2,128)(2,1)S(1)} %all_to_all.10.b_ref), custom_call_target="tpu_custom_call" | custom-call | flops 419758080 | bytes 1311744 | tf_op jit(solution)/shard_map/unpack/pallas_call | solution.py:240
  (6 shorter events, 0.0 us)
Async XLA Ops:
  0.0 28.6 %collective-permute-start = (bf16[320,1281]{1,0:T(8,128)(2,1)}, bf16[320,1281]{1,0:T(8,128)(2,1)S(1)}, u32[]{:S(2)}, u32[]{:S(2)}) collective-permute-start(bf16[320,1281]{1,0:T(8,128)(2,1)} %bitcast.4), channel_id=1, source_target_pairs={{0,2},{1,7},{2,4},{3,1},{4,6},{5,3},{6,0},{7,5},{8,10},{9,15},{10,... | collective-permute-start | bytes 2459528 | tf_op jit(solution)/shard_map/ppermute | solution.py:300
  8.1 30.6 %collective-permute-start.1 = (bf16[320,1281]{1,0:T(8,128)(2,1)}, bf16[320,1281]{1,0:T(8,128)(2,1)S(1)}, u32[]{:S(2)}, u32[]{:S(2)}) collective-permute-start(bf16[320,1281]{1,0:T(8,128)(2,1)} %get-tuple-element.22), channel_id=1, source_target_pairs={{0,6},{1,3},{2,0},{3,5},{4,2},{5,7},{6,4},{7,1},{8,14},{9,11},{10,... | collective-permute-start | bytes 2459528 | tf_op jit(solution)/shard_map/ppermute | solution.py:300
  10.0 17.1 %copy-start.4 = (s32[2560]{0:T(1024)S(1)}, s32[2560]{0:T(1024)}, u32[]{:S(2)}) copy-start(s32[2560]{0:T(1024)} %param.8) | copy-start | bytes 30724
  10.0 17.2 %copy-start = (bf16[64,2,640]{2,1,0:T(2,128)(2,1)S(1)}, bf16[64,2,640]{2,1,0:T(2,128)(2,1)}, u32[]{:S(2)}) copy-start(bf16[64,2,640]{2,1,0:T(2,128)(2,1)} %get-tuple-element.19.token_ref) | copy-start | bytes 491524
  10.1 28.2 %all-to-all-start = ((bf16[64,2,640]{2,1,0:T(2,128)(2,1)}), bf16[64,2,640]{2,1,0:T(2,128)(2,1)S(1)}, u32[]{:S(2)}, u32[]{:S(2)}) async-start(bf16[64,2,640]{2,1,0:T(2,128)(2,1)} %get-tuple-element.19.token_ref), calls=%async_computation | async-start | bytes 327680 | tf_op jit(solution)/shard_map/all_to_all | solution.py:313
  27.2 0.7 copy-start.1
  27.2 0.7 copy-start.2
  28.6 22.2 %collective-permute-start.5 = (bf16[320,1281]{1,0:T(8,128)(2,1)S(1)}, bf16[320,1281]{1,0:T(8,128)(2,1)S(1)}, u32[]{:S(2)}, u32[]{:S(2)}) collective-permute-start(bf16[320,1281]{1,0:T(8,128)(2,1)S(1)} %pass_on.3.refs_1_), channel_id=1, source_target_pairs={{0,2},{1,7},{2,4},{3,1},{4,6},{5,3},{6,0},{7,5},{8,10},{9,15},{10,... | collective-permute-start | bytes 2459528 | tf_op jit(solution)/shard_map/ppermute | solution.py:300
  38.7 1.2 %copy-start.3 = (bf16[1,1281,320]{1,2,0:T(8,128)(2,1)S(1)}, bf16[1,1281,320]{1,2,0:T(8,128)(2,1)}, u32[]{:S(2)}) copy-start(bf16[1,1281,320]{1,2,0:T(8,128)(2,1)} %param.7) | copy-start | bytes 2459524
  41.6 11.1 %collective-permute-start.2 = (bf16[320,1281]{1,0:T(8,128)(2,1)S(1)}, bf16[320,1281]{1,0:T(8,128)(2,1)S(1)}, u32[]{:S(2)}, u32[]{:S(2)}) collective-permute-start(bf16[320,1281]{1,0:T(8,128)(2,1)S(1)} %get-tuple-element.24), channel_id=1, source_target_pairs={{0,1},{1,0},{2,3},{3,2},{4,5},{5,4},{6,7},{7,6},{8,9},{9,8},{10,11... | collective-permute-start | bytes 2459528 | tf_op jit(solution)/shard_map/ppermute | solution.py:304
  46.4 6.3 %collective-permute-start.3 = (bf16[320,1281]{1,0:T(8,128)(2,1)S(1)}, bf16[320,1281]{1,0:T(8,128)(2,1)S(1)}, u32[]{:S(2)}, u32[]{:S(2)}) collective-permute-start(bf16[320,1281]{1,0:T(8,128)(2,1)S(1)} %pass_on.3.refs_1_), channel_id=1, source_target_pairs={{0,1},{1,0},{2,3},{3,2},{4,5},{5,4},{6,7},{7,6},{8,9},{9,8},{10,11... | collective-permute-start | bytes 2459528 | tf_op jit(solution)/shard_map/ppermute | solution.py:304
  48.4 4.5 %collective-permute-start.4 = (bf16[320,1281]{1,0:T(8,128)(2,1)S(1)}, bf16[320,1281]{1,0:T(8,128)(2,1)S(1)}, u32[]{:S(2)}, u32[]{:S(2)}) collective-permute-start(bf16[320,1281]{1,0:T(8,128)(2,1)S(1)} %pass_on.4.refs_2_), channel_id=1, source_target_pairs={{0,1},{1,0},{2,3},{3,2},{4,5},{5,4},{6,7},{7,6},{8,9},{9,8},{10,11... | collective-permute-start | bytes 2459528 | tf_op jit(solution)/shard_map/ppermute | solution.py:304
  50.8 4.3 %collective-permute-start.6 = (bf16[320,1281]{1,0:T(8,128)(2,1)S(1)}, bf16[320,1281]{1,0:T(8,128)(2,1)S(1)}, u32[]{:S(2)}, u32[]{:S(2)}) collective-permute-start(bf16[320,1281]{1,0:T(8,128)(2,1)S(1)} %pass_on.5.refs_3_), channel_id=1, source_target_pairs={{0,1},{1,0},{2,3},{3,2},{4,5},{5,4},{6,7},{7,6},{8,9},{9,8},{10,11... | collective-permute-start | bytes 2459528 | tf_op jit(solution)/shard_map/ppermute | solution.py:304

commit v7 on v5

--- a/solution.py
+++ b/solution.py
@@ -17,7 +17,7 @@
 STEPS = R // 4
 COLS = 32
 HALF = 640
-NEAR = 73 * 10**8
+NEAR = 75 * 10**8
 NEARS = 3
 FARS = 4
 
@@ -154,17 +154,16 @@
 
 
 def near_kernel(lev_ref, w_ref, *refs):
-    tabs, raw_ref, turned, same_ref, held, sems = refs[:NEARS], refs[NEARS], refs[NEARS + 1:-3], *refs[-3:]
-    places = [same_ref] + [held.at[n] for n in range(NEARS - 1)]
-    copies = [pltpu.make_async_copy(tabs[n], places[n], sems.at[n]) for n in range(NEARS)]
+    tabs, raw_ref, turned, held, sems = refs[:NEARS], refs[NEARS], refs[NEARS + 1:-2], *refs[-2:]
+    copies = [pltpu.make_async_copy(tabs[n], held.at[n], sems.at[n]) for n in range(NEARS)]
     for copy in copies:
         copy.start()
     slabs = slab_order(lev_ref[0])
     raw = None
     for n in range(NEARS):
         copies[n].wait()
-        raw = add_up(raw, w_ref, slabs[n:n + 1], places[n:n + 1])
-        turned[n][...] = places[n][...].T
+        raw = add_up(raw, w_ref, slabs[n:n + 1], [held.at[n]])
+        turned[n][...] = held[n].T
     raw_ref[...] = raw
 
 
@@ -267,9 +266,9 @@
 
 def near(lev, w, tabs):
     return pl.pallas_call(
-        near_kernel, out_shape=(RAW,) + (TURNED,) * NEARS + (like(tabs[0]),),
-        in_specs=[SMEM, VMEM] + [ANY] * NEARS, out_specs=(VMEM,) * (2 + NEARS),
-        scratch_shapes=[pltpu.VMEM((NEARS - 1, SLAB, KP), jnp.bfloat16), pltpu.SemaphoreType.DMA((NEARS,))],
+        near_kernel, out_shape=(RAW,) + (TURNED,) * NEARS, in_specs=[SMEM, VMEM] + [ANY] * NEARS,
+        out_specs=(VMEM,) * (1 + NEARS),
+        scratch_shapes=[pltpu.VMEM((NEARS, SLAB, KP), jnp.bfloat16), pltpu.SemaphoreType.DMA((NEARS,))],
         compiler_params=params(12), cost_estimate=pl.CostEstimate(flops=NEAR, bytes_accessed=0, transcendentals=0),
         name="near")(lev, w, *tabs)
 
@@ -308,12 +307,12 @@
     first = pass_on(level, first)
     third = along_x(first, 1)
     second = pass_on(sent, second)
-    cores = [other_core(first), other_core(second)]
+    cores = [other_core(tab) for tab in (copied, first, second)]
     weighted = weigh(moved, scale)
-    raw, *tabs, own = near(lev, weighted, [own, first, second])
+    raw, *tabs = near(lev, weighted, [own, first, second])
     third = pass_on(raw, third)
     last = other_core(third)
-    raw, *more = far(lev, weighted, raw, [other_core(own)] + cores + [third])
+    raw, *more = far(lev, weighted, raw, cores + [third])
     tabs += more + [last]
     result = solve(pair_low, lev, level, weighted, scale, raw, tabs)
     back = lax.all_to_all(result, "wave", split_axis=0, concat_axis=0, tiled=True)

time: 78.8 us -> 78.8 us (level)
  waiting for transfers between devices: 6.23 us -> 2.93 us
  blocking collectives: 19.5 us -> 22 us
  starting transfers between devices: 39.2 us -> 40.8 us
  local copies, waits for them, and re-layouts: 1.82 us -> 0.68 us
    all_to_all x1, waiting for transfers between devices: 5.06 us -> 2.13 us  [local(): lax.all_to_all(sent, 'wave', split_axis=0, concat_axis=0, tiled=True)]
    all_to_all x1, blocking collectives: 19.5 us -> 22 us  [local(): lax.all_to_all(result, 'wave', split_axis=0, concat_axis=0, tiled=True)]
    ppermute x4, starting transfers between devices: 11.1 us -> 12.7 us  [other_core(): return lax.ppermute(array, 'lev', [(d, d ^ 1) for d in range(SLABS)])]
    unnamed x10, local copies, waits for them, and re-layouts: 1.81 us -> 0.67 us
  transfers between devices with their start and end apart: 8 -> 8, of which waited for: 3 -> 2; matrix products, arithmetic and copies ran while one was open for 0% -> 0% of each run, Pallas kernels for 9% -> 9%
where the time goes in v7:
time: 78.8 us; the launch traced here: 78.2 us
  starting transfers between devices  40.8 us (52%)
  blocking collectives  22 us (28%)
  Pallas kernels  10.8 us (14%)
  waiting for transfers between devices  2.93 us (4%)
  between operations  0.91 us (1%)
    all_to_all x1, blocking collectives, local(): lax.all_to_all(result, 'wave', split_axis=0, concat_axis=0, tiled=True)  22 us
    all_to_all x1, starting transfers between devices, local(): lax.all_to_all(sent, 'wave', split_axis=0, concat_axis=0, tiled=True)  16.4 us
    ppermute x4, starting transfers between devices, other_core(): return lax.ppermute(array, 'lev', [(d, d ^ 1) for d in range(SLABS)])  12.7 us
    ppermute x3, starting transfers between devices, along_x(): lax.ppermute(array, 'lev', [(d, (d + 2 * step * (1 - 2 * (d % 2))) % SLAB...  11.7 us
    pallas_call x1, Pallas kernels, pack(): pl.pallas_call(pack_kernel, out_shape=(chunks(), like(tab)), in_specs=[AN...  2.88 us
    pallas_call x1, Pallas kernels, solve(): pl.pallas_call(solve_kernel, out_shape=chunks(), in_specs=[SMEM] * 2 + [V...  2.24 us
    all_to_all x1, waiting for transfers between devices, local(): lax.all_to_all(sent, 'wave', split_axis=0, concat_axis=0, tiled=True)  2.13 us
    pallas_call x1, Pallas kernels, near(): pl.pallas_call(near_kernel, out_shape=(RAW,) + (TURNED,) * NEARS, in_spec...  1.96 us
  transfers between devices with their start and end apart: 8, of which 2 were waited for; matrix products, arithmetic and copies ran while one was open for 0% of the time, Pallas kernels for 9%

profile of v7, /device:TPU:1, one launch (start us, length us, event | category | flops | bytes accessed | tf_op | source)
XLA Modules:
  0.0 78.2 jit_solution(4148902438969159409)
XLA Ops:
  0.0 5.2 %collective-permute-start = (bf16[320,1281]{1,0:T(8,128)(2,1)}, bf16[320,1281]{1,0:T(8,128)(2,1)S(1)}, u32[]{:S(2)}, u32[]{:S(2)}) collective-permute-start(bf16[320,1281]{1,0:T(8,128)(2,1)} %bitcast.4), channel_id=1, source_target_pairs={{0,2},{1,7},{2,4},{3,1},{4,6},{5,3},{6,0},{7,5},{8,10},{9,15},{10,... | collective-permute-start | bytes 2459528 | tf_op jit(solution)/shard_map/ppermute | solution.py:292
  5.2 2.9 %pack.1 = (bf16[64,2,640]{2,1,0:T(2,128)(2,1)}, bf16[320,1281]{1,0:T(8,128)(2,1)}) custom-call(bf16[2,4,40,256]{3,2,1,0:T(8,128)(2,1)} %x_ref.1, bf16[320,1281]{1,0:T(8,128)(2,1)} %bitcast.5), custom_call_target="tpu_custom_call" | custom-call | flops 419758080 | bytes 1639680 | tf_op jit(solution)/shard_map/pack/pallas_call | solution.py:225
  8.1 1.9 %collective-permute-start.1 = (bf16[320,1281]{1,0:T(8,128)(2,1)}, bf16[320,1281]{1,0:T(8,128)(2,1)}, u32[]{:S(2)}, u32[]{:S(2)}) collective-permute-start(bf16[320,1281]{1,0:T(8,128)(2,1)} %get-tuple-element.21), channel_id=1, source_target_pairs={{0,6},{1,3},{2,0},{3,5},{4,2},{5,7},{6,4},{7,1},{8,14},{9,11},{10,... | collective-permute-start | bytes 2459528 | tf_op jit(solution)/shard_map/ppermute | solution.py:292
  10.0 0.0 copy-start.4
  10.0 0.0 copy-start
  10.1 16.4 %all-to-all-start = ((bf16[64,2,640]{2,1,0:T(2,128)(2,1)}), bf16[64,2,640]{2,1,0:T(2,128)(2,1)S(1)}, u32[]{:S(2)}, u32[]{:S(2)}) async-start(bf16[64,2,640]{2,1,0:T(2,128)(2,1)} %get-tuple-element.18.token_ref), calls=%async_computation | async-start | bytes 327680 | tf_op jit(solution)/shard_map/all_to_all | solution.py:305
  27.2 0.0 copy-start.1
  27.2 0.0 copy-start.2
  27.2 0.0 copy-done
  27.2 0.6 copy-done.1
  27.8 0.0 copy-done.2
  27.9 0.8 coef.1
  28.6 0.0 collective-permute-done.tab_ref
  28.6 4.6 %collective-permute-start.5 = (bf16[320,1281]{1,0:T(8,128)(2,1)S(1)}, bf16[320,1281]{1,0:T(8,128)(2,1)S(1)}, u32[]{:S(2)}, u32[]{:S(2)}) collective-permute-start(bf16[320,1281]{1,0:T(8,128)(2,1)S(1)} %pass_on.3.refs_1_), channel_id=1, source_target_pairs={{0,2},{1,7},{2,4},{3,1},{4,6},{5,3},{6,0},{7,5},{8,10},{9,15},{10,... | collective-permute-start | bytes 2459528 | tf_op jit(solution)/shard_map/ppermute | solution.py:292
  33.2 2.9 %collective-permute-start.2 = (bf16[320,1281]{1,0:T(8,128)(2,1)}, bf16[320,1281]{1,0:T(8,128)(2,1)S(1)}, u32[]{:S(2)}, u32[]{:S(2)}) collective-permute-start(bf16[320,1281]{1,0:T(8,128)(2,1)} %get-tuple-element.21), channel_id=1, source_target_pairs={{0,1},{1,0},{2,3},{3,2},{4,5},{5,4},{6,7},{7,6},{8,9},{9,8},{10,11... | collective-permute-start | bytes 2459528 | tf_op jit(solution)/shard_map/ppermute | solution.py:296
  36.2 2.1 %all-to-all-done.y_ref = bf16[64,2,640]{2,1,0:T(2,128)(2,1)S(1)} async-done(((bf16[64,2,640]{2,1,0:T(2,128)(2,1)}), bf16[64,2,640]{2,1,0:T(2,128)(2,1)S(1)}, u32[]{:S(2)}, u32[]{:S(2)}) %all-to-all-start) | async-done | bytes 163872 | tf_op jit(solution)/shard_map/all_to_all | solution.py:305
  38.3 0.4 weigh.1.w_ref
  38.7 0.0 copy-start.3
  38.7 4.9 %collective-permute-start.3 = (bf16[320,1281]{1,0:T(8,128)(2,1)S(1)}, bf16[320,1281]{1,0:T(8,128)(2,1)S(1)}, u32[]{:S(2)}, u32[]{:S(2)}) collective-permute-start(bf16[320,1281]{1,0:T(8,128)(2,1)S(1)} %pass_on.3.refs_1_), channel_id=1, source_target_pairs={{0,1},{1,0},{2,3},{3,2},{4,5},{5,4},{6,7},{7,6},{8,9},{9,8},{10,11... | collective-permute-start | bytes 2459528 | tf_op jit(solution)/shard_map/ppermute | solution.py:296
  43.7 0.0 collective-permute-done.1.tab_ref
  43.7 1.9 %collective-permute-start.4 = (bf16[320,1281]{1,0:T(8,128)(2,1)}, bf16[320,1281]{1,0:T(8,128)(2,1)S(1)}, u32[]{:S(2)}, u32[]{:S(2)}) collective-permute-start(bf16[320,1281]{1,0:T(8,128)(2,1)} %pass_on.4.refs_2_), channel_id=1, source_target_pairs={{0,1},{1,0},{2,3},{3,2},{4,5},{5,4},{6,7},{7,6},{8,9},{9,8},{10,11... | collective-permute-start | bytes 2459528 | tf_op jit(solution)/shard_map/ppermute | solution.py:296
  45.7 2.0 %near.1 = (f32[32,1281]{1,0:T(8,128)S(1)}, bf16[1281,320]{1,0:T(8,128)(2,1)S(1)}, bf16[1281,320]{1,0:T(8,128)(2,1)S(1)}, bf16[1281,320]{1,0:T(8,128)(2,1)S(1)}) custom-call(s32[1]{0:T(128)} %bitcast.lev_ref, bf16[8,32,320]{2,1,0:T(8,128)(2,1)S(1)} %weigh.1.w_ref, bf16[320,1281]{1,0:T(8,128)(2,1)S(1)} %bitcast.6, bf16[320,1281]{1,0:T(8,128)(2,1)S(1)} %pass_on.3.refs_1_, ...), custom_call_target="tpu_custom_call" | custom-call | flops 7500000256 | tf_op jit(solution)/shard_map/near/pallas_call | solution.py:268
  47.6 0.0 collective-permute-done.5.tab_ref
  47.7 2.9 %collective-permute-start.6 = (bf16[320,1281]{1,0:T(8,128)(2,1)S(1)}, bf16[320,1281]{1,0:T(8,128)(2,1)S(1)}, u32[]{:S(2)}, u32[]{:S(2)}) collective-permute-start(bf16[320,1281]{1,0:T(8,128)(2,1)S(1)} %pass_on.5.refs_3_), channel_id=1, source_target_pairs={{0,1},{1,0},{2,3},{3,2},{4,5},{5,4},{6,7},{7,6},{8,9},{9,8},{10,11... | collective-permute-start | bytes 2459528 | tf_op jit(solution)/shard_map/ppermute | solution.py:296
  50.5 0.0 collective-permute-done.2.refs_0_
  50.5 0.0 collective-permute-done.3.refs_1_
  50.6 0.0 collective-permute-done.4.refs_2_
  50.6 1.2 %far.1 = (f32[32,1281]{1,0:T(8,128)S(1)}, bf16[1281,320]{1,0:T(8,128)(2,1)S(1)}, bf16[1281,320]{1,0:T(8,128)(2,1)S(1)}, bf16[1281,320]{1,0:T(8,128)(2,1)S(1)}, bf16[1281,320]{1,0:T(8,128)(2,1)S(1)}) custom-call(s32[1]{0:T(128)} %bitcast.lev_ref, bf16[8,32,320]{2,1,0:T(8,128)(2,1)S(1)} %weigh.1.w_ref, f32[32,1281]{1,0:T(8,128)S(1)} %get-tuple-element.22.token_ref.raw_ref, ...), custom_call_target="tpu_custom_call" | custom-call | flops 839516160 | bytes 3279360 | tf_op jit(solution)/shard_map/far/pallas_call | solution.py:277
  51.8 0.8 %collective-permute-done.6.refs_7_ = bf16[320,1281]{1,0:T(8,128)(2,1)S(1)} collective-permute-done((bf16[320,1281]{1,0:T(8,128)(2,1)S(1)}, bf16[320,1281]{1,0:T(8,128)(2,1)S(1)}, u32[]{:S(2)}, u32[]{:S(2)}) %collective-permute-start.6) | collective-permute-done | bytes 819872 | tf_op jit(solution)/shard_map/ppermute | solution.py:296
  52.6 2.2 %solve.1 = bf16[64,2,640]{2,1,0:T(2,128)(2,1)S(1)} custom-call(s32[1]{0:T(128)S(6)} %copy.13.low_ref, s32[1]{0:T(128)} %bitcast.lev_ref, f32[2,8,128]{2,1,0:T(8,128)S(1)} %get-tuple-element.19.token_ref.level_ref, bf16[8,32,320]{2,1,0:T(8,128)(2,1)S(1)} %weigh.1.w_ref, f32[8,2,320]{2,1,0:T(2,128)S(1)} %get-tuple-element.20.scale_ref, ...), custom_call_target="tpu_custom_call" | custom-call | flops 1888911360 | bytes 7378560 | tf_op jit(solution)/shard_map/solve/pallas_call | solution.py:284
  54.8 22.0 %all_to_all.10.b_ref = bf16[64,2,640]{2,1,0:T(2,128)(2,1)S(1)} all-to-all(bf16[64,2,640]{2,1,0:T(2,128)(2,1)S(1)} %solve.1), channel_id=1, replica_groups=mesh['wave'=64,'lev'=8] {'wave'}, dimensions={0} | all-to-all | bytes 327680 | tf_op jit(solution)/shard_map/all_to_all | solution.py:318
  76.9 1.3 %unpack.1 = bf16[2,4,40,256]{3,2,1,0:T(8,128)(2,1)} custom-call(bf16[64,2,640]{2,1,0:T(2,128)(2,1)S(1)} %all_to_all.10.b_ref), custom_call_target="tpu_custom_call" | custom-call | flops 419758080 | bytes 1311744 | tf_op jit(solution)/shard_map/unpack/pallas_call | solution.py:232
  (6 shorter events, 0.0 us)
Async XLA Ops:
  0.0 28.6 %collective-permute-start = (bf16[320,1281]{1,0:T(8,128)(2,1)}, bf16[320,1281]{1,0:T(8,128)(2,1)S(1)}, u32[]{:S(2)}, u32[]{:S(2)}) collective-permute-start(bf16[320,1281]{1,0:T(8,128)(2,1)} %bitcast.4), channel_id=1, source_target_pairs={{0,2},{1,7},{2,4},{3,1},{4,6},{5,3},{6,0},{7,5},{8,10},{9,15},{10,... | collective-permute-start | bytes 2459528 | tf_op jit(solution)/shard_map/ppermute | solution.py:292
  8.1 35.6 %collective-permute-start.1 = (bf16[320,1281]{1,0:T(8,128)(2,1)}, bf16[320,1281]{1,0:T(8,128)(2,1)}, u32[]{:S(2)}, u32[]{:S(2)}) collective-permute-start(bf16[320,1281]{1,0:T(8,128)(2,1)} %get-tuple-element.21), channel_id=1, source_target_pairs={{0,6},{1,3},{2,0},{3,5},{4,2},{5,7},{6,4},{7,1},{8,14},{9,11},{10,... | collective-permute-start | bytes 2459528 | tf_op jit(solution)/shard_map/ppermute | solution.py:292
  10.0 17.1 %copy-start.4 = (s32[2560]{0:T(1024)S(1)}, s32[2560]{0:T(1024)}, u32[]{:S(2)}) copy-start(s32[2560]{0:T(1024)} %param.8) | copy-start | bytes 30724
  10.0 17.2 %copy-start = (bf16[64,2,640]{2,1,0:T(2,128)(2,1)S(1)}, bf16[64,2,640]{2,1,0:T(2,128)(2,1)}, u32[]{:S(2)}) copy-start(bf16[64,2,640]{2,1,0:T(2,128)(2,1)} %get-tuple-element.18.token_ref) | copy-start | bytes 491524
  10.1 28.2 %all-to-all-start = ((bf16[64,2,640]{2,1,0:T(2,128)(2,1)}), bf16[64,2,640]{2,1,0:T(2,128)(2,1)S(1)}, u32[]{:S(2)}, u32[]{:S(2)}) async-start(bf16[64,2,640]{2,1,0:T(2,128)(2,1)} %get-tuple-element.18.token_ref), calls=%async_computation | async-start | bytes 327680 | tf_op jit(solution)/shard_map/all_to_all | solution.py:305
  27.2 0.7 copy-start.1
  27.2 0.7 copy-start.2
  28.6 19.0 %collective-permute-start.5 = (bf16[320,1281]{1,0:T(8,128)(2,1)S(1)}, bf16[320,1281]{1,0:T(8,128)(2,1)S(1)}, u32[]{:S(2)}, u32[]{:S(2)}) collective-permute-start(bf16[320,1281]{1,0:T(8,128)(2,1)S(1)} %pass_on.3.refs_1_), channel_id=1, source_target_pairs={{0,2},{1,7},{2,4},{3,1},{4,6},{5,3},{6,0},{7,5},{8,10},{9,15},{10,... | collective-permute-start | bytes 2459528 | tf_op jit(solution)/shard_map/ppermute | solution.py:292
  33.2 17.3 %collective-permute-start.2 = (bf16[320,1281]{1,0:T(8,128)(2,1)}, bf16[320,1281]{1,0:T(8,128)(2,1)S(1)}, u32[]{:S(2)}, u32[]{:S(2)}) collective-permute-start(bf16[320,1281]{1,0:T(8,128)(2,1)} %get-tuple-element.21), channel_id=1, source_target_pairs={{0,1},{1,0},{2,3},{3,2},{4,5},{5,4},{6,7},{7,6},{8,9},{9,8},{10,11... | collective-permute-start | bytes 2459528 | tf_op jit(solution)/shard_map/ppermute | solution.py:296
  38.7 6.9 %copy-start.3 = (bf16[1,1281,320]{1,2,0:T(8,128)(2,1)S(1)}, bf16[1,1281,320]{1,2,0:T(8,128)(2,1)}, u32[]{:S(2)}) copy-start(bf16[1,1281,320]{1,2,0:T(8,128)(2,1)} %param.7) | copy-start | bytes 2459524
  38.7 11.8 %collective-permute-start.3 = (bf16[320,1281]{1,0:T(8,128)(2,1)S(1)}, bf16[320,1281]{1,0:T(8,128)(2,1)S(1)}, u32[]{:S(2)}, u32[]{:S(2)}) collective-permute-start(bf16[320,1281]{1,0:T(8,128)(2,1)S(1)} %pass_on.3.refs_1_), channel_id=1, source_target_pairs={{0,1},{1,0},{2,3},{3,2},{4,5},{5,4},{6,7},{7,6},{8,9},{9,8},{10,11... | collective-permute-start | bytes 2459528 | tf_op jit(solution)/shard_map/ppermute | solution.py:296
  43.7 6.8 %collective-permute-start.4 = (bf16[320,1281]{1,0:T(8,128)(2,1)}, bf16[320,1281]{1,0:T(8,128)(2,1)S(1)}, u32[]{:S(2)}, u32[]{:S(2)}) collective-permute-start(bf16[320,1281]{1,0:T(8,128)(2,1)} %pass_on.4.refs_2_), channel_id=1, source_target_pairs={{0,1},{1,0},{2,3},{3,2},{4,5},{5,4},{6,7},{7,6},{8,9},{9,8},{10,11... | collective-permute-start | bytes 2459528 | tf_op jit(solution)/shard_map/ppermute | solution.py:296
  47.7 4.9 %collective-permute-start.6 = (bf16[320,1281]{1,0:T(8,128)(2,1)S(1)}, bf16[320,1281]{1,0:T(8,128)(2,1)S(1)}, u32[]{:S(2)}, u32[]{:S(2)}) collective-permute-start(bf16[320,1281]{1,0:T(8,128)(2,1)S(1)} %pass_on.5.refs_3_), channel_id=1, source_target_pairs={{0,1},{1,0},{2,3},{3,2},{4,5},{5,4},{6,7},{7,6},{8,9},{9,8},{10,11... | collective-permute-start | bytes 2459528 | tf_op jit(solution)/shard_map/ppermute | solution.py:296

commit v8 on v7

--- a/solution.py
+++ b/solution.py
@@ -105,7 +105,7 @@
     return (iota((4 * COLS, SLAB), 0) >> 5) == (iota((4 * COLS, SLAB), 1) & 3)
 
 
-def coef_kernel(low_ref, lev_ref, gamma_ref, beta_ref, points_ref, token_ref, scale_ref, level_ref):
+def coef_kernel(low_ref, lev_ref, gamma_ref, beta_ref, points_ref, scale_ref, level_ref):
     low = low_ref[0]
     points = jnp.concatenate([points_ref[:, s * SLAB:(s + 1) * SLAB] for s in range(SLABS)], axis=0)
     pts = points.astype(jnp.float32)
@@ -234,12 +234,12 @@
                           name="unpack")(b)
 
 
-def coef(low, lev, gamma, beta, points, token):
+def coef(low, lev, gamma, beta, points):
     return pl.pallas_call(
         coef_kernel, out_shape=(jax.ShapeDtypeStruct((SLABS, 2, SLAB), jnp.float32),
                                 jax.ShapeDtypeStruct((2, SLABS, 128), jnp.float32)),
-        in_specs=[SMEM] * 4 + [VMEM, ANY], out_specs=(VMEM,) * 2, compiler_params=params(8),
-        name="coef")(low, lev, gamma, beta, points, token)
+        in_specs=[SMEM] * 4 + [VMEM], out_specs=(VMEM,) * 2, compiler_params=params(8),
+        name="coef")(low, lev, gamma, beta, points)
 
 
 def like(tab):
@@ -303,8 +303,8 @@
     sent, copied = pack(fourier_in, own)
     second = along_x(copied, -1)
     moved = lax.all_to_all(sent, "wave", split_axis=0, concat_axis=0, tiled=True)
-    scale, level = coef(pair_low, lev, gamma, beta, points.reshape(1, NLAT), sent)
-    first = pass_on(level, first)
+    scale, level = coef(pair_low, lev, gamma, beta, points.reshape(1, NLAT))
+    first = pass_on(sent, first)
     third = along_x(first, 1)
     second = pass_on(sent, second)
     cores = [other_core(tab) for tab in (copied, first, second)]

time: 78.8 us -> 77 us (0.977)
  starting transfers between devices: 40.8 us -> 43.2 us
  blocking collectives: 22 us -> 19.7 us
  waiting for transfers between devices: 2.93 us -> 0.8 us
    ppermute x4, starting transfers between devices: 12.7 us -> 15 us  [other_core(): return lax.ppermute(array, 'lev', [(d, d ^ 1) for d in range(SLABS)])]
    all_to_all x1, blocking collectives: 22 us -> 19.7 us  [local(): lax.all_to_all(result, 'wave', split_axis=0, concat_axis=0, tiled=True)]
    all_to_all x1, waiting for transfers between devices: 2.13 us -> 0.01 us  [local(): lax.all_to_all(sent, 'wave', split_axis=0, concat_axis=0, tiled=True)]
  transfers between devices with their start and end apart: 8 -> 8, of which waited for: 2 -> 1; matrix products, arithmetic and copies ran while one was open for 0% -> 0% of each run, Pallas kernels for 9% -> 10%
where the time goes in v8:
time: 77 us; the launch traced here: 76.3 us
  starting transfers between devices  43.2 us (56%)
  blocking collectives  19.7 us (26%)
  Pallas kernels  11 us (14%)
  between operations  0.91 us (1%)
  waiting for transfers between devices  0.8 us (1%)
    all_to_all x1, blocking collectives, local(): lax.all_to_all(result, 'wave', split_axis=0, concat_axis=0, tiled=True)  19.7 us
    all_to_all x1, starting transfers between devices, local(): lax.all_to_all(sent, 'wave', split_axis=0, concat_axis=0, tiled=True)  16.5 us
    ppermute x4, starting transfers between devices, other_core(): return lax.ppermute(array, 'lev', [(d, d ^ 1) for d in range(SLABS)])  15 us
    ppermute x3, starting transfers between devices, along_x(): lax.ppermute(array, 'lev', [(d, (d + 2 * step * (1 - 2 * (d % 2))) % SLAB...  11.7 us
    pallas_call x1, Pallas kernels, pack(): pl.pallas_call(pack_kernel, out_shape=(chunks(), like(tab)), in_specs=[AN...  2.88 us
    pallas_call x1, Pallas kernels, solve(): pl.pallas_call(solve_kernel, out_shape=chunks(), in_specs=[SMEM] * 2 + [V...  2.24 us
    pallas_call x1, Pallas kernels, near(): pl.pallas_call(near_kernel, out_shape=(RAW,) + (TURNED,) * NEARS, in_spec...  2.15 us
  transfers between devices with their start and end apart: 8, of which 1 were waited for; matrix products, arithmetic and copies ran while one was open for 0% of the time, Pallas kernels for 10%

profile of v8, /device:TPU:1, one launch (start us, length us, event | category | flops | bytes accessed | tf_op | source)
XLA Modules:
  0.0 76.3 jit_solution(557334453227912670)
XLA Ops:
  0.0 5.2 %collective-permute-start = (bf16[320,1281]{1,0:T(8,128)(2,1)}, bf16[320,1281]{1,0:T(8,128)(2,1)}, u32[]{:S(2)}, u32[]{:S(2)}) collective-permute-start(bf16[320,1281]{1,0:T(8,128)(2,1)} %bitcast.4), channel_id=1, source_target_pairs={{0,2},{1,7},{2,4},{3,1},{4,6},{5,3},{6,0},{7,5},{8,10},{9,15},{10,... | collective-permute-start | bytes 2459528 | tf_op jit(solution)/shard_map/ppermute | solution.py:292
  5.2 2.9 %pack.1 = (bf16[64,2,640]{2,1,0:T(2,128)(2,1)}, bf16[320,1281]{1,0:T(8,128)(2,1)}) custom-call(bf16[2,4,40,256]{3,2,1,0:T(8,128)(2,1)} %x_ref.1, bf16[320,1281]{1,0:T(8,128)(2,1)} %bitcast.5), custom_call_target="tpu_custom_call" | custom-call | flops 419758080 | bytes 1639680 | tf_op jit(solution)/shard_map/pack/pallas_call | solution.py:225
  8.1 1.9 %collective-permute-start.1 = (bf16[320,1281]{1,0:T(8,128)(2,1)}, bf16[320,1281]{1,0:T(8,128)(2,1)S(1)}, u32[]{:S(2)}, u32[]{:S(2)}) collective-permute-start(bf16[320,1281]{1,0:T(8,128)(2,1)} %get-tuple-element.21), channel_id=1, source_target_pairs={{0,6},{1,3},{2,0},{3,5},{4,2},{5,7},{6,4},{7,1},{8,14},{9,11},{10,... | collective-permute-start | bytes 2459528 | tf_op jit(solution)/shard_map/ppermute | solution.py:292
  10.0 0.0 copy-start
  10.0 16.5 %all-to-all-start = ((bf16[64,2,640]{2,1,0:T(2,128)(2,1)}), bf16[64,2,640]{2,1,0:T(2,128)(2,1)S(1)}, u32[]{:S(2)}, u32[]{:S(2)}) async-start(bf16[64,2,640]{2,1,0:T(2,128)(2,1)} %get-tuple-element.19.token_ref), calls=%async_computation | async-start | bytes 327680 | tf_op jit(solution)/shard_map/all_to_all | solution.py:305
  26.5 0.0 collective-permute-done.tab_ref
  26.5 0.0 copy-start.4
  26.5 4.6 %collective-permute-start.5 = (bf16[320,1281]{1,0:T(8,128)(2,1)}, bf16[320,1281]{1,0:T(8,128)(2,1)S(1)}, u32[]{:S(2)}, u32[]{:S(2)}) collective-permute-start(bf16[320,1281]{1,0:T(8,128)(2,1)} %pass_on.3.refs_1_), channel_id=1, source_target_pairs={{0,2},{1,7},{2,4},{3,1},{4,6},{5,3},{6,0},{7,5},{8,10},{9,15},{10,... | collective-permute-start | bytes 2459528 | tf_op jit(solution)/shard_map/ppermute | solution.py:292
  31.1 5.3 %collective-permute-start.2 = (bf16[320,1281]{1,0:T(8,128)(2,1)}, bf16[320,1281]{1,0:T(8,128)(2,1)S(1)}, u32[]{:S(2)}, u32[]{:S(2)}) collective-permute-start(bf16[320,1281]{1,0:T(8,128)(2,1)} %get-tuple-element.21), channel_id=1, source_target_pairs={{0,1},{1,0},{2,3},{3,2},{4,5},{5,4},{6,7},{7,6},{8,9},{9,8},{10,11... | collective-permute-start | bytes 2459528 | tf_op jit(solution)/shard_map/ppermute | solution.py:296
  37.1 0.0 copy-start.1
  37.1 0.0 copy-start.2
  37.1 0.6 copy-done.1
  37.7 0.0 copy-done.2
  37.7 0.8 coef.1
  38.5 0.0 all-to-all-done.y_ref
  38.5 0.4 weigh.1.w_ref
  39.0 0.0 copy-start.3
  39.0 4.7 %collective-permute-start.3 = (bf16[320,1281]{1,0:T(8,128)(2,1)}, bf16[320,1281]{1,0:T(8,128)(2,1)S(1)}, u32[]{:S(2)}, u32[]{:S(2)}) collective-permute-start(bf16[320,1281]{1,0:T(8,128)(2,1)} %pass_on.3.refs_1_), channel_id=1, source_target_pairs={{0,1},{1,0},{2,3},{3,2},{4,5},{5,4},{6,7},{7,6},{8,9},{9,8},{10,11... | collective-permute-start | bytes 2459528 | tf_op jit(solution)/shard_map/ppermute | solution.py:296
  43.7 0.0 collective-permute-done.1.tab_ref
  43.7 1.9 %collective-permute-start.4 = (bf16[320,1281]{1,0:T(8,128)(2,1)S(1)}, bf16[320,1281]{1,0:T(8,128)(2,1)S(1)}, u32[]{:S(2)}, u32[]{:S(2)}) collective-permute-start(bf16[320,1281]{1,0:T(8,128)(2,1)S(1)} %pass_on.4.refs_2_), channel_id=1, source_target_pairs={{0,1},{1,0},{2,3},{3,2},{4,5},{5,4},{6,7},{7,6},{8,9},{9,8},{10,11... | collective-permute-start | bytes 2459528 | tf_op jit(solution)/shard_map/ppermute | solution.py:296
  45.6 0.0 copy-done.3
  45.6 2.1 %near.1 = (f32[32,1281]{1,0:T(8,128)S(1)}, bf16[1281,320]{1,0:T(8,128)(2,1)S(1)}, bf16[1281,320]{1,0:T(8,128)(2,1)S(1)}, bf16[1281,320]{1,0:T(8,128)(2,1)S(1)}) custom-call(s32[1]{0:T(128)} %bitcast.lev_ref, bf16[8,32,320]{2,1,0:T(8,128)(2,1)S(1)} %weigh.1.w_ref, bf16[320,1281]{1,0:T(8,128)(2,1)S(1)} %bitcast.6, bf16[320,1281]{1,0:T(8,128)(2,1)} %pass_on.3.refs_1_, ...), custom_call_target="tpu_custom_call" | custom-call | flops 7500000256 | tf_op jit(solution)/shard_map/near/pallas_call | solution.py:268
  47.8 0.0 collective-permute-done.5.tab_ref
  47.8 3.2 %collective-permute-start.6 = (bf16[320,1281]{1,0:T(8,128)(2,1)S(1)}, bf16[320,1281]{1,0:T(8,128)(2,1)S(1)}, u32[]{:S(2)}, u32[]{:S(2)}) collective-permute-start(bf16[320,1281]{1,0:T(8,128)(2,1)S(1)} %pass_on.5.refs_3_), channel_id=1, source_target_pairs={{0,1},{1,0},{2,3},{3,2},{4,5},{5,4},{6,7},{7,6},{8,9},{9,8},{10,11... | collective-permute-start | bytes 2459528 | tf_op jit(solution)/shard_map/ppermute | solution.py:296
  51.0 0.0 collective-permute-done.2.refs_0_
  51.0 0.0 collective-permute-done.3.refs_1_
  51.0 0.0 collective-permute-done.4.refs_2_
  51.0 1.2 %far.1 = (f32[32,1281]{1,0:T(8,128)S(1)}, bf16[1281,320]{1,0:T(8,128)(2,1)S(1)}, bf16[1281,320]{1,0:T(8,128)(2,1)S(1)}, bf16[1281,320]{1,0:T(8,128)(2,1)S(1)}, bf16[1281,320]{1,0:T(8,128)(2,1)S(1)}) custom-call(s32[1]{0:T(128)} %bitcast.lev_ref, bf16[8,32,320]{2,1,0:T(8,128)(2,1)S(1)} %weigh.1.w_ref, f32[32,1281]{1,0:T(8,128)S(1)} %get-tuple-element.22.token_ref.raw_ref, ...), custom_call_target="tpu_custom_call" | custom-call | flops 839516160 | bytes 3279360 | tf_op jit(solution)/shard_map/far/pallas_call | solution.py:277
  52.3 0.8 %collective-permute-done.6.refs_7_ = bf16[320,1281]{1,0:T(8,128)(2,1)S(1)} collective-permute-done((bf16[320,1281]{1,0:T(8,128)(2,1)S(1)}, bf16[320,1281]{1,0:T(8,128)(2,1)S(1)}, u32[]{:S(2)}, u32[]{:S(2)}) %collective-permute-start.6) | collective-permute-done | bytes 819872 | tf_op jit(solution)/shard_map/ppermute | solution.py:296
  53.0 2.2 %solve.1 = bf16[64,2,640]{2,1,0:T(2,128)(2,1)S(1)} custom-call(s32[1]{0:T(128)S(6)} %copy.13.low_ref, s32[1]{0:T(128)} %bitcast.lev_ref, f32[2,8,128]{2,1,0:T(8,128)S(1)} %get-tuple-element.18.level_ref, bf16[8,32,320]{2,1,0:T(8,128)(2,1)S(1)} %weigh.1.w_ref, f32[8,2,320]{2,1,0:T(2,128)S(1)} %get-tuple-element.20.scale_ref, ...), custom_call_target="tpu_custom_call" | custom-call | flops 1888911360 | bytes 7378560 | tf_op jit(solution)/shard_map/solve/pallas_call | solution.py:284
  55.3 19.7 %all_to_all.10.b_ref = bf16[64,2,640]{2,1,0:T(2,128)(2,1)S(1)} all-to-all(bf16[64,2,640]{2,1,0:T(2,128)(2,1)S(1)} %solve.1), channel_id=1, replica_groups=mesh['wave'=64,'lev'=8] {'wave'}, dimensions={0} | all-to-all | bytes 327680 | tf_op jit(solution)/shard_map/all_to_all | solution.py:318
  75.0 1.3 %unpack.1 = bf16[2,4,40,256]{3,2,1,0:T(8,128)(2,1)} custom-call(bf16[64,2,640]{2,1,0:T(2,128)(2,1)S(1)} %all_to_all.10.b_ref), custom_call_target="tpu_custom_call" | custom-call | flops 419758080 | bytes 1311744 | tf_op jit(solution)/shard_map/unpack/pallas_call | solution.py:232
  (6 shorter events, 0.0 us)
Async XLA Ops:
  0.0 26.5 %collective-permute-start = (bf16[320,1281]{1,0:T(8,128)(2,1)}, bf16[320,1281]{1,0:T(8,128)(2,1)}, u32[]{:S(2)}, u32[]{:S(2)}) collective-permute-start(bf16[320,1281]{1,0:T(8,128)(2,1)} %bitcast.4), channel_id=1, source_target_pairs={{0,2},{1,7},{2,4},{3,1},{4,6},{5,3},{6,0},{7,5},{8,10},{9,15},{10,... | collective-permute-start | bytes 2459528 | tf_op jit(solution)/shard_map/ppermute | solution.py:292
  8.1 35.6 %collective-permute-start.1 = (bf16[320,1281]{1,0:T(8,128)(2,1)}, bf16[320,1281]{1,0:T(8,128)(2,1)S(1)}, u32[]{:S(2)}, u32[]{:S(2)}) collective-permute-start(bf16[320,1281]{1,0:T(8,128)(2,1)} %get-tuple-element.21), channel_id=1, source_target_pairs={{0,6},{1,3},{2,0},{3,5},{4,2},{5,7},{6,4},{7,1},{8,14},{9,11},{10,... | collective-permute-start | bytes 2459528 | tf_op jit(solution)/shard_map/ppermute | solution.py:292
  10.0 16.5 %copy-start = (bf16[64,2,640]{2,1,0:T(2,128)(2,1)S(1)}, bf16[64,2,640]{2,1,0:T(2,128)(2,1)}, u32[]{:S(2)}) copy-start(bf16[64,2,640]{2,1,0:T(2,128)(2,1)} %get-tuple-element.19.token_ref) | copy-start | bytes 491524
  10.0 28.5 %all-to-all-start = ((bf16[64,2,640]{2,1,0:T(2,128)(2,1)}), bf16[64,2,640]{2,1,0:T(2,128)(2,1)S(1)}, u32[]{:S(2)}, u32[]{:S(2)}) async-start(bf16[64,2,640]{2,1,0:T(2,128)(2,1)} %get-tuple-element.19.token_ref), calls=%async_computation | async-start | bytes 327680 | tf_op jit(solution)/shard_map/all_to_all | solution.py:305
  26.5 10.5 %copy-start.4 = (s32[2560]{0:T(1024)S(1)}, s32[2560]{0:T(1024)}, u32[]{:S(2)}) copy-start(s32[2560]{0:T(1024)} %param.8) | copy-start | bytes 30724
  26.5 21.3 %collective-permute-start.5 = (bf16[320,1281]{1,0:T(8,128)(2,1)}, bf16[320,1281]{1,0:T(8,128)(2,1)S(1)}, u32[]{:S(2)}, u32[]{:S(2)}) collective-permute-start(bf16[320,1281]{1,0:T(8,128)(2,1)} %pass_on.3.refs_1_), channel_id=1, source_target_pairs={{0,2},{1,7},{2,4},{3,1},{4,6},{5,3},{6,0},{7,5},{8,10},{9,15},{10,... | collective-permute-start | bytes 2459528 | tf_op jit(solution)/shard_map/ppermute | solution.py:292
  31.1 19.9 %collective-permute-start.2 = (bf16[320,1281]{1,0:T(8,128)(2,1)}, bf16[320,1281]{1,0:T(8,128)(2,1)S(1)}, u32[]{:S(2)}, u32[]{:S(2)}) collective-permute-start(bf16[320,1281]{1,0:T(8,128)(2,1)} %get-tuple-element.21), channel_id=1, source_target_pairs={{0,1},{1,0},{2,3},{3,2},{4,5},{5,4},{6,7},{7,6},{8,9},{9,8},{10,11... | collective-permute-start | bytes 2459528 | tf_op jit(solution)/shard_map/ppermute | solution.py:296
  37.1 0.7 copy-start.1
  37.1 0.7 copy-start.2
  39.0 6.7 %copy-start.3 = (bf16[1,1281,320]{1,2,0:T(8,128)(2,1)S(1)}, bf16[1,1281,320]{1,2,0:T(8,128)(2,1)}, u32[]{:S(2)}) copy-start(bf16[1,1281,320]{1,2,0:T(8,128)(2,1)} %param.7) | copy-start | bytes 2459524
  39.0 12.0 %collective-permute-start.3 = (bf16[320,1281]{1,0:T(8,128)(2,1)}, bf16[320,1281]{1,0:T(8,128)(2,1)S(1)}, u32[]{:S(2)}, u32[]{:S(2)}) collective-permute-start(bf16[320,1281]{1,0:T(8,128)(2,1)} %pass_on.3.refs_1_), channel_id=1, source_target_pairs={{0,1},{1,0},{2,3},{3,2},{4,5},{5,4},{6,7},{7,6},{8,9},{9,8},{10,11... | collective-permute-start | bytes 2459528 | tf_op jit(solution)/shard_map/ppermute | solution.py:296
  43.7 7.3 %collective-permute-start.4 = (bf16[320,1281]{1,0:T(8,128)(2,1)S(1)}, bf16[320,1281]{1,0:T(8,128)(2,1)S(1)}, u32[]{:S(2)}, u32[]{:S(2)}) collective-permute-start(bf16[320,1281]{1,0:T(8,128)(2,1)S(1)} %pass_on.4.refs_2_), channel_id=1, source_target_pairs={{0,1},{1,0},{2,3},{3,2},{4,5},{5,4},{6,7},{7,6},{8,9},{9,8},{10,11... | collective-permute-start | bytes 2459528 | tf_op jit(solution)/shard_map/ppermute | solution.py:296
  47.8 5.2 %collective-permute-start.6 = (bf16[320,1281]{1,0:T(8,128)(2,1)S(1)}, bf16[320,1281]{1,0:T(8,128)(2,1)S(1)}, u32[]{:S(2)}, u32[]{:S(2)}) collective-permute-start(bf16[320,1281]{1,0:T(8,128)(2,1)S(1)} %pass_on.5.refs_3_), channel_id=1, source_target_pairs={{0,1},{1,0},{2,3},{3,2},{4,5},{5,4},{6,7},{7,6},{8,9},{9,8},{10,11... | collective-permute-start | bytes 2459528 | tf_op jit(solution)/shard_map/ppermute | solution.py:296

commit v9 on v8

--- a/solution.py
+++ b/solution.py
@@ -64,12 +64,13 @@
     put_tab = pltpu.make_async_copy(held_tab, copy_ref, sems.at[2])
     get_x.start()
     get_tab.start()
+    member, place = by_member(), by_place()
     get_x.wait()
     x = held_x[...].astype(jnp.float32).reshape(F * V * R, 4 * PAIRS).astype(jnp.bfloat16)
-    turned = mul(by_member(), x, NT).astype(jnp.bfloat16)
+    turned = mul(member, x, NT).astype(jnp.bfloat16)
     get_tab.wait()
     put_tab.start()
-    placed = mul(turned, by_place(), NN)
+    placed = mul(turned, place, NN)
     part = lane_part((PAIRS, STEPS * 128))
     out = placed[:PAIRS]
     for q in range(1, 4):
@@ -79,13 +80,13 @@
     put_tab.wait()
 
 
-def unpack_kernel(b_ref, o_ref):
+def unpack_kernel(b_ref, place_ref, member_ref, o_ref):
     b = jnp.swapaxes(b_ref[...].astype(jnp.float32), 0, 1)
     b = jnp.concatenate([b[0], b[1]], axis=1)
     part = lane_part((PAIRS, STEPS * 128))
     parts = [jnp.where(part == q, b, 0.0).astype(jnp.bfloat16) for q in range(4)]
-    turned = mul(by_place(), jnp.concatenate(parts, axis=0), NT).astype(jnp.bfloat16)
-    x = mul(turned, by_member(), NN)
+    turned = mul(place_ref[...], jnp.concatenate(parts, axis=0), NT).astype(jnp.bfloat16)
+    x = mul(turned, member_ref[...], NN)
     o_ref[...] = x.reshape(F, V, R, 4 * PAIRS).astype(jnp.bfloat16)
 
 
@@ -168,17 +169,19 @@
 
 
 def far_kernel(lev_ref, w_ref, raw_ref, *refs):
-    tabs, total_ref, turned = refs[:FARS], refs[FARS], refs[FARS + 1:]
+    tabs, total_ref, turned, made = refs[:FARS], refs[FARS], refs[FARS + 1:-3], refs[-3:]
     total_ref[...] = add_up(raw_ref[...], w_ref, slab_order(lev_ref[0])[NEARS:], tabs)
     for tab, turn in zip(tabs, turned):
         turn[...] = tab[...].T
+    for made_ref, make in zip(made, (by_place, by_member, place_rows)):
+        made_ref[...] = make()
 
 
 def pass_kernel(token_ref, tab_ref, same_ref):
     pass
 
 
-def solve_kernel(low_ref, lev_ref, level_ref, w_ref, scale_ref, raw_ref, *refs):
+def solve_kernel(low_ref, lev_ref, level_ref, w_ref, scale_ref, raw_ref, rows_ref, *refs):
     *tabs, o_ref, out_ref = refs
     low = low_ref[0]
     slabs = slab_order(lev_ref[0])
@@ -198,7 +201,7 @@
     for n, slab in enumerate(slabs):
         part = mul(expanded, tabs[n][...], NN if n < NEARS + FARS else NT)
         rows.append(jnp.where(members(scale_ref[slab]) > 0.0, part, 0.0).astype(jnp.bfloat16))
-    placed = mul(jnp.concatenate(rows, axis=0), place_rows(), NN)
+    placed = mul(jnp.concatenate(rows, axis=0), rows_ref[...], NN)
     for n, slab in enumerate(slabs):
         part = placed[n * COLS:(n + 1) * COLS]
         block = jnp.concatenate([part[:, g * 128:(g + 1) * 128] for g in range(4)], axis=0).T
@@ -228,10 +231,10 @@
         compiler_params=params(60), cost_estimate=cost(PAIRS * 4, SLAB, 2 * KP), name="pack")(x, tab)
 
 
-def unpack(b):
+def unpack(b, place, member):
     return pl.pallas_call(unpack_kernel, out_shape=jax.ShapeDtypeStruct((F, V, R, 4 * PAIRS), jnp.bfloat16),
-                          in_specs=[VMEM], out_specs=VMEM, compiler_params=params(12), cost_estimate=cost(SLAB, PAIRS * 4, 2 * KP),
-                          name="unpack")(b)
+                          in_specs=[VMEM] * 3, out_specs=VMEM, compiler_params=params(12),
+                          cost_estimate=cost(SLAB, PAIRS * 4, 2 * KP), name="unpack")(b, place, member)
 
 
 def coef(low, lev, gamma, beta, points):
@@ -261,6 +264,8 @@
 RAW = jax.ShapeDtypeStruct((COLS, KP), jnp.float32)
 
 
+MADE = tuple(jax.ShapeDtypeStruct(shape, jnp.bfloat16)
+             for shape in ((F * V * R, STEPS * 128), (4 * PAIRS, 4 * PAIRS), (SLAB, 512)))
 TURNED = jax.ShapeDtypeStruct((KP, SLAB), jnp.bfloat16)
 
 
@@ -275,17 +280,17 @@
 
 def far(lev, w, raw, tabs):
     return pl.pallas_call(
-        far_kernel, out_shape=(RAW,) + (TURNED,) * FARS, in_specs=[SMEM] + [VMEM] * (2 + FARS),
-        out_specs=(VMEM,) * (1 + FARS),
+        far_kernel, out_shape=(RAW,) + (TURNED,) * FARS + MADE, in_specs=[SMEM] + [VMEM] * (2 + FARS),
+        out_specs=(VMEM,) * (4 + FARS),
         compiler_params=params(8), cost_estimate=cost(COLS, 4 * SLAB, KP), name="far")(lev, w, raw, *tabs)
 
 
-def solve(low, lev, level, w, scale, raw, tabs):
-    return pl.pallas_call(
-        solve_kernel, out_shape=chunks(), in_specs=[SMEM] * 2 + [VMEM] * (4 + len(tabs)), out_specs=VMEM,
+def solve(low, lev, level, w, scale, raw, rows, tabs):
+    return pl.pallas_call(
+        solve_kernel, out_shape=chunks(), in_specs=[SMEM] * 2 + [VMEM] * (5 + len(tabs)), out_specs=VMEM,
         scratch_shapes=[pltpu.VMEM((2, PAIRS, HALF), jnp.float32)],
         compiler_params=params(12), cost_estimate=cost(COLS, 9 * SLAB, KP),
-        name="solve")(low, lev, level, w, scale, raw, *tabs)
+        name="solve")(low, lev, level, w, scale, raw, rows, *tabs)
 
 
 def along_x(array, step):
@@ -312,11 +317,11 @@
     raw, *tabs = near(lev, weighted, [own, first, second])
     third = pass_on(raw, third)
     last = other_core(third)
-    raw, *more = far(lev, weighted, raw, cores + [third])
+    raw, *more, place, member, rows = far(lev, weighted, raw, cores + [third])
     tabs += more + [last]
-    result = solve(pair_low, lev, level, weighted, scale, raw, tabs)
+    result = solve(pair_low, lev, level, weighted, scale, raw, rows, tabs)
     back = lax.all_to_all(result, "wave", split_axis=0, concat_axis=0, tiled=True)
-    return unpack(back)
+    return unpack(back, place, member)
 
 
 def solution(mesh):

time: 77 us -> 77 us (level)
  transfers between devices with their start and end apart: 8 -> 8, of which waited for: 1 -> 1; matrix products, arithmetic and copies ran while one was open for 0% -> 0% of each run, Pallas kernels for 10% -> 11%
where the time goes in v9:
time: 77 us; the launch traced here: 76.3 us
  starting transfers between devices  43.2 us (56%)
  blocking collectives  19.7 us (26%)
  Pallas kernels  11.5 us (15%)
  between operations  0.91 us (1%)
    all_to_all x1, blocking collectives, local(): lax.all_to_all(result, 'wave', split_axis=0, concat_axis=0, tiled=True)  19.7 us
    all_to_all x1, starting transfers between devices, local(): lax.all_to_all(sent, 'wave', split_axis=0, concat_axis=0, tiled=True)  16.5 us
    ppermute x4, starting transfers between devices, other_core(): return lax.ppermute(array, 'lev', [(d, d ^ 1) for d in range(SLABS)])  15 us
    ppermute x3, starting transfers between devices, along_x(): lax.ppermute(array, 'lev', [(d, (d + 2 * step * (1 - 2 * (d % 2))) % SLAB...  11.7 us
    pallas_call x1, Pallas kernels, pack(): pl.pallas_call(pack_kernel, out_shape=(chunks(), like(tab)), in_specs=[AN...  2.88 us
    pallas_call x1, Pallas kernels, solve(): pl.pallas_call(solve_kernel, out_shape=chunks(), in_specs=[SMEM] * 2 + [V...  2.24 us
    pallas_call x1, Pallas kernels, near(): pl.pallas_call(near_kernel, out_shape=(RAW,) + (TURNED,) * NEARS, in_spec...  2.15 us
    pallas_call x1, Pallas kernels, far(): pl.pallas_call(far_kernel, out_shape=(RAW,) + (TURNED,) * FARS + MADE, in...  1.79 us
  transfers between devices with their start and end apart: 8, of which 1 were waited for; matrix products, arithmetic and copies ran while one was open for 0% of the time, Pallas kernels for 11%

profile of v9, /device:TPU:1, one launch (start us, length us, event | category | flops | bytes accessed | tf_op | source)
XLA Modules:
  0.0 76.3 jit_solution(5009555241425791894)
XLA Ops:
  0.0 5.2 %collective-permute-start = (bf16[320,1281]{1,0:T(8,128)(2,1)}, bf16[320,1281]{1,0:T(8,128)(2,1)}, u32[]{:S(2)}, u32[]{:S(2)}) collective-permute-start(bf16[320,1281]{1,0:T(8,128)(2,1)} %bitcast.4), channel_id=1, source_target_pairs={{0,2},{1,7},{2,4},{3,1},{4,6},{5,3},{6,0},{7,5},{8,10},{9,15},{10,... | collective-permute-start | bytes 2459528 | tf_op jit(solution)/shard_map/ppermute | solution.py:297
  5.2 2.9 %pack.1 = (bf16[64,2,640]{2,1,0:T(2,128)(2,1)}, bf16[320,1281]{1,0:T(8,128)(2,1)}) custom-call(bf16[2,4,40,256]{3,2,1,0:T(8,128)(2,1)} %x_ref.1, bf16[320,1281]{1,0:T(8,128)(2,1)} %bitcast.5), custom_call_target="tpu_custom_call" | custom-call | flops 419758080 | bytes 1639680 | tf_op jit(solution)/shard_map/pack/pallas_call | solution.py:228
  8.1 1.9 %collective-permute-start.1 = (bf16[320,1281]{1,0:T(8,128)(2,1)}, bf16[320,1281]{1,0:T(8,128)(2,1)S(1)}, u32[]{:S(2)}, u32[]{:S(2)}) collective-permute-start(bf16[320,1281]{1,0:T(8,128)(2,1)} %get-tuple-element.24), channel_id=1, source_target_pairs={{0,6},{1,3},{2,0},{3,5},{4,2},{5,7},{6,4},{7,1},{8,14},{9,11},{10,... | collective-permute-start | bytes 2459528 | tf_op jit(solution)/shard_map/ppermute | solution.py:297
  10.0 0.0 copy-start
  10.0 16.5 %all-to-all-start = ((bf16[64,2,640]{2,1,0:T(2,128)(2,1)}), bf16[64,2,640]{2,1,0:T(2,128)(2,1)S(1)}, u32[]{:S(2)}, u32[]{:S(2)}) async-start(bf16[64,2,640]{2,1,0:T(2,128)(2,1)} %get-tuple-element.22.token_ref), calls=%async_computation | async-start | bytes 327680 | tf_op jit(solution)/shard_map/all_to_all | solution.py:310
  26.5 0.0 collective-permute-done.tab_ref
  26.5 0.0 copy-start.4
  26.5 4.6 %collective-permute-start.5 = (bf16[320,1281]{1,0:T(8,128)(2,1)}, bf16[320,1281]{1,0:T(8,128)(2,1)S(1)}, u32[]{:S(2)}, u32[]{:S(2)}) collective-permute-start(bf16[320,1281]{1,0:T(8,128)(2,1)} %pass_on.3.refs_1_), channel_id=1, source_target_pairs={{0,2},{1,7},{2,4},{3,1},{4,6},{5,3},{6,0},{7,5},{8,10},{9,15},{10,... | collective-permute-start | bytes 2459528 | tf_op jit(solution)/shard_map/ppermute | solution.py:297
  31.1 5.3 %collective-permute-start.2 = (bf16[320,1281]{1,0:T(8,128)(2,1)}, bf16[320,1281]{1,0:T(8,128)(2,1)S(1)}, u32[]{:S(2)}, u32[]{:S(2)}) collective-permute-start(bf16[320,1281]{1,0:T(8,128)(2,1)} %get-tuple-element.24), channel_id=1, source_target_pairs={{0,1},{1,0},{2,3},{3,2},{4,5},{5,4},{6,7},{7,6},{8,9},{9,8},{10,11... | collective-permute-start | bytes 2459528 | tf_op jit(solution)/shard_map/ppermute | solution.py:301
  37.1 0.0 copy-start.1
  37.1 0.0 copy-start.2
  37.1 0.6 copy-done.1
  37.7 0.0 copy-done.2
  37.7 0.8 coef.1
  38.5 0.0 all-to-all-done.y_ref
  38.5 0.4 weigh.1.w_ref
  39.0 0.0 copy-start.3
  39.0 4.7 %collective-permute-start.3 = (bf16[320,1281]{1,0:T(8,128)(2,1)}, bf16[320,1281]{1,0:T(8,128)(2,1)S(1)}, u32[]{:S(2)}, u32[]{:S(2)}) collective-permute-start(bf16[320,1281]{1,0:T(8,128)(2,1)} %pass_on.3.refs_1_), channel_id=1, source_target_pairs={{0,1},{1,0},{2,3},{3,2},{4,5},{5,4},{6,7},{7,6},{8,9},{9,8},{10,11... | collective-permute-start | bytes 2459528 | tf_op jit(solution)/shard_map/ppermute | solution.py:301
  43.7 0.0 collective-permute-done.1.tab_ref
  43.7 1.9 %collective-permute-start.4 = (bf16[320,1281]{1,0:T(8,128)(2,1)S(1)}, bf16[320,1281]{1,0:T(8,128)(2,1)S(1)}, u32[]{:S(2)}, u32[]{:S(2)}) collective-permute-start(bf16[320,1281]{1,0:T(8,128)(2,1)S(1)} %pass_on.4.refs_2_), channel_id=1, source_target_pairs={{0,1},{1,0},{2,3},{3,2},{4,5},{5,4},{6,7},{7,6},{8,9},{9,8},{10,11... | collective-permute-start | bytes 2459528 | tf_op jit(solution)/shard_map/ppermute | solution.py:301
  45.6 0.0 copy-done.3
  45.6 2.1 %near.1 = (f32[32,1281]{1,0:T(8,128)S(1)}, bf16[1281,320]{1,0:T(8,128)(2,1)S(1)}, bf16[1281,320]{1,0:T(8,128)(2,1)S(1)}, bf16[1281,320]{1,0:T(8,128)(2,1)S(1)}) custom-call(s32[1]{0:T(128)} %bitcast.lev_ref, bf16[8,32,320]{2,1,0:T(8,128)(2,1)S(1)} %weigh.1.w_ref, bf16[320,1281]{1,0:T(8,128)(2,1)S(1)} %bitcast.6, bf16[320,1281]{1,0:T(8,128)(2,1)} %pass_on.3.refs_1_, ...), custom_call_target="tpu_custom_call" | custom-call | flops 7500000256 | tf_op jit(solution)/shard_map/near/pallas_call | solution.py:273
  47.8 0.0 collective-permute-done.5.tab_ref
  47.8 3.2 %collective-permute-start.6 = (bf16[320,1281]{1,0:T(8,128)(2,1)S(1)}, bf16[320,1281]{1,0:T(8,128)(2,1)S(1)}, u32[]{:S(2)}, u32[]{:S(2)}) collective-permute-start(bf16[320,1281]{1,0:T(8,128)(2,1)S(1)} %pass_on.5.refs_3_), channel_id=1, source_target_pairs={{0,1},{1,0},{2,3},{3,2},{4,5},{5,4},{6,7},{7,6},{8,9},{9,8},{10,11... | collective-permute-start | bytes 2459528 | tf_op jit(solution)/shard_map/ppermute | solution.py:301
  51.0 0.0 collective-permute-done.2.refs_0_
  51.0 0.0 collective-permute-done.3.refs_1_
  51.0 0.0 collective-permute-done.4.refs_2_
  51.0 1.8 %far.1 = (f32[32,1281]{1,0:T(8,128)S(1)}, bf16[1281,320]{1,0:T(8,128)(2,1)S(1)}, bf16[1281,320]{1,0:T(8,128)(2,1)S(1)}, bf16[1281,320]{1,0:T(8,128)(2,1)S(1)}, b...) custom-call(s32[1]{0:T(128)} %bitcast.lev_ref, ...), custom_call_target="tpu_custom_call" | custom-call | flops 839516160 | bytes 3279360 | tf_op jit(solution)/shard_map/far/pallas_call | solution.py:282
  52.8 0.2 collective-permute-done.6.refs_7_
  53.0 2.2 %solve.1 = bf16[64,2,640]{2,1,0:T(2,128)(2,1)S(1)} custom-call(s32[1]{0:T(128)S(6)} %copy.13.low_ref, s32[1]{0:T(128)} %bitcast.lev_ref, f32[2,8,128]{2,1,0:T(8,128)S(1)} %get-tuple-element.21.level_ref, bf16[8,32,320]{2,1,0:T(8,128)(2,1)S(1)} %weigh.1.w_ref, f32[8,2,320]{2,1,0:T(2,128)S(1)} %get-tuple-element.23.scale_ref, ...), custom_call_target="tpu_custom_call" | custom-call | flops 1888911360 | bytes 7378560 | tf_op jit(solution)/shard_map/solve/pallas_call | solution.py:289
  55.3 19.7 %all_to_all.10.b_ref = bf16[64,2,640]{2,1,0:T(2,128)(2,1)S(1)} all-to-all(bf16[64,2,640]{2,1,0:T(2,128)(2,1)S(1)} %solve.1), channel_id=1, replica_groups=mesh['wave'=64,'lev'=8] {'wave'}, dimensions={0} | all-to-all | bytes 327680 | tf_op jit(solution)/shard_map/all_to_all | solution.py:323
  75.0 1.3 %unpack.1 = bf16[2,4,40,256]{3,2,1,0:T(8,128)(2,1)} custom-call(bf16[64,2,640]{2,1,0:T(2,128)(2,1)S(1)} %all_to_all.10.b_ref, bf16[320,1280]{1,0:T(8,128)(2,1)S(1)} %get-tuple-element.35.place_ref, bf16[256,256]{1,0:T(8,128)(2,1)S(1)} %get-tuple-element.36.member_ref), custom_call_target="tpu_custom_call" | custom-call | flops 419758080 | bytes 1311744 | tf_op jit(solution)/shard_map/unpack/pallas_call | solution.py:235
  (6 shorter events, 0.0 us)
Async XLA Ops:
  0.0 26.5 %collective-permute-start = (bf16[320,1281]{1,0:T(8,128)(2,1)}, bf16[320,1281]{1,0:T(8,128)(2,1)}, u32[]{:S(2)}, u32[]{:S(2)}) collective-permute-start(bf16[320,1281]{1,0:T(8,128)(2,1)} %bitcast.4), channel_id=1, source_target_pairs={{0,2},{1,7},{2,4},{3,1},{4,6},{5,3},{6,0},{7,5},{8,10},{9,15},{10,... | collective-permute-start | bytes 2459528 | tf_op jit(solution)/shard_map/ppermute | solution.py:297
  8.1 35.6 %collective-permute-start.1 = (bf16[320,1281]{1,0:T(8,128)(2,1)}, bf16[320,1281]{1,0:T(8,128)(2,1)S(1)}, u32[]{:S(2)}, u32[]{:S(2)}) collective-permute-start(bf16[320,1281]{1,0:T(8,128)(2,1)} %get-tuple-element.24), channel_id=1, source_target_pairs={{0,6},{1,3},{2,0},{3,5},{4,2},{5,7},{6,4},{7,1},{8,14},{9,11},{10,... | collective-permute-start | bytes 2459528 | tf_op jit(solution)/shard_map/ppermute | solution.py:297
  10.0 16.5 %copy-start = (bf16[64,2,640]{2,1,0:T(2,128)(2,1)S(1)}, bf16[64,2,640]{2,1,0:T(2,128)(2,1)}, u32[]{:S(2)}) copy-start(bf16[64,2,640]{2,1,0:T(2,128)(2,1)} %get-tuple-element.22.token_ref) | copy-start | bytes 491524
  10.0 28.5 %all-to-all-start = ((bf16[64,2,640]{2,1,0:T(2,128)(2,1)}), bf16[64,2,640]{2,1,0:T(2,128)(2,1)S(1)}, u32[]{:S(2)}, u32[]{:S(2)}) async-start(bf16[64,2,640]{2,1,0:T(2,128)(2,1)} %get-tuple-element.22.token_ref), calls=%async_computation | async-start | bytes 327680 | tf_op jit(solution)/shard_map/all_to_all | solution.py:310
  26.5 10.5 %copy-start.4 = (s32[2560]{0:T(1024)S(1)}, s32[2560]{0:T(1024)}, u32[]{:S(2)}) copy-start(s32[2560]{0:T(1024)} %param.8) | copy-start | bytes 30724
  26.5 21.3 %collective-permute-start.5 = (bf16[320,1281]{1,0:T(8,128)(2,1)}, bf16[320,1281]{1,0:T(8,128)(2,1)S(1)}, u32[]{:S(2)}, u32[]{:S(2)}) collective-permute-start(bf16[320,1281]{1,0:T(8,128)(2,1)} %pass_on.3.refs_1_), channel_id=1, source_target_pairs={{0,2},{1,7},{2,4},{3,1},{4,6},{5,3},{6,0},{7,5},{8,10},{9,15},{10,... | collective-permute-start | bytes 2459528 | tf_op jit(solution)/shard_map/ppermute | solution.py:297
  31.1 19.9 %collective-permute-start.2 = (bf16[320,1281]{1,0:T(8,128)(2,1)}, bf16[320,1281]{1,0:T(8,128)(2,1)S(1)}, u32[]{:S(2)}, u32[]{:S(2)}) collective-permute-start(bf16[320,1281]{1,0:T(8,128)(2,1)} %get-tuple-element.24), channel_id=1, source_target_pairs={{0,1},{1,0},{2,3},{3,2},{4,5},{5,4},{6,7},{7,6},{8,9},{9,8},{10,11... | collective-permute-start | bytes 2459528 | tf_op jit(solution)/shard_map/ppermute | solution.py:301
  37.1 0.7 copy-start.1
  37.1 0.7 copy-start.2
  39.0 6.7 %copy-start.3 = (bf16[1,1281,320]{1,2,0:T(8,128)(2,1)S(1)}, bf16[1,1281,320]{1,2,0:T(8,128)(2,1)}, u32[]{:S(2)}) copy-start(bf16[1,1281,320]{1,2,0:T(8,128)(2,1)} %param.7) | copy-start | bytes 2459524
  39.0 12.0 %collective-permute-start.3 = (bf16[320,1281]{1,0:T(8,128)(2,1)}, bf16[320,1281]{1,0:T(8,128)(2,1)S(1)}, u32[]{:S(2)}, u32[]{:S(2)}) collective-permute-start(bf16[320,1281]{1,0:T(8,128)(2,1)} %pass_on.3.refs_1_), channel_id=1, source_target_pairs={{0,1},{1,0},{2,3},{3,2},{4,5},{5,4},{6,7},{7,6},{8,9},{9,8},{10,11... | collective-permute-start | bytes 2459528 | tf_op jit(solution)/shard_map/ppermute | solution.py:301
  43.7 7.3 %collective-permute-start.4 = (bf16[320,1281]{1,0:T(8,128)(2,1)S(1)}, bf16[320,1281]{1,0:T(8,128)(2,1)S(1)}, u32[]{:S(2)}, u32[]{:S(2)}) collective-permute-start(bf16[320,1281]{1,0:T(8,128)(2,1)S(1)} %pass_on.4.refs_2_), channel_id=1, source_target_pairs={{0,1},{1,0},{2,3},{3,2},{4,5},{5,4},{6,7},{7,6},{8,9},{9,8},{10,11... | collective-permute-start | bytes 2459528 | tf_op jit(solution)/shard_map/ppermute | solution.py:301
  47.8 5.2 %collective-permute-start.6 = (bf16[320,1281]{1,0:T(8,128)(2,1)S(1)}, bf16[320,1281]{1,0:T(8,128)(2,1)S(1)}, u32[]{:S(2)}, u32[]{:S(2)}) collective-permute-start(bf16[320,1281]{1,0:T(8,128)(2,1)S(1)} %pass_on.5.refs_3_), channel_id=1, source_target_pairs={{0,1},{1,0},{2,3},{3,2},{4,5},{5,4},{6,7},{7,6},{8,9},{9,8},{10,11... | collective-permute-start | bytes 2459528 | tf_op jit(solution)/shard_map/ppermute | solution.py:301

commit v10 on v5

--- a/solution.py
+++ b/solution.py
@@ -105,7 +105,7 @@
     return (iota((4 * COLS, SLAB), 0) >> 5) == (iota((4 * COLS, SLAB), 1) & 3)
 
 
-def coef_kernel(low_ref, lev_ref, gamma_ref, beta_ref, points_ref, token_ref, scale_ref, level_ref):
+def coef_kernel(low_ref, lev_ref, gamma_ref, beta_ref, points_ref, scale_ref, level_ref):
     low = low_ref[0]
     points = jnp.concatenate([points_ref[:, s * SLAB:(s + 1) * SLAB] for s in range(SLABS)], axis=0)
     pts = points.astype(jnp.float32)
@@ -235,12 +235,12 @@
                           name="unpack")(b)
 
 
-def coef(low, lev, gamma, beta, points, token):
+def coef(low, lev, gamma, beta, points):
     return pl.pallas_call(
         coef_kernel, out_shape=(jax.ShapeDtypeStruct((SLABS, 2, SLAB), jnp.float32),
                                 jax.ShapeDtypeStruct((2, SLABS, 128), jnp.float32)),
-        in_specs=[SMEM] * 4 + [VMEM, ANY], out_specs=(VMEM,) * 2, compiler_params=params(8),
-        name="coef")(low, lev, gamma, beta, points, token)
+        in_specs=[SMEM] * 4 + [VMEM], out_specs=(VMEM,) * 2, compiler_params=params(8),
+        name="coef")(low, lev, gamma, beta, points)
 
 
 def like(tab):
@@ -304,8 +304,8 @@
     sent, copied = pack(fourier_in, own)
     second = along_x(copied, -1)
     moved = lax.all_to_all(sent, "wave", split_axis=0, concat_axis=0, tiled=True)
-    scale, level = coef(pair_low, lev, gamma, beta, points.reshape(1, NLAT), sent)
-    first = pass_on(level, first)
+    scale, level = coef(pair_low, lev, gamma, beta, points.reshape(1, NLAT))
+    first = pass_on(sent, first)
     third = along_x(first, 1)
     second = pass_on(sent, second)
     cores = [other_core(first), other_core(second)]

time: 78.8 us -> 76.8 us (0.975)
  blocking collectives: 19.5 us -> 17.4 us
    all_to_all x1, blocking collectives: 19.5 us -> 17.4 us  [local(): lax.all_to_all(result, 'wave', split_axis=0, concat_axis=0, tiled=True)]
where the time goes in v10:
time: 76.8 us; the launch traced here: 76.1 us
  starting transfers between devices  39.2 us (51%)
  blocking collectives  17.4 us (23%)
  Pallas kernels  10.6 us (14%)
  waiting for transfers between devices  6.21 us (8%)
  local copies, waits for them, and re-layouts  1.83 us (2%)
  between operations  0.89 us (1%)
    all_to_all x1, blocking collectives, local(): lax.all_to_all(result, 'wave', split_axis=0, concat_axis=0, tiled=True)  17.4 us
    all_to_all x1, starting transfers between devices, local(): lax.all_to_all(sent, 'wave', split_axis=0, concat_axis=0, tiled=True)  16.4 us
    ppermute x3, starting transfers between devices, along_x(): lax.ppermute(array, 'lev', [(d, (d + 2 * step * (1 - 2 * (d % 2))) % SLAB...  11.7 us
    ppermute x4, starting transfers between devices, other_core(): return lax.ppermute(array, 'lev', [(d, d ^ 1) for d in range(SLABS)])  11.1 us
    all_to_all x1, waiting for transfers between devices, local(): lax.all_to_all(sent, 'wave', split_axis=0, concat_axis=0, tiled=True)  5.04 us
    pallas_call x1, Pallas kernels, pack(): pl.pallas_call(pack_kernel, out_shape=(chunks(), like(tab)), in_specs=[AN...  2.88 us
    pallas_call x1, Pallas kernels, solve(): pl.pallas_call(solve_kernel, out_shape=chunks(), in_specs=[SMEM] * 2 + [V...  2.24 us
    unnamed x10, local copies, waits for them, and re-layouts  1.82 us
  transfers between devices with their start and end apart: 8, of which 3 were waited for; matrix products, arithmetic and copies ran while one was open for 0% of the time, Pallas kernels for 9%

profile of v10, /device:TPU:1, one launch (start us, length us, event | category | flops | bytes accessed | tf_op | source)
XLA Modules:
  0.0 76.1 jit_solution(17856405737906479896)
XLA Ops:
  0.0 5.2 %collective-permute-start = (bf16[320,1281]{1,0:T(8,128)(2,1)}, bf16[320,1281]{1,0:T(8,128)(2,1)S(1)}, u32[]{:S(2)}, u32[]{:S(2)}) collective-permute-start(bf16[320,1281]{1,0:T(8,128)(2,1)} %bitcast.4), channel_id=1, source_target_pairs={{0,2},{1,7},{2,4},{3,1},{4,6},{5,3},{6,0},{7,5},{8,10},{9,15},{10,... | collective-permute-start | bytes 2459528 | tf_op jit(solution)/shard_map/ppermute | solution.py:293
  5.2 2.9 %pack.1 = (bf16[64,2,640]{2,1,0:T(2,128)(2,1)}, bf16[320,1281]{1,0:T(8,128)(2,1)}) custom-call(bf16[2,4,40,256]{3,2,1,0:T(8,128)(2,1)} %x_ref.1, bf16[320,1281]{1,0:T(8,128)(2,1)} %bitcast.5), custom_call_target="tpu_custom_call" | custom-call | flops 419758080 | bytes 1639680 | tf_op jit(solution)/shard_map/pack/pallas_call | solution.py:226
  8.1 1.9 %collective-permute-start.1 = (bf16[320,1281]{1,0:T(8,128)(2,1)}, bf16[320,1281]{1,0:T(8,128)(2,1)S(1)}, u32[]{:S(2)}, u32[]{:S(2)}) collective-permute-start(bf16[320,1281]{1,0:T(8,128)(2,1)} %get-tuple-element.22), channel_id=1, source_target_pairs={{0,6},{1,3},{2,0},{3,5},{4,2},{5,7},{6,4},{7,1},{8,14},{9,11},{10,... | collective-permute-start | bytes 2459528 | tf_op jit(solution)/shard_map/ppermute | solution.py:293
  10.0 0.0 copy-start
  10.0 16.4 %all-to-all-start = ((bf16[64,2,640]{2,1,0:T(2,128)(2,1)}), bf16[64,2,640]{2,1,0:T(2,128)(2,1)S(1)}, u32[]{:S(2)}, u32[]{:S(2)}) async-start(bf16[64,2,640]{2,1,0:T(2,128)(2,1)} %get-tuple-element.20.token_ref), calls=%async_computation | async-start | bytes 327680 | tf_op jit(solution)/shard_map/all_to_all | solution.py:306
  26.5 0.0 collective-permute-done.tab_ref
  26.5 0.0 copy-start.4
  26.5 4.6 %collective-permute-start.5 = (bf16[320,1281]{1,0:T(8,128)(2,1)S(1)}, bf16[320,1281]{1,0:T(8,128)(2,1)S(1)}, u32[]{:S(2)}, u32[]{:S(2)}) collective-permute-start(bf16[320,1281]{1,0:T(8,128)(2,1)S(1)} %pass_on.3.refs_1_), channel_id=1, source_target_pairs={{0,2},{1,7},{2,4},{3,1},{4,6},{5,3},{6,0},{7,5},{8,10},{9,15},{10,... | collective-permute-start | bytes 2459528 | tf_op jit(solution)/shard_map/ppermute | solution.py:293
  31.8 0.0 copy-start.1
  31.8 0.0 copy-start.2
  31.8 0.6 copy-done.1
  32.5 0.0 copy-done.2
  32.5 0.8 coef.1
  33.2 5.0 %all-to-all-done.y_ref = bf16[64,2,640]{2,1,0:T(2,128)(2,1)S(1)} async-done(((bf16[64,2,640]{2,1,0:T(2,128)(2,1)}), bf16[64,2,640]{2,1,0:T(2,128)(2,1)S(1)}, u32[]{:S(2)}, u32[]{:S(2)}) %all-to-all-start) | async-done | bytes 163872 | tf_op jit(solution)/shard_map/all_to_all | solution.py:306
  38.3 0.4 weigh.1.w_ref
  38.7 0.0 copy-start.3
  38.7 0.0 collective-permute-done.1.tab_ref
  38.8 1.1 %copy-done.3 = bf16[1,1281,320]{1,2,0:T(8,128)(2,1)S(1)} copy-done((bf16[1,1281,320]{1,2,0:T(8,128)(2,1)S(1)}, bf16[1,1281,320]{1,2,0:T(8,128)(2,1)}, u32[]{:S(2)}) %copy-start.3) | copy-done | bytes 819864
  39.9 1.7 %near.1 = (f32[32,1281]{1,0:T(8,128)S(1)}, bf16[1281,320]{1,0:T(8,128)(2,1)S(1)}, bf16[1281,320]{1,0:T(8,128)(2,1)S(1)}, bf16[1281,320]{1,0:T(8,128)(2,1)S(1)}, bf16[320,1281]{1,0:T(8,128)(2,1)S(1)}) custom-call(s32[1]{0:T(128)} %bitcast.lev_ref, bf16[8,32,320]{2,1,0:T(8,128)(2,1)S(1)} %weigh.1.w_ref, bf16[320,1281]{1,0:T(8,128)(2,1)S(1)} %bitcast.6, ...), custom_call_target="tpu_custom_call" | custom-call | flops 7299999744 | tf_op jit(solution)/shard_map/near/pallas_call | solution.py:269
  41.6 4.8 %collective-permute-start.2 = (bf16[320,1281]{1,0:T(8,128)(2,1)S(1)}, bf16[320,1281]{1,0:T(8,128)(2,1)S(1)}, u32[]{:S(2)}, u32[]{:S(2)}) collective-permute-start(bf16[320,1281]{1,0:T(8,128)(2,1)S(1)} %get-tuple-element.24), channel_id=1, source_target_pairs={{0,1},{1,0},{2,3},{3,2},{4,5},{5,4},{6,7},{7,6},{8,9},{9,8},{10,11... | collective-permute-start | bytes 2459528 | tf_op jit(solution)/shard_map/ppermute | solution.py:297
  46.4 1.9 %collective-permute-start.3 = (bf16[320,1281]{1,0:T(8,128)(2,1)S(1)}, bf16[320,1281]{1,0:T(8,128)(2,1)S(1)}, u32[]{:S(2)}, u32[]{:S(2)}) collective-permute-start(bf16[320,1281]{1,0:T(8,128)(2,1)S(1)} %pass_on.3.refs_1_), channel_id=1, source_target_pairs={{0,1},{1,0},{2,3},{3,2},{4,5},{5,4},{6,7},{7,6},{8,9},{9,8},{10,11... | collective-permute-start | bytes 2459528 | tf_op jit(solution)/shard_map/ppermute | solution.py:297
  48.4 2.4 %collective-permute-start.4 = (bf16[320,1281]{1,0:T(8,128)(2,1)S(1)}, bf16[320,1281]{1,0:T(8,128)(2,1)S(1)}, u32[]{:S(2)}, u32[]{:S(2)}) collective-permute-start(bf16[320,1281]{1,0:T(8,128)(2,1)S(1)} %pass_on.4.refs_2_), channel_id=1, source_target_pairs={{0,1},{1,0},{2,3},{3,2},{4,5},{5,4},{6,7},{7,6},{8,9},{9,8},{10,11... | collective-permute-start | bytes 2459528 | tf_op jit(solution)/shard_map/ppermute | solution.py:297
  50.8 0.0 collective-permute-done.5.tab_ref
  50.8 1.9 %collective-permute-start.6 = (bf16[320,1281]{1,0:T(8,128)(2,1)S(1)}, bf16[320,1281]{1,0:T(8,128)(2,1)S(1)}, u32[]{:S(2)}, u32[]{:S(2)}) collective-permute-start(bf16[320,1281]{1,0:T(8,128)(2,1)S(1)} %pass_on.5.refs_3_), channel_id=1, source_target_pairs={{0,1},{1,0},{2,3},{3,2},{4,5},{5,4},{6,7},{7,6},{8,9},{9,8},{10,11... | collective-permute-start | bytes 2459528 | tf_op jit(solution)/shard_map/ppermute | solution.py:297
  52.7 0.0 collective-permute-done.2.refs_0_
  52.7 0.0 collective-permute-done.3.refs_1_
  52.7 0.1 collective-permute-done.4.refs_2_
  52.8 1.2 %far.1 = (f32[32,1281]{1,0:T(8,128)S(1)}, bf16[1281,320]{1,0:T(8,128)(2,1)S(1)}, bf16[1281,320]{1,0:T(8,128)(2,1)S(1)}, bf16[1281,320]{1,0:T(8,128)(2,1)S(1)}, bf16[1281,320]{1,0:T(8,128)(2,1)S(1)}) custom-call(s32[1]{0:T(128)} %bitcast.lev_ref, bf16[8,32,320]{2,1,0:T(8,128)(2,1)S(1)} %weigh.1.w_ref, f32[32,1281]{1,0:T(8,128)S(1)} %get-tuple-element.23.token_ref.raw_ref, ...), custom_call_target="tpu_custom_call" | custom-call | flops 839516160 | bytes 3279360 | tf_op jit(solution)/shard_map/far/pallas_call | solution.py:278
  54.1 1.1 %collective-permute-done.6.refs_7_ = bf16[320,1281]{1,0:T(8,128)(2,1)S(1)} collective-permute-done((bf16[320,1281]{1,0:T(8,128)(2,1)S(1)}, bf16[320,1281]{1,0:T(8,128)(2,1)S(1)}, u32[]{:S(2)}, u32[]{:S(2)}) %collective-permute-start.6) | collective-permute-done | bytes 819872 | tf_op jit(solution)/shard_map/ppermute | solution.py:297
  55.1 2.2 %solve.1 = bf16[64,2,640]{2,1,0:T(2,128)(2,1)S(1)} custom-call(s32[1]{0:T(128)S(6)} %copy.13.low_ref, s32[1]{0:T(128)} %bitcast.lev_ref, f32[2,8,128]{2,1,0:T(8,128)S(1)} %get-tuple-element.19.level_ref, bf16[8,32,320]{2,1,0:T(8,128)(2,1)S(1)} %weigh.1.w_ref, f32[8,2,320]{2,1,0:T(2,128)S(1)} %get-tuple-element.21.scale_ref, ...), custom_call_target="tpu_custom_call" | custom-call | flops 1888911360 | bytes 7378560 | tf_op jit(solution)/shard_map/solve/pallas_call | solution.py:285
  57.4 17.4 %all_to_all.10.b_ref = bf16[64,2,640]{2,1,0:T(2,128)(2,1)S(1)} all-to-all(bf16[64,2,640]{2,1,0:T(2,128)(2,1)S(1)} %solve.1), channel_id=1, replica_groups=mesh['wave'=64,'lev'=8] {'wave'}, dimensions={0} | all-to-all | bytes 327680 | tf_op jit(solution)/shard_map/all_to_all | solution.py:319
  74.8 1.3 %unpack.1 = bf16[2,4,40,256]{3,2,1,0:T(8,128)(2,1)} custom-call(bf16[64,2,640]{2,1,0:T(2,128)(2,1)S(1)} %all_to_all.10.b_ref), custom_call_target="tpu_custom_call" | custom-call | flops 419758080 | bytes 1311744 | tf_op jit(solution)/shard_map/unpack/pallas_call | solution.py:233
  (6 shorter events, 0.0 us)
Async XLA Ops:
  0.0 26.5 %collective-permute-start = (bf16[320,1281]{1,0:T(8,128)(2,1)}, bf16[320,1281]{1,0:T(8,128)(2,1)S(1)}, u32[]{:S(2)}, u32[]{:S(2)}) collective-permute-start(bf16[320,1281]{1,0:T(8,128)(2,1)} %bitcast.4), channel_id=1, source_target_pairs={{0,2},{1,7},{2,4},{3,1},{4,6},{5,3},{6,0},{7,5},{8,10},{9,15},{10,... | collective-permute-start | bytes 2459528 | tf_op jit(solution)/shard_map/ppermute | solution.py:293
  8.1 30.6 %collective-permute-start.1 = (bf16[320,1281]{1,0:T(8,128)(2,1)}, bf16[320,1281]{1,0:T(8,128)(2,1)S(1)}, u32[]{:S(2)}, u32[]{:S(2)}) collective-permute-start(bf16[320,1281]{1,0:T(8,128)(2,1)} %get-tuple-element.22), channel_id=1, source_target_pairs={{0,6},{1,3},{2,0},{3,5},{4,2},{5,7},{6,4},{7,1},{8,14},{9,11},{10,... | collective-permute-start | bytes 2459528 | tf_op jit(solution)/shard_map/ppermute | solution.py:293
  10.0 16.5 %copy-start = (bf16[64,2,640]{2,1,0:T(2,128)(2,1)S(1)}, bf16[64,2,640]{2,1,0:T(2,128)(2,1)}, u32[]{:S(2)}) copy-start(bf16[64,2,640]{2,1,0:T(2,128)(2,1)} %get-tuple-element.20.token_ref) | copy-start | bytes 491524
  10.0 28.2 %all-to-all-start = ((bf16[64,2,640]{2,1,0:T(2,128)(2,1)}), bf16[64,2,640]{2,1,0:T(2,128)(2,1)S(1)}, u32[]{:S(2)}, u32[]{:S(2)}) async-start(bf16[64,2,640]{2,1,0:T(2,128)(2,1)} %get-tuple-element.20.token_ref), calls=%async_computation | async-start | bytes 327680 | tf_op jit(solution)/shard_map/all_to_all | solution.py:306
  26.5 5.3 %copy-start.4 = (s32[2560]{0:T(1024)S(1)}, s32[2560]{0:T(1024)}, u32[]{:S(2)}) copy-start(s32[2560]{0:T(1024)} %param.8) | copy-start | bytes 30724
  26.5 24.2 %collective-permute-start.5 = (bf16[320,1281]{1,0:T(8,128)(2,1)S(1)}, bf16[320,1281]{1,0:T(8,128)(2,1)S(1)}, u32[]{:S(2)}, u32[]{:S(2)}) collective-permute-start(bf16[320,1281]{1,0:T(8,128)(2,1)S(1)} %pass_on.3.refs_1_), channel_id=1, source_target_pairs={{0,2},{1,7},{2,4},{3,1},{4,6},{5,3},{6,0},{7,5},{8,10},{9,15},{10,... | collective-permute-start | bytes 2459528 | tf_op jit(solution)/shard_map/ppermute | solution.py:293
  31.8 0.7 copy-start.1
  31.8 0.7 copy-start.2
  38.7 1.2 %copy-start.3 = (bf16[1,1281,320]{1,2,0:T(8,128)(2,1)S(1)}, bf16[1,1281,320]{1,2,0:T(8,128)(2,1)}, u32[]{:S(2)}) copy-start(bf16[1,1281,320]{1,2,0:T(8,128)(2,1)} %param.7) | copy-start | bytes 2459524
  41.6 11.1 %collective-permute-start.2 = (bf16[320,1281]{1,0:T(8,128)(2,1)S(1)}, bf16[320,1281]{1,0:T(8,128)(2,1)S(1)}, u32[]{:S(2)}, u32[]{:S(2)}) collective-permute-start(bf16[320,1281]{1,0:T(8,128)(2,1)S(1)} %get-tuple-element.24), channel_id=1, source_target_pairs={{0,1},{1,0},{2,3},{3,2},{4,5},{5,4},{6,7},{7,6},{8,9},{9,8},{10,11... | collective-permute-start | bytes 2459528 | tf_op jit(solution)/shard_map/ppermute | solution.py:297
  46.4 6.3 %collective-permute-start.3 = (bf16[320,1281]{1,0:T(8,128)(2,1)S(1)}, bf16[320,1281]{1,0:T(8,128)(2,1)S(1)}, u32[]{:S(2)}, u32[]{:S(2)}) collective-permute-start(bf16[320,1281]{1,0:T(8,128)(2,1)S(1)} %pass_on.3.refs_1_), channel_id=1, source_target_pairs={{0,1},{1,0},{2,3},{3,2},{4,5},{5,4},{6,7},{7,6},{8,9},{9,8},{10,11... | collective-permute-start | bytes 2459528 | tf_op jit(solution)/shard_map/ppermute | solution.py:297
  48.4 4.5 %collective-permute-start.4 = (bf16[320,1281]{1,0:T(8,128)(2,1)S(1)}, bf16[320,1281]{1,0:T(8,128)(2,1)S(1)}, u32[]{:S(2)}, u32[]{:S(2)}) collective-permute-start(bf16[320,1281]{1,0:T(8,128)(2,1)S(1)} %pass_on.4.refs_2_), channel_id=1, source_target_pairs={{0,1},{1,0},{2,3},{3,2},{4,5},{5,4},{6,7},{7,6},{8,9},{9,8},{10,11... | collective-permute-start | bytes 2459528 | tf_op jit(solution)/shard_map/ppermute | solution.py:297
  50.8 4.3 %collective-permute-start.6 = (bf16[320,1281]{1,0:T(8,128)(2,1)S(1)}, bf16[320,1281]{1,0:T(8,128)(2,1)S(1)}, u32[]{:S(2)}, u32[]{:S(2)}) collective-permute-start(bf16[320,1281]{1,0:T(8,128)(2,1)S(1)} %pass_on.5.refs_3_), channel_id=1, source_target_pairs={{0,1},{1,0},{2,3},{3,2},{4,5},{5,4},{6,7},{7,6},{8,9},{9,8},{10,11... | collective-permute-start | bytes 2459528 | tf_op jit(solution)/shard_map/ppermute | solution.py:297

commit v11 on v10

--- a/solution.py
+++ b/solution.py
@@ -19,6 +19,7 @@
 HALF = 640
 NEAR = 73 * 10**8
 NEARS = 3
+PARTS = 4
 FARS = 4
 
 NT = (((1,), (1,)), ((), ()))
@@ -60,15 +61,18 @@
 
 def pack_kernel(x_ref, tab_ref, o_ref, copy_ref, held_x, held_tab, sems):
     get_x = pltpu.make_async_copy(x_ref, held_x, sems.at[0])
-    get_tab = pltpu.make_async_copy(tab_ref, held_tab, sems.at[1])
-    put_tab = pltpu.make_async_copy(held_tab, copy_ref, sems.at[2])
     get_x.start()
-    get_tab.start()
+    parts = [pl.ds(n * SLAB // PARTS, SLAB // PARTS) for n in range(PARTS)]
+    gets = [pltpu.make_async_copy(tab_ref.at[p], held_tab.at[p], sems.at[1 + n]) for n, p in enumerate(parts)]
+    puts = [pltpu.make_async_copy(held_tab.at[p], copy_ref.at[p], sems.at[1 + PARTS + n]) for n, p in enumerate(parts)]
+    for get in gets:
+        get.start()
     get_x.wait()
     x = held_x[...].astype(jnp.float32).reshape(F * V * R, 4 * PAIRS).astype(jnp.bfloat16)
     turned = mul(by_member(), x, NT).astype(jnp.bfloat16)
-    get_tab.wait()
-    put_tab.start()
+    for get, put in zip(gets, puts):
+        get.wait()
+        put.start()
     placed = mul(turned, by_place(), NN)
     part = lane_part((PAIRS, STEPS * 128))
     out = placed[:PAIRS]
@@ -76,7 +80,8 @@
         out = jnp.where(part == q, placed[q * PAIRS:(q + 1) * PAIRS], out)
     halves = jnp.stack([out[:, :HALF], out[:, HALF:]], axis=0)
     o_ref[...] = jnp.swapaxes(halves, 0, 1).astype(jnp.bfloat16)
-    put_tab.wait()
+    for put in puts:
+        put.wait()
 
 
 def unpack_kernel(b_ref, o_ref):
@@ -225,7 +230,7 @@
 def pack(x, tab):
     return pl.pallas_call(
         pack_kernel, out_shape=(chunks(), like(tab)), in_specs=[ANY, ANY], out_specs=(VMEM, ANY),
-        scratch_shapes=[pltpu.VMEM(x.shape, x.dtype), pltpu.VMEM(tab.shape, tab.dtype), pltpu.SemaphoreType.DMA((3,))],
+        scratch_shapes=[pltpu.VMEM(x.shape, x.dtype), pltpu.VMEM(tab.shape, tab.dtype), pltpu.SemaphoreType.DMA((1 + 2 * PARTS,))],
         compiler_params=params(60), cost_estimate=cost(PAIRS * 4, SLAB, 2 * KP), name="pack")(x, tab)
 
 

time: 76.8 us -> 76.7 us (level)
  no operation moved by 1% of the time
where the time goes in v11:
time: 76.7 us; the launch traced here: 76 us
  starting transfers between devices  39.2 us (51%)
  blocking collectives  17.4 us (23%)
  Pallas kernels  10.5 us (14%)
  waiting for transfers between devices  6.21 us (8%)
  local copies, waits for them, and re-layouts  1.83 us (2%)
  between operations  0.89 us (1%)
    all_to_all x1, blocking collectives, local(): lax.all_to_all(result, 'wave', split_axis=0, concat_axis=0, tiled=True)  17.4 us
    all_to_all x1, starting transfers between devices, local(): lax.all_to_all(sent, 'wave', split_axis=0, concat_axis=0, tiled=True)  16.4 us
    ppermute x3, starting transfers between devices, along_x(): lax.ppermute(array, 'lev', [(d, (d + 2 * step * (1 - 2 * (d % 2))) % SLAB...  11.7 us
    ppermute x4, starting transfers between devices, other_core(): return lax.ppermute(array, 'lev', [(d, d ^ 1) for d in range(SLABS)])  11.1 us
    all_to_all x1, waiting for transfers between devices, local(): lax.all_to_all(sent, 'wave', split_axis=0, concat_axis=0, tiled=True)  5.04 us
    pallas_call x1, Pallas kernels, pack(): pl.pallas_call(pack_kernel, out_shape=(chunks(), like(tab)), in_specs=[AN...  2.83 us
    pallas_call x1, Pallas kernels, solve(): pl.pallas_call(solve_kernel, out_shape=chunks(), in_specs=[SMEM] * 2 + [V...  2.24 us
    unnamed x10, local copies, waits for them, and re-layouts  1.82 us
  transfers between devices with their start and end apart: 8, of which 3 were waited for; matrix products, arithmetic and copies ran while one was open for 0% of the time, Pallas kernels for 9%

profile of v11, /device:TPU:1, one launch (start us, length us, event | category | flops | bytes accessed | tf_op | source)
XLA Modules:
  0.0 76.0 jit_solution(12775032336166762994)
XLA Ops:
  0.0 5.2 %collective-permute-start = (bf16[320,1281]{1,0:T(8,128)(2,1)}, bf16[320,1281]{1,0:T(8,128)(2,1)S(1)}, u32[]{:S(2)}, u32[]{:S(2)}) collective-permute-start(bf16[320,1281]{1,0:T(8,128)(2,1)} %bitcast.4), channel_id=1, source_target_pairs={{0,2},{1,7},{2,4},{3,1},{4,6},{5,3},{6,0},{7,5},{8,10},{9,15},{10,... | collective-permute-start | bytes 2459528 | tf_op jit(solution)/shard_map/ppermute | solution.py:298
  5.2 2.8 %pack.1 = (bf16[64,2,640]{2,1,0:T(2,128)(2,1)}, bf16[320,1281]{1,0:T(8,128)(2,1)}) custom-call(bf16[2,4,40,256]{3,2,1,0:T(8,128)(2,1)} %x_ref.1, bf16[320,1281]{1,0:T(8,128)(2,1)} %bitcast.5), custom_call_target="tpu_custom_call" | custom-call | flops 419758080 | bytes 1639680 | tf_op jit(solution)/shard_map/pack/pallas_call | solution.py:231
  8.1 1.9 %collective-permute-start.1 = (bf16[320,1281]{1,0:T(8,128)(2,1)}, bf16[320,1281]{1,0:T(8,128)(2,1)S(1)}, u32[]{:S(2)}, u32[]{:S(2)}) collective-permute-start(bf16[320,1281]{1,0:T(8,128)(2,1)} %get-tuple-element.22), channel_id=1, source_target_pairs={{0,6},{1,3},{2,0},{3,5},{4,2},{5,7},{6,4},{7,1},{8,14},{9,11},{10,... | collective-permute-start | bytes 2459528 | tf_op jit(solution)/shard_map/ppermute | solution.py:298
  10.0 0.0 copy-start
  10.0 16.4 %all-to-all-start = ((bf16[64,2,640]{2,1,0:T(2,128)(2,1)}), bf16[64,2,640]{2,1,0:T(2,128)(2,1)S(1)}, u32[]{:S(2)}, u32[]{:S(2)}) async-start(bf16[64,2,640]{2,1,0:T(2,128)(2,1)} %get-tuple-element.20.token_ref), calls=%async_computation | async-start | bytes 327680 | tf_op jit(solution)/shard_map/all_to_all | solution.py:311
  26.5 0.0 collective-permute-done.tab_ref
  26.5 0.0 copy-start.4
  26.5 4.6 %collective-permute-start.5 = (bf16[320,1281]{1,0:T(8,128)(2,1)S(1)}, bf16[320,1281]{1,0:T(8,128)(2,1)S(1)}, u32[]{:S(2)}, u32[]{:S(2)}) collective-permute-start(bf16[320,1281]{1,0:T(8,128)(2,1)S(1)} %pass_on.3.refs_1_), channel_id=1, source_target_pairs={{0,2},{1,7},{2,4},{3,1},{4,6},{5,3},{6,0},{7,5},{8,10},{9,15},{10,... | collective-permute-start | bytes 2459528 | tf_op jit(solution)/shard_map/ppermute | solution.py:298
  31.8 0.0 copy-start.1
  31.8 0.0 copy-start.2
  31.8 0.6 copy-done.1
  32.4 0.0 copy-done.2
  32.4 0.8 coef.1
  33.2 5.0 %all-to-all-done.y_ref = bf16[64,2,640]{2,1,0:T(2,128)(2,1)S(1)} async-done(((bf16[64,2,640]{2,1,0:T(2,128)(2,1)}), bf16[64,2,640]{2,1,0:T(2,128)(2,1)S(1)}, u32[]{:S(2)}, u32[]{:S(2)}) %all-to-all-start) | async-done | bytes 163872 | tf_op jit(solution)/shard_map/all_to_all | solution.py:311
  38.2 0.4 weigh.1.w_ref
  38.7 0.0 copy-start.3
  38.7 0.0 collective-permute-done.1.tab_ref
  38.7 1.1 %copy-done.3 = bf16[1,1281,320]{1,2,0:T(8,128)(2,1)S(1)} copy-done((bf16[1,1281,320]{1,2,0:T(8,128)(2,1)S(1)}, bf16[1,1281,320]{1,2,0:T(8,128)(2,1)}, u32[]{:S(2)}) %copy-start.3) | copy-done | bytes 819864
  39.9 1.7 %near.1 = (f32[32,1281]{1,0:T(8,128)S(1)}, bf16[1281,320]{1,0:T(8,128)(2,1)S(1)}, bf16[1281,320]{1,0:T(8,128)(2,1)S(1)}, bf16[1281,320]{1,0:T(8,128)(2,1)S(1)}, bf16[320,1281]{1,0:T(8,128)(2,1)S(1)}) custom-call(s32[1]{0:T(128)} %bitcast.lev_ref, bf16[8,32,320]{2,1,0:T(8,128)(2,1)S(1)} %weigh.1.w_ref, bf16[320,1281]{1,0:T(8,128)(2,1)S(1)} %bitcast.6, ...), custom_call_target="tpu_custom_call" | custom-call | flops 7299999744 | tf_op jit(solution)/shard_map/near/pallas_call | solution.py:274
  41.6 4.8 %collective-permute-start.2 = (bf16[320,1281]{1,0:T(8,128)(2,1)S(1)}, bf16[320,1281]{1,0:T(8,128)(2,1)S(1)}, u32[]{:S(2)}, u32[]{:S(2)}) collective-permute-start(bf16[320,1281]{1,0:T(8,128)(2,1)S(1)} %get-tuple-element.24), channel_id=1, source_target_pairs={{0,1},{1,0},{2,3},{3,2},{4,5},{5,4},{6,7},{7,6},{8,9},{9,8},{10,11... | collective-permute-start | bytes 2459528 | tf_op jit(solution)/shard_map/ppermute | solution.py:302
  46.4 1.9 %collective-permute-start.3 = (bf16[320,1281]{1,0:T(8,128)(2,1)S(1)}, bf16[320,1281]{1,0:T(8,128)(2,1)S(1)}, u32[]{:S(2)}, u32[]{:S(2)}) collective-permute-start(bf16[320,1281]{1,0:T(8,128)(2,1)S(1)} %pass_on.3.refs_1_), channel_id=1, source_target_pairs={{0,1},{1,0},{2,3},{3,2},{4,5},{5,4},{6,7},{7,6},{8,9},{9,8},{10,11... | collective-permute-start | bytes 2459528 | tf_op jit(solution)/shard_map/ppermute | solution.py:302
  48.3 2.4 %collective-permute-start.4 = (bf16[320,1281]{1,0:T(8,128)(2,1)S(1)}, bf16[320,1281]{1,0:T(8,128)(2,1)S(1)}, u32[]{:S(2)}, u32[]{:S(2)}) collective-permute-start(bf16[320,1281]{1,0:T(8,128)(2,1)S(1)} %pass_on.4.refs_2_), channel_id=1, source_target_pairs={{0,1},{1,0},{2,3},{3,2},{4,5},{5,4},{6,7},{7,6},{8,9},{9,8},{10,11... | collective-permute-start | bytes 2459528 | tf_op jit(solution)/shard_map/ppermute | solution.py:302
  50.7 0.0 collective-permute-done.5.tab_ref
  50.8 1.9 %collective-permute-start.6 = (bf16[320,1281]{1,0:T(8,128)(2,1)S(1)}, bf16[320,1281]{1,0:T(8,128)(2,1)S(1)}, u32[]{:S(2)}, u32[]{:S(2)}) collective-permute-start(bf16[320,1281]{1,0:T(8,128)(2,1)S(1)} %pass_on.5.refs_3_), channel_id=1, source_target_pairs={{0,1},{1,0},{2,3},{3,2},{4,5},{5,4},{6,7},{7,6},{8,9},{9,8},{10,11... | collective-permute-start | bytes 2459528 | tf_op jit(solution)/shard_map/ppermute | solution.py:302
  52.7 0.0 collective-permute-done.2.refs_0_
  52.7 0.0 collective-permute-done.3.refs_1_
  52.7 0.1 collective-permute-done.4.refs_2_
  52.8 1.2 %far.1 = (f32[32,1281]{1,0:T(8,128)S(1)}, bf16[1281,320]{1,0:T(8,128)(2,1)S(1)}, bf16[1281,320]{1,0:T(8,128)(2,1)S(1)}, bf16[1281,320]{1,0:T(8,128)(2,1)S(1)}, bf16[1281,320]{1,0:T(8,128)(2,1)S(1)}) custom-call(s32[1]{0:T(128)} %bitcast.lev_ref, bf16[8,32,320]{2,1,0:T(8,128)(2,1)S(1)} %weigh.1.w_ref, f32[32,1281]{1,0:T(8,128)S(1)} %get-tuple-element.23.token_ref.raw_ref, ...), custom_call_target="tpu_custom_call" | custom-call | flops 839516160 | bytes 3279360 | tf_op jit(solution)/shard_map/far/pallas_call | solution.py:283
  54.0 1.1 %collective-permute-done.6.refs_7_ = bf16[320,1281]{1,0:T(8,128)(2,1)S(1)} collective-permute-done((bf16[320,1281]{1,0:T(8,128)(2,1)S(1)}, bf16[320,1281]{1,0:T(8,128)(2,1)S(1)}, u32[]{:S(2)}, u32[]{:S(2)}) %collective-permute-start.6) | collective-permute-done | bytes 819872 | tf_op jit(solution)/shard_map/ppermute | solution.py:302
  55.1 2.2 %solve.1 = bf16[64,2,640]{2,1,0:T(2,128)(2,1)S(1)} custom-call(s32[1]{0:T(128)S(6)} %copy.13.low_ref, s32[1]{0:T(128)} %bitcast.lev_ref, f32[2,8,128]{2,1,0:T(8,128)S(1)} %get-tuple-element.19.level_ref, bf16[8,32,320]{2,1,0:T(8,128)(2,1)S(1)} %weigh.1.w_ref, f32[8,2,320]{2,1,0:T(2,128)S(1)} %get-tuple-element.21.scale_ref, ...), custom_call_target="tpu_custom_call" | custom-call | flops 1888911360 | bytes 7378560 | tf_op jit(solution)/shard_map/solve/pallas_call | solution.py:290
  57.3 17.4 %all_to_all.10.b_ref = bf16[64,2,640]{2,1,0:T(2,128)(2,1)S(1)} all-to-all(bf16[64,2,640]{2,1,0:T(2,128)(2,1)S(1)} %solve.1), channel_id=1, replica_groups=mesh['wave'=64,'lev'=8] {'wave'}, dimensions={0} | all-to-all | bytes 327680 | tf_op jit(solution)/shard_map/all_to_all | solution.py:324
  74.7 1.3 %unpack.1 = bf16[2,4,40,256]{3,2,1,0:T(8,128)(2,1)} custom-call(bf16[64,2,640]{2,1,0:T(2,128)(2,1)S(1)} %all_to_all.10.b_ref), custom_call_target="tpu_custom_call" | custom-call | flops 419758080 | bytes 1311744 | tf_op jit(solution)/shard_map/unpack/pallas_call | solution.py:238
  (6 shorter events, 0.0 us)
Async XLA Ops:
  0.0 26.5 %collective-permute-start = (bf16[320,1281]{1,0:T(8,128)(2,1)}, bf16[320,1281]{1,0:T(8,128)(2,1)S(1)}, u32[]{:S(2)}, u32[]{:S(2)}) collective-permute-start(bf16[320,1281]{1,0:T(8,128)(2,1)} %bitcast.4), channel_id=1, source_target_pairs={{0,2},{1,7},{2,4},{3,1},{4,6},{5,3},{6,0},{7,5},{8,10},{9,15},{10,... | collective-permute-start | bytes 2459528 | tf_op jit(solution)/shard_map/ppermute | solution.py:298
  8.1 30.6 %collective-permute-start.1 = (bf16[320,1281]{1,0:T(8,128)(2,1)}, bf16[320,1281]{1,0:T(8,128)(2,1)S(1)}, u32[]{:S(2)}, u32[]{:S(2)}) collective-permute-start(bf16[320,1281]{1,0:T(8,128)(2,1)} %get-tuple-element.22), channel_id=1, source_target_pairs={{0,6},{1,3},{2,0},{3,5},{4,2},{5,7},{6,4},{7,1},{8,14},{9,11},{10,... | collective-permute-start | bytes 2459528 | tf_op jit(solution)/shard_map/ppermute | solution.py:298
  10.0 16.5 %copy-start = (bf16[64,2,640]{2,1,0:T(2,128)(2,1)S(1)}, bf16[64,2,640]{2,1,0:T(2,128)(2,1)}, u32[]{:S(2)}) copy-start(bf16[64,2,640]{2,1,0:T(2,128)(2,1)} %get-tuple-element.20.token_ref) | copy-start | bytes 491524
  10.0 28.2 %all-to-all-start = ((bf16[64,2,640]{2,1,0:T(2,128)(2,1)}), bf16[64,2,640]{2,1,0:T(2,128)(2,1)S(1)}, u32[]{:S(2)}, u32[]{:S(2)}) async-start(bf16[64,2,640]{2,1,0:T(2,128)(2,1)} %get-tuple-element.20.token_ref), calls=%async_computation | async-start | bytes 327680 | tf_op jit(solution)/shard_map/all_to_all | solution.py:311
  26.5 5.3 %copy-start.4 = (s32[2560]{0:T(1024)S(1)}, s32[2560]{0:T(1024)}, u32[]{:S(2)}) copy-start(s32[2560]{0:T(1024)} %param.8) | copy-start | bytes 30724
  26.5 24.2 %collective-permute-start.5 = (bf16[320,1281]{1,0:T(8,128)(2,1)S(1)}, bf16[320,1281]{1,0:T(8,128)(2,1)S(1)}, u32[]{:S(2)}, u32[]{:S(2)}) collective-permute-start(bf16[320,1281]{1,0:T(8,128)(2,1)S(1)} %pass_on.3.refs_1_), channel_id=1, source_target_pairs={{0,2},{1,7},{2,4},{3,1},{4,6},{5,3},{6,0},{7,5},{8,10},{9,15},{10,... | collective-permute-start | bytes 2459528 | tf_op jit(solution)/shard_map/ppermute | solution.py:298
  31.8 0.7 copy-start.1
  31.8 0.7 copy-start.2
  38.7 1.2 %copy-start.3 = (bf16[1,1281,320]{1,2,0:T(8,128)(2,1)S(1)}, bf16[1,1281,320]{1,2,0:T(8,128)(2,1)}, u32[]{:S(2)}) copy-start(bf16[1,1281,320]{1,2,0:T(8,128)(2,1)} %param.7) | copy-start | bytes 2459524
  41.6 11.1 %collective-permute-start.2 = (bf16[320,1281]{1,0:T(8,128)(2,1)S(1)}, bf16[320,1281]{1,0:T(8,128)(2,1)S(1)}, u32[]{:S(2)}, u32[]{:S(2)}) collective-permute-start(bf16[320,1281]{1,0:T(8,128)(2,1)S(1)} %get-tuple-element.24), channel_id=1, source_target_pairs={{0,1},{1,0},{2,3},{3,2},{4,5},{5,4},{6,7},{7,6},{8,9},{9,8},{10,11... | collective-permute-start | bytes 2459528 | tf_op jit(solution)/shard_map/ppermute | solution.py:302
  46.4 6.3 %collective-permute-start.3 = (bf16[320,1281]{1,0:T(8,128)(2,1)S(1)}, bf16[320,1281]{1,0:T(8,128)(2,1)S(1)}, u32[]{:S(2)}, u32[]{:S(2)}) collective-permute-start(bf16[320,1281]{1,0:T(8,128)(2,1)S(1)} %pass_on.3.refs_1_), channel_id=1, source_target_pairs={{0,1},{1,0},{2,3},{3,2},{4,5},{5,4},{6,7},{7,6},{8,9},{9,8},{10,11... | collective-permute-start | bytes 2459528 | tf_op jit(solution)/shard_map/ppermute | solution.py:302
  48.3 4.5 %collective-permute-start.4 = (bf16[320,1281]{1,0:T(8,128)(2,1)S(1)}, bf16[320,1281]{1,0:T(8,128)(2,1)S(1)}, u32[]{:S(2)}, u32[]{:S(2)}) collective-permute-start(bf16[320,1281]{1,0:T(8,128)(2,1)S(1)} %pass_on.4.refs_2_), channel_id=1, source_target_pairs={{0,1},{1,0},{2,3},{3,2},{4,5},{5,4},{6,7},{7,6},{8,9},{9,8},{10,11... | collective-permute-start | bytes 2459528 | tf_op jit(solution)/shard_map/ppermute | solution.py:302
  50.8 4.3 %collective-permute-start.6 = (bf16[320,1281]{1,0:T(8,128)(2,1)S(1)}, bf16[320,1281]{1,0:T(8,128)(2,1)S(1)}, u32[]{:S(2)}, u32[]{:S(2)}) collective-permute-start(bf16[320,1281]{1,0:T(8,128)(2,1)S(1)} %pass_on.5.refs_3_), channel_id=1, source_target_pairs={{0,1},{1,0},{2,3},{3,2},{4,5},{5,4},{6,7},{7,6},{8,9},{9,8},{10,11... | collective-permute-start | bytes 2459528 | tf_op jit(solution)/shard_map/ppermute | solution.py:302
